TPU v7x, 256 devices: a whole 4x4x8 slice. The times are simulated.
256 devices in a mesh: frames: 32 (over z_lo, y, core), feat: 8 (over z_hi, x).
Axes of the slice: x: 4, y: 4, z: 8 (z_hi: 2, z_lo: 4; z = z_hi * 4 + z_lo), core: 2. Of those that a mesh axis runs over, the one named last changes fastest.
Arguments:
- frames_data: bfloat16 [32768, 8192], P('frames', 'feat')
- starts: int32 [64], replicated, may hold values from 0 to 32511, as said below
- lags: int32 [64], replicated, may hold values from 1 to 10, as said below
Outputs:
- panel_rows: float32 [8, 1024, 512], P('feat', 'frames')
- whitened_cross: float32 [8, 1024, 512], P('feat', 'frames')
- whitened_tau: float32 [512, 512], P('frames')
Inputs may be any that keep to these rules, and one draw needn't show every extreme that they name: starts rise strictly, starts[0] = 0; trajectory k holds frames starts[k] to starts[k+1] - 1, the last one runs to the end. `lags`: some trajectory has lag 10.
All inputs are finite; a program needn't handle non-finite values.
Results may differ from a plain program's by a relative error of at most 0.0003.
Values may be sent and summed in bfloat16 or wider, within the bound.
No kernel may reach another device: no remote copies, remote signals or barrier semaphores. Data moves between devices by JAX's collectives and lax.ppermute only.
A program may use at most 64 MiB of HBM per device.

v0:
```python
import functools

import jax
import jax.numpy as jnp
from jax import lax
from jax.experimental import pallas as pl
from jax.experimental.pallas import tpu as pltpu
from jax.sharding import Mesh
from jax.sharding import PartitionSpec as P

P_SIZE = 512
RIM = 16
NB = 128
HI = lax.Precision.HIGHEST
F32 = jnp.float32
BF16 = jnp.bfloat16
AXES = ("z", "y", "c", "w", "x")
SIZES = (4, 4, 2, 2, 4)
CHUNK = 272
FIRST = CHUNK - 2 * RIM
STEP0 = 1024 - 3 * CHUNK


def coords():
    for z in range(4):
        for y in range(4):
            for c in range(2):
                for w in range(2):
                    for x in range(4):
                        yield (z, y, c, w, x)


def flat(p):
    i = 0
    for v, n in zip(p, SIZES):
        i = i * n + v
    return i


def move(value, target):
    pairs = []
    for p in coords():
        q = target(*p)
        if q is not None:
            pairs.append((flat(p), flat(q)))
    return lax.ppermute(value, AXES, pairs)


def call(kernel, outs, args, name, scratch=(), flops=0, vmem=16, hbm=()):
    specs = [pl.BlockSpec(memory_space=pltpu.VMEM)] * len(args)
    specs[0] = pl.BlockSpec(memory_space=pltpu.SMEM)
    for i in hbm:
        specs[i] = pl.BlockSpec(memory_space=pltpu.HBM)
    return pl.pallas_call(
        kernel,
        out_shape=outs,
        in_specs=specs,
        out_specs=[pl.BlockSpec(memory_space=pltpu.VMEM)] * len(outs),
        scratch_shapes=list(scratch),
        compiler_params=pltpu.CompilerParams(vmem_limit_bytes=vmem * 2**20),
        cost_estimate=pl.CostEstimate(flops=flops, bytes_accessed=2**20, transcendentals=0),
        name=name,
    )(*args)


def mm(a, b, precision=None):
    return lax.dot_general(
        a, b, (((0,), (0,)), ((), ())), precision=precision, preferred_element_type=F32
    )


def mn(a, b):
    return lax.dot_general(
        a, b, (((1,), (0,)), ((), ())), precision=HI, preferred_element_type=F32
    )


def mt(a, b):
    return lax.dot_general(
        a, b, (((1,), (1,)), ((), ())), precision=HI, preferred_element_type=F32
    )


def frame_info(first, rows, table):
    starts, ends, lags = (table[i : i + 1, :].astype(F32) for i in range(3))
    t = (first + lax.broadcasted_iota(jnp.int32, (rows, 1), 0)).astype(F32)
    here = (starts <= t) & (t < ends)
    pick = lambda v: jnp.sum(jnp.where(here, v, 0.0), axis=1, keepdims=True)
    lag = pick(lags)
    ahead = jnp.where(t + lag < pick(ends), 1.0, 0.0)
    behind = jnp.where(t - lag >= pick(starts), 1.0, 0.0)
    return lag, ahead, behind


def pair_count(table):
    starts, ends, lags = (table[i : i + 1, :].astype(F32) for i in range(3))
    return jnp.sum(jnp.maximum(ends - starts - lags, 0.0), axis=1, keepdims=True)


def shifted(window, lag, ahead, behind):
    rows, width = lag.shape[0], window.shape[0]
    off = (
        lax.broadcasted_iota(jnp.int32, (rows, width), 1)
        - lax.broadcasted_iota(jnp.int32, (rows, width), 0)
        - RIM
    ).astype(F32)
    later = jnp.where((off == lag) & (ahead > 0.0), 1.0, 0.0).astype(BF16)
    earlier = jnp.where((off == -lag) & (behind > 0.0), 1.0, 0.0).astype(BF16)
    dims = (((1,), (0,)), ((), ()))
    zp = lax.dot_general(later, window, dims, preferred_element_type=F32)
    zm = lax.dot_general(earlier, window, dims, preferred_element_type=F32)
    return zp.astype(BF16), zm.astype(BF16)


def diag_kernel(pos, table, xp, before, after, mine, theirs, ext, right):
    rows = xp.shape[0]
    ext[0:RIM, :] = before[...]
    ext[RIM : RIM + rows, :] = xp[...]
    ext[RIM + rows :, :] = after[...]
    fill_right(pos, table, ext, right, rows, P_SIZE)
    scale = 1.0 / pair_count(table)
    c = pos[1]
    v = xp[...]
    for half in range(2):
        cols = slice(256 * half, 256 * half + 256)
        d0 = mm(v[:, cols], right[:, :P_SIZE]) * scale
        d1 = mm(v[:, cols], right[:, P_SIZE : 2 * P_SIZE]) + mm(v[:, cols], right[:, 2 * P_SIZE :])
        d1 = d1 * (0.5 * scale)
        r = lax.broadcasted_iota(jnp.int32, d0.shape, 0) + 256 * half
        l = lax.broadcasted_iota(jnp.int32, d0.shape, 1)
        packed = jnp.where(r >= l, d0, d1)
        diag = jnp.sum(jnp.where(r == l, d1, 0.0), axis=1, keepdims=True)
        diag = jnp.broadcast_to(diag, (256, NB))

        @pl.when(c == half)
        def _():
            mine[:, :P_SIZE] = packed
            mine[:, P_SIZE:] = diag

        @pl.when(c != half)
        def _():
            theirs[:, :P_SIZE] = packed
            theirs[:, P_SIZE:] = diag


def fill_right(pos, table, ext, right, rows, n):
    for b in range(0, rows, 256):
        lag, ahead, behind = frame_info(pos[0] + b, 256, table)
        zp, zm = shifted(ext[b : b + 256 + 2 * RIM, :], lag, ahead, behind)
        own = ext[b + RIM : b + RIM + 256, :]
        right[b : b + 256, :n] = own * (0.5 * (ahead + behind)).astype(BF16)
        right[b : b + 256, n : 2 * n] = zp
        right[b : b + 256, 2 * n :] = zm


def cov_kernel(pos, table, x, g0, g1, g2, g3, out, ext, right, sem):
    rows, n = x.shape[0], P_SIZE
    z, col = pos[3], pos[5]
    for wait in (False, True):
        for k, g in enumerate((g0, g1, g2, g3)):
            q = lax.rem(col - k + 4, 4)

            def bring(src, dst, i):
                copy = pltpu.make_async_copy(src, dst, sem.at[k, i])
                copy.wait() if wait else copy.start()

            @pl.when(q == 0)
            def _():
                bring(g.at[0:RIM, :], ext.at[0:RIM, :], 0)
                bring(g.at[RIM : 2 * RIM, :], ext.at[RIM + rows : 2 * RIM + rows, :], 1)
                bring(g.at[2 * RIM : CHUNK, :], ext.at[RIM : RIM + FIRST, :], 2)

            @pl.when(q != 0)
            def _():
                at = pl.multiple_of(RIM + STEP0 + CHUNK * (q - 1), 16)
                bring(g, ext.at[pl.ds(at, CHUNK), :], 0)

    fill_right(pos, table, ext, right, rows, n)
    scale = 1.0 / pair_count(table)
    for zz in range(4):
        left = x[:, 256 * zz : 256 * zz + 256]
        d0 = mm(left, right[:, :n]) * scale
        d1 = mm(left, right[:, n : 2 * n]) + mm(left, right[:, 2 * n :])
        d1 = d1 * (0.5 * scale)
        at = pl.multiple_of(lax.rem(zz - z + 4, 4) * 32, 32)
        for k in range(8):
            out[k, pl.ds(at, 32), :n] = d0[32 * k : 32 * k + 32, :]
            out[k, pl.ds(at, 32), n:] = d1[32 * k : 32 * k + 32, :]


def factor(s):
    n = NB
    groups = [s[8 * i : 8 * i + 8, :] for i in range(n // 8)]
    sub = lax.broadcasted_iota(jnp.int32, (8, n), 0)
    lane = lax.broadcasted_iota(jnp.int32, (8, n), 1)
    for j in range(n // 8):
        r0 = 8 * j
        look = j + 1 < n // 8
        block = (lane >= r0) & (lane < r0 + 8)
        rows = groups[j]
        cols = [jnp.broadcast_to(rows[:, r0 + r : r0 + r + 1], (8, n)) for r in range(8)]
        rows = jnp.where(block, jnp.where(lane - r0 == sub, 1.0, 0.0), rows)
        if look:
            more = groups[j + 1]
            below = [jnp.broadcast_to(more[:, r0 + r : r0 + r + 1], (8, n)) for r in range(8)]
            more = jnp.where(block, 0.0, more)
        for r in range(8):
            rs = lax.rsqrt(cols[r][r : r + 1, :])
            l = cols[r] * rs
            lm = jnp.where(sub > r, l, 0.0)
            row = rows[r : r + 1, :] * rs
            rows = jnp.where(sub == r, row, rows - lm * row)
            if look:
                lq = below[r] * rs
                more = more - lq * row
            for s_ in range(r + 1, 8):
                at = l[s_ : s_ + 1, :]
                cols[s_] = cols[s_] - lm * at
                if look:
                    below[s_] = below[s_] - lq * at
        groups[j] = rows
        if look:
            groups[j + 1] = more
        if j + 2 < n // 8:
            m = n - r0 - 16
            rest = jnp.concatenate(groups[j + 2 :], axis=0)
            lanes = lax.broadcasted_iota(jnp.int32, (m, n), 1)
            rest = jnp.where((lanes >= r0) & (lanes < r0 + 8), 0.0, rest)
            rest = rest - mm(rows, rows, HI)[r0 + 16 :, :]
            for i in range(j + 2, n // 8):
                groups[i] = rest[8 * (i - j - 2) : 8 * (i - j - 1), :]
    return lower_part(jnp.concatenate(groups, axis=0))


def lower_part(v):
    r = lax.broadcasted_iota(jnp.int32, v.shape, 0)
    c = lax.broadcasted_iota(jnp.int32, v.shape, 1)
    return jnp.where(r >= c, v, 0.0)


def unpack_kernel(pos, own, other, w, up):
    c = pos[1]
    r = lax.broadcasted_iota(jnp.int32, (P_SIZE // 2, P_SIZE), 0)
    l = lax.broadcasted_iota(jnp.int32, (P_SIZE // 2, P_SIZE), 1)
    for half in range(2):
        at = slice(256 * half, 256 * half + 256)
        v = jnp.where(c == half, own[:, :P_SIZE], other[:, :P_SIZE])
        d = jnp.where(c == half, own[:, P_SIZE : P_SIZE + 1], other[:, P_SIZE : P_SIZE + 1])
        w[at, :] = v
        up[at, :] = jnp.where(l > r + 256 * half, v, jnp.where(l == r + 256 * half, d, 0.0))
    r = lax.broadcasted_iota(jnp.int32, (NB, NB), 0)
    l = lax.broadcasted_iota(jnp.int32, (NB, NB), 1)
    for o in range(0, P_SIZE, NB):
        s = jnp.where(r >= l, w[o : o + NB, o : o + NB], 0.0)
        w[o : o + NB, o : o + NB] = s + jnp.where(r < l, s.T, 0.0)
    inverse_step(0, w)


def inverse_step(o, w):
    e = o + NB
    t = factor(w[o:e, o:e])
    w[o:e, o:e] = t
    if o:
        w[o:e, :o] = mn(t, w[o:e, :o])
    if e < P_SIZE:
        low = mt(w[e:, o:e], t)
        w[e:, o:e] = -mn(low, t)
        if o:
            w[e:, :o] = w[e:, :o] - mn(low, w[o:e, :o])
        w[e:, e:] = w[e:, e:] - mt(low, low)
    else:
        w[...] = lower_part(w[...])


def inverse_kernel(o, pos, v, w):
    w[...] = v[...]
    inverse_step(o, w)


def whiten_kernel(pos, inv, up, p0, p1, p2, p3, panel, cross, tau, left):
    m = inv[...]
    s = (p0[...] + p1[...]) + (p2[...] + p3[...])
    left[0:32, :] = s[:, :P_SIZE]
    left[32:64, :] = s[:, P_SIZE:]
    rows = inv[pl.ds(pl.multiple_of(pos[2], 16), 16), :]
    u = up[...]
    r = lax.broadcasted_iota(jnp.int32, u.shape, 0)
    l = lax.broadcasted_iota(jnp.int32, u.shape, 1)
    left[64:80, :] = mn(rows, u) + mt(rows, jnp.where(l > r, u, 0.0))
    res = mt(left[...], m)
    panel[0] = res[0:32, :]
    cross[0] = res[32:64, :]
    tau[...] = res[64:80, :]


def swap_core(v, only=None):
    return move(v, lambda z, y, c, w, x: (z, y, 1 - c, w, x) if only is None or (w, x) == only else None)


def exchange(v, axes):
    return lax.all_to_all(v, axes, 0, 0, tiled=True)


def spread(v, axes, n):
    return exchange(jnp.broadcast_to(v[None], (n, *v.shape)), axes)


def together(*values):
    return lax.optimization_barrier(values)


def diag_half(mine, theirs):
    half = (mine + swap_core(theirs, (0, 0))).reshape(4, 64, mine.shape[1])
    return jnp.sum(exchange(half, "y"), axis=0)


def diag_rows(quarter):
    return jnp.sum(exchange(quarter.reshape(4, 16, quarter.shape[1]), "z"), axis=0)


def diag_feat(own, w):
    over = move(own, lambda z, y, c, w, x: (z, y, c, 1, 0) if (w, x) == (0, 0) else None)
    return spread(jnp.where(w == 0, own, over), "x", 4)[0]


def diag_gather(own):
    half = spread(own, ("y", "z"), 16).reshape(256, own.shape[1])
    return half, swap_core(half)


def body(frames_data, starts, lags):
    tok, width = frames_data.shape
    z, y, c, w, x = (lax.axis_index(a) for a in AXES)
    slab = z * 8 + y * 2 + c
    total = tok * 32
    ends = jnp.concatenate([starts[1:], jnp.array([total], dtype=jnp.int32)])
    table = jnp.stack([starts, ends, lags])
    pos = jnp.stack([slab * tok, c, slab * 16, z, y, x]).astype(jnp.int32)
    panel = frames_data[:, :P_SIZE]

    def step(by):
        def target(z, y, c, w, x):
            i = z * 8 + y * 2 + c + by
            return (i // 8, i // 2 % 4, i % 2, 0, 0) if (w, x) == (0, 0) and 0 <= i < 32 else None
        return target

    behind = move(panel[:RIM], step(-1))
    before = move(panel[tok - RIM :], step(1))

    packed = jax.ShapeDtypeStruct((256, P_SIZE + NB), F32)
    dz = call(
        diag_kernel, [packed, packed], (pos, table, panel, before, behind), "diagonal",
        scratch=[pltpu.VMEM((tok + 2 * RIM, P_SIZE), BF16), pltpu.VMEM((tok, 3 * P_SIZE), BF16)],
        flops=3 * 10**9,
    )
    sent = [
        move(panel[STEP0 + CHUNK * (k - 1) : STEP0 + CHUNK * k],
             lambda z, y, c, w, x: (z, y, c, w, k) if (w, x) == (0, 0) else None)
        for k in (2, 1, 3)
    ]
    first = jnp.concatenate([before, behind, panel[:FIRST]], axis=0)
    hold = jnp.where(x == 0, first, sent[0] + sent[1] + sent[2])
    mine, theirs = dz
    theirs, hold = together(theirs, hold)
    over = move(hold, lambda z, y, c, w, x: (z, y, c, 1, x) if w == 0 else None)
    quarter, over = together(diag_half(mine, theirs), over)
    rows16 = diag_rows(quarter)
    hold = jnp.where(w == 0, hold, over)
    gathered = [hold] + [
        move(hold, lambda z, y, c, w, x: (z, y, c, w, (x + k) % 4)) for k in (1, 2, 3)
    ]
    rows16, *gathered = together(rows16, *gathered)
    own, other = diag_gather(diag_feat(rows16, w))
    (part,) = call(
        cov_kernel, [jax.ShapeDtypeStruct((8, 128, 2 * P_SIZE), F32)], (pos, table, frames_data, *gathered), "covariance",
        scratch=[
            pltpu.VMEM((tok + 2 * RIM, P_SIZE), BF16),
            pltpu.VMEM((tok, 3 * P_SIZE), BF16),
            pltpu.SemaphoreType.DMA((4, 3)),
        ],
        flops=5 * 10**9, vmem=20, hbm=(3, 4, 5, 6),
    )
    t = lax.psum_scatter(part.reshape(1024, 2 * P_SIZE), ("y", "c"), scatter_dimension=0, tiled=True)
    rows = [t[:32]] + [
        move(t[32 * k : 32 * k + 32], lambda z, y, c, w, x: ((z + k) % 4, y, c, w, x)) for k in (2, 1, 3)
    ]

    full = jax.ShapeDtypeStruct((P_SIZE, P_SIZE), F32)
    inv, up = call(unpack_kernel, [full, full], (pos, own, other), "factor0", flops=5 * 10**9, vmem=8)
    for o in range(NB, P_SIZE, NB):
        (inv,) = call(functools.partial(inverse_kernel, o), [full], (pos, inv), "factor%d" % o, flops=5 * 10**9, vmem=8)
    own = jax.ShapeDtypeStruct((1, 32, P_SIZE), F32)
    return tuple(
        call(
            whiten_kernel, [own, own, jax.ShapeDtypeStruct((16, P_SIZE), F32)],
            (pos, inv, up, *rows), "whiten", scratch=[pltpu.VMEM((80, P_SIZE), F32)], flops=2 * 10**9,
        )
    )


def solution(mesh):
    split = Mesh(mesh.devices.reshape(SIZES), AXES)
    frames, feat = ("z", "y", "c"), ("w", "x")
    return jax.shard_map(
        body,
        mesh=split,
        in_specs=(P(frames, feat), P(), P()),
        out_specs=(P(feat, frames, None), P(feat, frames, None), P(frames, None)),
        check_vma=False,
    )
```

profile of v0, /device:TPU:2, one launch (start us, length us, event | category | flops | bytes accessed | tf_op | source)
XLA Modules:
  0.0 162.2 jit_solution(7114380684683538475)
XLA Ops:
  7.2 0.0 copy-start.1
  7.2 0.9 fusion.1
  8.1 0.7 collective-permute-start
  8.7 0.7 collective-permute-start.1
  9.4 2.0 %fusion = (bf16[272,512]{1,0:T(8,128)(2,1)}, bf16[272,512]{1,0:T(8,128)(2,1)}, bf16[272,512]{1,0:T(8,128)(2,1)}) fusion(bf16[1024,1024]{1,0:T(8,128)(2,1)} %x.1), kind=kLoop, calls=%fused_computation.6 | loop fusion | bytes 1671168 | tf_op jit(solution)/shard_map/slice | solution.py:357
  11.4 1.4 collective-permute-start.2
  12.8 1.3 collective-permute-start.3
  14.1 1.4 collective-permute-start.4
  15.5 0.7 slice.45
  16.2 0.1 add_bitcast_fusion
  16.3 0.7 pad_add_fusion.table
  16.9 1.3 slice.46.xp
  18.2 0.0 copy-done.1
  18.3 0.1 stack.39.pos
  18.4 0.0 collective-permute-done.before
  18.4 0.0 collective-permute-done.1.after
  18.4 4.3 %diagonal.1 = (f32[256,640]{1,0:T(8,128)S(1)}, f32[256,640]{1,0:T(8,128)S(1)}) custom-call(s32[6]{0:T(128)S(1)} %stack.39.pos, s32[3,64]{1,0:T(4,128)S(1)} %pad_add_fusion.table, bf16[1024,512]{1,0:T(8,128)(2,1)S(1)} %slice.46.xp, bf16[16,512]{1,0:T(8,128)(2,1)S(1)} %collective-permute-done.before, bf16[16,512]{1,0:T(8,128)(2,1)S(1)} %collective-permute-done.1.after), custom_call_target="tpu_custom_call" | custom-call | flops 3000000000 | bytes 1048576 | tf_op jit(solution)/shard_map/diagonal/pallas_call | solution.py:54
  22.6 0.0 collective-permute-done.2
  22.7 7.9 %collective-permute-done.3 = bf16[272,512]{1,0:T(8,128)(2,1)} collective-permute-done((bf16[272,512]{1,0:T(8,128)(2,1)}, bf16[272,512]{1,0:T(8,128)(2,1)}, u32[]{:S(2)}, u32[]{:S(2)}) %collective-permute-start.3) | collective-permute-done | bytes 278560 | tf_op jit(solution)/shard_map/ppermute | solution.py:46
  30.5 0.0 collective-permute-done.4
  30.5 1.3 maximum_select_fusion
  31.8 0.7 collective-permute-start.5
  32.5 0.0 collective-permute-done.5
  32.5 0.9 add.21
  33.5 4.3 %all-to-all-start = ((f32[4,64,640]{2,1,0:T(8,128)}), f32[4,64,640]{2,1,0:T(8,128)S(1)}, u32[]{:S(2)}, u32[]{:S(2)}) async-start(f32[4,64,640]{2,1,0:T(8,128)} %bitcast.9), calls=%async_computation | async-start | bytes 1310720 | tf_op jit(solution)/shard_map/all_to_all | solution.py:301
  37.7 0.0 reduce-scatter.2.cloned.1.call-start
  37.7 1.5 collective-permute-start.6
  39.2 9.0 %all-to-all-done = f32[4,64,640]{2,1,0:T(8,128)S(1)} async-done(((f32[4,64,640]{2,1,0:T(8,128)}), f32[4,64,640]{2,1,0:T(8,128)S(1)}, u32[]{:S(2)}, u32[]{:S(2)}) %all-to-all-start) | async-done | bytes 655392 | tf_op jit(solution)/shard_map/all_to_all | solution.py:301
  48.3 0.0 collective-permute-done.6
  48.3 0.1 collective-permute-start.7
  48.4 5.6 %collective-permute-start.8 = (bf16[272,512]{1,0:T(8,128)(2,1)S(1)}, bf16[272,512]{1,0:T(8,128)(2,1)S(1)}, u32[]{:S(2)}, u32[]{:S(2)}) collective-permute-start(bf16[272,512]{1,0:T(8,128)(2,1)S(1)} %broadcast_select_fusion.g0), channel_id=1, source_target_pairs={{0,2},{1,3},{2,0},{3,1},{4,6},{5,7},{6,4},{7,5},{8,10},{9,11},{10,... | collective-permute-start | bytes 835592 | tf_op jit(solution)/shard_map/ppermute | solution.py:46
  54.0 0.0 collective-permute-start.9
  54.0 13.3 %all_to_all.20 = f32[4,16,640]{2,1,0:T(8,128)S(1)} all-to-all(f32[4,16,640]{2,1,0:T(8,128)S(1)} %bitcast.19), channel_id=1, replica_groups=mesh['z'=4,'y'=4,'c'=2,'w'=2,'x'=4] {'z'}, dimensions={0} | all-to-all | bytes 327680 | tf_op jit(solution)/shard_map/all_to_all | solution.py:301
  67.3 0.0 collective-permute-done.7.g1
  67.3 0.0 collective-permute-done.8.g2
  67.3 0.0 collective-permute-done.9.g3
  67.3 5.8 %covariance.1 = f32[8,128,1024]{2,1,0:T(8,128)S(1)} custom-call(s32[6]{0:T(128)S(1)} %stack.39.pos, s32[3,64]{1,0:T(4,128)S(1)} %pad_add_fusion.table, bf16[1024,1024]{1,0:T(8,128)(2,1)S(1)} %copy-done.1, bf16[272,512]{1,0:T(8,128)(2,1)S(1)} %broadcast_select_fusion.g0, bf16[272,512]{1,0:T(8,128)(2,1)S(1)} %collective-permute-done.7.g1, ...), custom_call_target="tpu_custom_call" | custom-call | flops 5000000000 | bytes 1048576 | tf_op jit(solution)/shard_map/covariance/pallas_call | solution.py:54
  73.1 0.0 copy-start
  73.2 1.9 %copy-done = f32[8,128,1024]{2,1,0:T(8,128)} copy-done((f32[8,128,1024]{2,1,0:T(8,128)}, f32[8,128,1024]{2,1,0:T(8,128)S(1)}, u32[]{:S(2)}) %copy-start) | copy-done | bytes 4194328
  75.1 0.0 reduce-scatter.2.cloned.1.call-update
  75.1 0.7 collective-permute-start.10
  75.8 0.0 collective-permute-done.10
  75.9 17.1 %all_to_all.21 = f32[4,16,640]{2,1,0:T(8,128)S(1)} all-to-all(f32[4,16,640]{2,1,0:T(8,128)S(1)} %broadcast_in_dim.6), channel_id=1, replica_groups=mesh['z'=4,'y'=4,'c'=2,'w'=2,'x'=4] {'x'}, dimensions={0} | all-to-all | bytes 327680 | tf_op jit(solution)/shard_map/all_to_all | solution.py:301
  93.0 25.1 %all_to_all.22 = f32[16,16,640]{2,1,0:T(8,128)S(1)} all-to-all(f32[16,16,640]{2,1,0:T(8,128)S(1)} %broadcast_in_dim.15), channel_id=1, replica_groups=mesh['z'=4,'y'=4,'c'=2,'w'=2,'x'=4] {'y','z'}, dimensions={0} | all-to-all | bytes 1310720 | tf_op jit(solution)/shard_map/all_to_all | solution.py:301
  118.1 0.0 collective-permute-start.11
  118.1 2.1 %collective-permute-done.11.other = f32[256,640]{1,0:T(8,128)S(1)} collective-permute-done((f32[256,640]{1,0:T(8,128)S(1)}, f32[256,640]{1,0:T(8,128)S(1)}, u32[]{:S(2)}, u32[]{:S(2)}) %collective-permute-start.11) | collective-permute-done | bytes 655392 | tf_op jit(solution)/shard_map/ppermute | solution.py:46
  120.2 6.5 %factor0.1 = (f32[512,512]{1,0:T(8,128)S(1)}, f32[512,512]{1,0:T(8,128)S(1)}) custom-call(s32[6]{0:T(128)S(1)} %stack.39.pos, f32[256,640]{1,0:T(8,128)S(1)} %bitcast.18, f32[256,640]{1,0:T(8,128)S(1)} %collective-permute-done.11.other), custom_call_target="tpu_custom_call" | custom-call | flops 5000000000 | bytes 1048576 | tf_op jit(solution)/shard_map/factor0/pallas_call | solution.py:54
  126.7 6.0 %factor128.1.v = f32[512,512]{1,0:T(8,128)S(1)} custom-call(s32[6]{0:T(128)S(1)} %stack.39.pos, f32[512,512]{1,0:T(8,128)S(1)} %get-tuple-element.23.v), custom_call_target="tpu_custom_call" | custom-call | flops 5000000000 | bytes 1048576 | tf_op jit(solution)/shard_map/factor128/pallas_call | solution.py:54
  132.7 5.7 %factor256.1.v = f32[512,512]{1,0:T(8,128)S(1)} custom-call(s32[6]{0:T(128)S(1)} %stack.39.pos, f32[512,512]{1,0:T(8,128)S(1)} %factor128.1.v), custom_call_target="tpu_custom_call" | custom-call | flops 5000000000 | bytes 1048576 | tf_op jit(solution)/shard_map/factor256/pallas_call | solution.py:54
  138.3 0.0 reduce-scatter.2.cloned.1.call-done
  138.3 1.1 fusion.2
  139.5 0.9 collective-permute-start.12
  140.4 1.1 collective-permute-start.13
  141.5 2.7 %collective-permute-start.14 = (f32[32,1024]{1,0:T(8,128)S(1)}, f32[32,1024]{1,0:T(8,128)S(1)}, u32[]{:S(2)}, u32[]{:S(2)}) collective-permute-start(f32[32,1024]{1,0:T(8,128)S(1)} %get-tuple-element.34), channel_id=1, source_target_pairs={{0,192},{1,193},{2,194},{3,195},{4,196},{5,197},{6,198},{7,199},{8... | collective-permute-start | bytes 393224 | tf_op jit(solution)/shard_map/ppermute | solution.py:46
  144.2 5.2 %factor384.1.inv = f32[512,512]{1,0:T(8,128)S(1)} custom-call(s32[6]{0:T(128)S(1)} %stack.39.pos, f32[512,512]{1,0:T(8,128)S(1)} %factor256.1.v), custom_call_target="tpu_custom_call" | custom-call | flops 5000000000 | bytes 1048576 | tf_op jit(solution)/shard_map/factor384/pallas_call | solution.py:54
  149.4 2.5 %collective-permute-done.12.p1 = f32[32,1024]{1,0:T(8,128)S(1)} collective-permute-done((f32[32,1024]{1,0:T(8,128)S(1)}, f32[32,1024]{1,0:T(8,128)S(1)}, u32[]{:S(2)}, u32[]{:S(2)}) %collective-permute-start.12) | collective-permute-done | bytes 131104 | tf_op jit(solution)/shard_map/ppermute | solution.py:46
  151.9 0.0 collective-permute-done.13.p2
  152.0 0.0 collective-permute-done.14.p3
  152.0 3.4 %whiten.1 = (f32[1,32,512]{2,1,0:T(8,128)}, f32[1,32,512]{2,1,0:T(8,128)}, f32[16,512]{1,0:T(8,128)}) custom-call(s32[6]{0:T(128)S(1)} %stack.39.pos, f32[512,512]{1,0:T(8,128)S(1)} %factor384.1.inv, f32[512,512]{1,0:T(8,128)S(1)} %get-tuple-element.24.up, f32[32,1024]{1,0:T(8,128)S(1)} %get-tuple-element.37.p0, f32[32,1024]{1,0:T(8,128)S(1)} %collective-permute-done.12.p1, ...), custom_call_target="tpu_custom_call" | custom-call | flops 2000000000 | bytes 1048576 | tf_op jit(solution)/shard_map/whiten/pallas_call | solution.py:54
  (8 shorter events, 0.2 us)
Async XLA Ops:
  7.2 11.1 %copy-start.1 = (bf16[1024,1024]{1,0:T(8,128)(2,1)S(1)}, bf16[1024,1024]{1,0:T(8,128)(2,1)}, u32[]{:S(2)}) copy-start(bf16[1024,1024]{1,0:T(8,128)(2,1)} %x.1) | copy-start | bytes 6291460
  8.1 10.3 %collective-permute-start = (bf16[16,512]{1,0:T(8,128)(2,1)S(1)}, bf16[16,512]{1,0:T(8,128)(2,1)S(1)}, u32[]{:S(2)}, u32[]{:S(2)}) collective-permute-start(bf16[16,512]{1,0:T(8,128)(2,1)S(1)} %get-tuple-element.33), channel_id=1, source_target_pairs={{0,8},{8,16},{16,24},{24,32},{32,40},{40,48},{48,56},{56,64},{64,7... | collective-permute-start | bytes 49160 | tf_op jit(solution)/shard_map/ppermute | solution.py:46
  8.7 9.7 %collective-permute-start.1 = (bf16[16,512]{1,0:T(8,128)(2,1)S(1)}, bf16[16,512]{1,0:T(8,128)(2,1)S(1)}, u32[]{:S(2)}, u32[]{:S(2)}) collective-permute-start(bf16[16,512]{1,0:T(8,128)(2,1)S(1)} %get-tuple-element.32), channel_id=1, source_target_pairs={{8,0},{16,8},{24,16},{32,24},{40,32},{48,40},{56,48},{64,56},{72,6... | collective-permute-start | bytes 49160 | tf_op jit(solution)/shard_map/ppermute | solution.py:46
  11.4 11.2 %collective-permute-start.2 = (bf16[272,512]{1,0:T(8,128)(2,1)}, bf16[272,512]{1,0:T(8,128)(2,1)}, u32[]{:S(2)}, u32[]{:S(2)}) collective-permute-start(bf16[272,512]{1,0:T(8,128)(2,1)} %get-tuple-element.30), channel_id=1, source_target_pairs={{0,2},{8,10},{16,18},{24,26},{32,34},{40,42},{48,50},{56,58},{64,6... | collective-permute-start | bytes 835592 | tf_op jit(solution)/shard_map/ppermute | solution.py:46
  12.8 17.7 %collective-permute-start.3 = (bf16[272,512]{1,0:T(8,128)(2,1)}, bf16[272,512]{1,0:T(8,128)(2,1)}, u32[]{:S(2)}, u32[]{:S(2)}) collective-permute-start(bf16[272,512]{1,0:T(8,128)(2,1)} %get-tuple-element.29), channel_id=1, source_target_pairs={{0,1},{8,9},{16,17},{24,25},{32,33},{40,41},{48,49},{56,57},{64,65... | collective-permute-start | bytes 835592 | tf_op jit(solution)/shard_map/ppermute | solution.py:46
  14.1 16.5 %collective-permute-start.4 = (bf16[272,512]{1,0:T(8,128)(2,1)}, bf16[272,512]{1,0:T(8,128)(2,1)}, u32[]{:S(2)}, u32[]{:S(2)}) collective-permute-start(bf16[272,512]{1,0:T(8,128)(2,1)} %get-tuple-element.31), channel_id=1, source_target_pairs={{0,3},{8,11},{16,19},{24,27},{32,35},{40,43},{48,51},{56,59},{64,6... | collective-permute-start | bytes 835592 | tf_op jit(solution)/shard_map/ppermute | solution.py:46
  31.8 0.7 collective-permute-start.5
  33.5 14.8 %all-to-all-start = ((f32[4,64,640]{2,1,0:T(8,128)}), f32[4,64,640]{2,1,0:T(8,128)S(1)}, u32[]{:S(2)}, u32[]{:S(2)}) async-start(f32[4,64,640]{2,1,0:T(8,128)} %bitcast.9), calls=%async_computation | async-start | bytes 1310720 | tf_op jit(solution)/shard_map/all_to_all | solution.py:301
  37.7 100.6 %reduce-scatter.2.cloned.1.call-start = ((), (), s32[]{:S(2)}) async-start(), calls=%async_computation.5 | async-start | bytes 4718592 | tf_op jit(solution)/shard_map/reduce_scatter | solution.py:383
  37.7 10.5 %collective-permute-start.6 = (bf16[272,512]{1,0:T(8,128)(2,1)S(1)}, bf16[272,512]{1,0:T(8,128)(2,1)S(1)}, u32[]{:S(2)}, u32[]{:S(2)}) collective-permute-start(bf16[272,512]{1,0:T(8,128)(2,1)S(1)} %maximum_select_fusion), channel_id=1, source_target_pairs={{0,4},{1,5},{2,6},{3,7},{8,12},{9,13},{10,14},{11,15},{16,20},{17,... | collective-permute-start | bytes 835592 | tf_op jit(solution)/shard_map/ppermute | solution.py:46
  48.3 19.0 %collective-permute-start.7 = (bf16[272,512]{1,0:T(8,128)(2,1)S(1)}, bf16[272,512]{1,0:T(8,128)(2,1)S(1)}, u32[]{:S(2)}, u32[]{:S(2)}) collective-permute-start(bf16[272,512]{1,0:T(8,128)(2,1)S(1)} %broadcast_select_fusion.g0), channel_id=1, source_target_pairs={{0,1},{1,2},{2,3},{3,0},{4,5},{5,6},{6,7},{7,4},{8,9},{9,10},{10,1... | collective-permute-start | bytes 835592 | tf_op jit(solution)/shard_map/ppermute | solution.py:46
  48.4 18.9 %collective-permute-start.8 = (bf16[272,512]{1,0:T(8,128)(2,1)S(1)}, bf16[272,512]{1,0:T(8,128)(2,1)S(1)}, u32[]{:S(2)}, u32[]{:S(2)}) collective-permute-start(bf16[272,512]{1,0:T(8,128)(2,1)S(1)} %broadcast_select_fusion.g0), channel_id=1, source_target_pairs={{0,2},{1,3},{2,0},{3,1},{4,6},{5,7},{6,4},{7,5},{8,10},{9,11},{10,... | collective-permute-start | bytes 835592 | tf_op jit(solution)/shard_map/ppermute | solution.py:46
  54.0 13.3 %collective-permute-start.9 = (bf16[272,512]{1,0:T(8,128)(2,1)S(1)}, bf16[272,512]{1,0:T(8,128)(2,1)S(1)}, u32[]{:S(2)}, u32[]{:S(2)}) collective-permute-start(bf16[272,512]{1,0:T(8,128)(2,1)S(1)} %broadcast_select_fusion.g0), channel_id=1, source_target_pairs={{0,3},{1,0},{2,1},{3,2},{4,7},{5,4},{6,5},{7,6},{8,11},{9,8},{10,9... | collective-permute-start | bytes 835592 | tf_op jit(solution)/shard_map/ppermute | solution.py:46
  73.1 2.0 %copy-start = (f32[8,128,1024]{2,1,0:T(8,128)}, f32[8,128,1024]{2,1,0:T(8,128)S(1)}, u32[]{:S(2)}) copy-start(f32[8,128,1024]{2,1,0:T(8,128)S(1)} %covariance.1) | copy-start | bytes 12582916
  75.1 0.7 collective-permute-start.10
  118.1 2.1 %collective-permute-start.11 = (f32[256,640]{1,0:T(8,128)S(1)}, f32[256,640]{1,0:T(8,128)S(1)}, u32[]{:S(2)}, u32[]{:S(2)}) collective-permute-start(f32[256,640]{1,0:T(8,128)S(1)} %bitcast.17), channel_id=1, source_target_pairs={{0,8},{1,9},{2,10},{3,11},{4,12},{5,13},{6,14},{7,15},{8,0},{9,1},... | collective-permute-start | bytes 1966088 | tf_op jit(solution)/shard_map/ppermute | solution.py:46
  139.5 12.5 %collective-permute-start.12 = (f32[32,1024]{1,0:T(8,128)S(1)}, f32[32,1024]{1,0:T(8,128)S(1)}, u32[]{:S(2)}, u32[]{:S(2)}) collective-permute-start(f32[32,1024]{1,0:T(8,128)S(1)} %get-tuple-element.36), channel_id=1, source_target_pairs={{0,128},{1,129},{2,130},{3,131},{4,132},{5,133},{6,134},{7,135},{8... | collective-permute-start | bytes 393224 | tf_op jit(solution)/shard_map/ppermute | solution.py:46
  140.4 11.5 %collective-permute-start.13 = (f32[32,1024]{1,0:T(8,128)S(1)}, f32[32,1024]{1,0:T(8,128)S(1)}, u32[]{:S(2)}, u32[]{:S(2)}) collective-permute-start(f32[32,1024]{1,0:T(8,128)S(1)} %get-tuple-element.35), channel_id=1, source_target_pairs={{0,64},{1,65},{2,66},{3,67},{4,68},{5,69},{6,70},{7,71},{8,72},{9,... | collective-permute-start | bytes 393224 | tf_op jit(solution)/shard_map/ppermute | solution.py:46
  141.5 10.4 %collective-permute-start.14 = (f32[32,1024]{1,0:T(8,128)S(1)}, f32[32,1024]{1,0:T(8,128)S(1)}, u32[]{:S(2)}, u32[]{:S(2)}) collective-permute-start(f32[32,1024]{1,0:T(8,128)S(1)} %get-tuple-element.34), channel_id=1, source_target_pairs={{0,192},{1,193},{2,194},{3,195},{4,196},{5,197},{6,198},{7,199},{8... | collective-permute-start | bytes 393224 | tf_op jit(solution)/shard_map/ppermute | solution.py:46
Sparse Core Ops, SparseCore 0:
  75.3 50.6 reduce-scatter.1
where the time goes:
time: 165 us; the launch traced here: 162 us
  blocking collectives  55.4 us (34%)
  Pallas kernels  36.8 us (22%)
  starting transfers between devices  22.9 us (14%)
  waiting for transfers between devices  21.5 us (13%)
  between operations  14.3 us (9%)
  local copies, waits for them, and re-layouts  8.2 us (5%)
  other arithmetic  3.04 us (2%)
    all_to_all x3, blocking collectives, exchange(): return lax.all_to_all(v, axes, 0, 0, tiled=True)  55.4 us
    pallas_call x7, Pallas kernels, call(): pl.pallas_call(kernel, out_shape=outs, in_specs=specs, out_specs=[pl.Bloc...  36.8 us
    ppermute x15, starting transfers between devices, move(): return lax.ppermute(value, AXES, pairs)  18.6 us
    ppermute x15, waiting for transfers between devices, move(): return lax.ppermute(value, AXES, pairs)  12.5 us
    all_to_all x1, waiting for transfers between devices, exchange(): return lax.all_to_all(v, axes, 0, 0, tiled=True)  8.99 us
    all_to_all x1, starting transfers between devices, exchange(): return lax.all_to_all(v, axes, 0, 0, tiled=True)  4.28 us
  transfers between devices with their start and end apart: 17, of which 4 were waited for; matrix products, arithmetic and copies ran while one was open for 3% of the time, Pallas kernels for 17%

commit v1 on v0

--- a/solution.py
+++ b/solution.py
@@ -46,13 +46,16 @@
     return lax.ppermute(value, AXES, pairs)
 
 
-def call(kernel, outs, args, name, scratch=(), flops=0, vmem=16, hbm=()):
+def call(kernel, outs, args, name, scratch=(), flops=0, vmem=16, hbm=(), block=None):
     specs = [pl.BlockSpec(memory_space=pltpu.VMEM)] * len(args)
     specs[0] = pl.BlockSpec(memory_space=pltpu.SMEM)
     for i in hbm:
         specs[i] = pl.BlockSpec(memory_space=pltpu.HBM)
+    for i, shape in (block or {}).items():
+        specs[i] = pl.BlockSpec(shape, lambda i: (0, 0))
     return pl.pallas_call(
         kernel,
+        grid=(1,),
         out_shape=outs,
         in_specs=specs,
         out_specs=[pl.BlockSpec(memory_space=pltpu.VMEM)] * len(outs),
@@ -318,11 +321,6 @@
     return jnp.sum(exchange(quarter.reshape(4, 16, quarter.shape[1]), "z"), axis=0)
 
 
-def diag_feat(own, w):
-    over = move(own, lambda z, y, c, w, x: (z, y, c, 1, 0) if (w, x) == (0, 0) else None)
-    return spread(jnp.where(w == 0, own, over), "x", 4)[0]
-
-
 def diag_gather(own):
     half = spread(own, ("y", "z"), 16).reshape(256, own.shape[1])
     return half, swap_core(half)
@@ -348,20 +346,18 @@
     before = move(panel[tok - RIM :], step(1))
 
     packed = jax.ShapeDtypeStruct((256, P_SIZE + NB), F32)
-    dz = call(
-        diag_kernel, [packed, packed], (pos, table, panel, before, behind), "diagonal",
+    mine, theirs = call(
+        diag_kernel, [packed, packed], (pos, table, frames_data, before, behind), "diagonal",
         scratch=[pltpu.VMEM((tok + 2 * RIM, P_SIZE), BF16), pltpu.VMEM((tok, 3 * P_SIZE), BF16)],
-        flops=3 * 10**9,
-    )
+        flops=3 * 10**9, block={2: (tok, P_SIZE)},
+    )
+    theirs, *chunks = together(theirs, *(panel[STEP0 + CHUNK * (k - 1) : STEP0 + CHUNK * k] for k in (2, 1, 3)))
     sent = [
-        move(panel[STEP0 + CHUNK * (k - 1) : STEP0 + CHUNK * k],
-             lambda z, y, c, w, x: (z, y, c, w, k) if (w, x) == (0, 0) else None)
-        for k in (2, 1, 3)
+        move(v, lambda z, y, c, w, x: (z, y, c, w, k) if (w, x) == (0, 0) else None)
+        for k, v in zip((2, 1, 3), chunks)
     ]
     first = jnp.concatenate([before, behind, panel[:FIRST]], axis=0)
     hold = jnp.where(x == 0, first, sent[0] + sent[1] + sent[2])
-    mine, theirs = dz
-    theirs, hold = together(theirs, hold)
     over = move(hold, lambda z, y, c, w, x: (z, y, c, 1, x) if w == 0 else None)
     quarter, over = together(diag_half(mine, theirs), over)
     rows16 = diag_rows(quarter)
@@ -369,8 +365,9 @@
     gathered = [hold] + [
         move(hold, lambda z, y, c, w, x: (z, y, c, w, (x + k) % 4)) for k in (1, 2, 3)
     ]
-    rows16, *gathered = together(rows16, *gathered)
-    own, other = diag_gather(diag_feat(rows16, w))
+    over = move(rows16, lambda z, y, c, w, x: (z, y, c, 1, 0) if (w, x) == (0, 0) else None)
+    over, *gathered = together(over, *gathered)
+    own, other = diag_gather(spread(jnp.where(w == 0, rows16, over), "x", 4)[0])
     (part,) = call(
         cov_kernel, [jax.ShapeDtypeStruct((8, 128, 2 * P_SIZE), F32)], (pos, table, frames_data, *gathered), "covariance",
         scratch=[

time: 165 us -> 163 us (0.988)
  the two profiles are of different devices: /device:TPU:2 before, /device:TPU:161 now
where the time goes in v1:
time: 163 us; the launch traced here: 162 us
  waiting for transfers between devices  42.7 us (26%)
  Pallas kernels  36.8 us (23%)
  blocking collectives  29.4 us (18%)
  starting transfers between devices  26 us (16%)
  between operations  14.2 us (9%)
  local copies, waits for them, and re-layouts  8.31 us (5%)
  other arithmetic  4.83 us (3%)
    pallas_call x7, Pallas kernels, call(): pl.pallas_call(kernel, grid=(1,), out_shape=outs, in_specs=specs, out_spe...  36.8 us
    ppermute x15, waiting for transfers between devices, move(): return lax.ppermute(value, AXES, pairs)  35.4 us
    all_to_all x2, blocking collectives, exchange(): return lax.all_to_all(v, axes, 0, 0, tiled=True)  29.4 us
    ppermute x15, starting transfers between devices, move(): return lax.ppermute(value, AXES, pairs)  18.4 us
    all_to_all x2, starting transfers between devices, exchange(): return lax.all_to_all(v, axes, 0, 0, tiled=True)  7.51 us
    all_to_all x2, waiting for transfers between devices, exchange(): return lax.all_to_all(v, axes, 0, 0, tiled=True)  7.21 us
    unnamed x6, local copies, waits for them, and re-layouts  3.53 us
  transfers between devices with their start and end apart: 18, of which 8 were waited for; matrix products, arithmetic and copies ran while one was open for 5% of the time, Pallas kernels for 14%

profile of v1, /device:TPU:161, one launch (start us, length us, event | category | flops | bytes accessed | tf_op | source)
XLA Modules:
  0.0 162.2 jit_solution(7654364265338261751)
XLA Ops:
  7.2 0.7 fusion.1
  7.9 0.7 collective-permute-start
  8.6 0.7 collective-permute-start.1
  9.2 2.0 %fusion = (bf16[272,512]{1,0:T(8,128)(2,1)S(1)}, bf16[272,512]{1,0:T(8,128)(2,1)}, bf16[272,512]{1,0:T(8,128)(2,1)}) fusion(bf16[1024,1024]{1,0:T(8,128)(2,1)} %x.1), kind=kLoop, calls=%fused_computation.6 | loop fusion | bytes 1671168 | tf_op jit(solution)/shard_map/slice | solution.py:354
  11.3 0.7 slice.43
  12.0 0.1 add_bitcast_fusion
  12.1 0.7 pad_add_fusion.table
  12.7 0.1 stack.39.pos
  12.8 0.0 collective-permute-done.before
  12.8 0.0 collective-permute-done.1.after
  12.8 0.0 copy-start.1
  12.8 1.6 copy-done.1
  14.4 4.2 %diagonal.1 = (f32[256,640]{1,0:T(8,128)S(1)}, f32[256,640]{1,0:T(8,128)S(1)}) custom-call(s32[6]{0:T(128)S(1)} %stack.39.pos, s32[3,64]{1,0:T(4,128)S(1)} %pad_add_fusion.table, bf16[1024,1024]{1,0:T(8,128)(2,1)S(1)} %copy-done.1, bf16[16,512]{1,0:T(8,128)(2,1)S(1)} %collective-permute-done.before, bf16[16,512]{1,0:T(8,128)(2,1)S(1)} %collective-permute-done.1.after), custom_call_target="tpu_custom_call" | custom-call | flops 3000000000 | bytes 1048576 | tf_op jit(solution)/shard_map/diagonal/pallas_call | solution.py:56
  18.6 0.7 collective-permute-start.2
  19.3 1.4 collective-permute-start.3
  20.7 1.4 collective-permute-start.4
  22.1 1.4 collective-permute-start.5
  23.5 0.0 collective-permute-done.2
  23.5 0.9 add.19
  24.4 4.2 %all-to-all-start = ((f32[4,64,640]{2,1,0:T(8,128)}), f32[4,64,640]{2,1,0:T(8,128)S(1)}, u32[]{:S(2)}, u32[]{:S(2)}) async-start(f32[4,64,640]{2,1,0:T(8,128)} %bitcast.9), calls=%async_computation | async-start | bytes 1310720 | tf_op jit(solution)/shard_map/all_to_all | solution.py:304
  28.6 0.0 copy-start.2
  28.6 0.0 collective-permute-done.3
  28.6 0.0 collective-permute-done.4
  28.6 0.0 collective-permute-done.5
  28.6 1.4 maximum_select_fusion
  30.0 1.3 collective-permute-start.6
  31.3 7.2 %all-to-all-done = f32[4,64,640]{2,1,0:T(8,128)S(1)} async-done(((f32[4,64,640]{2,1,0:T(8,128)}), f32[4,64,640]{2,1,0:T(8,128)S(1)}, u32[]{:S(2)}, u32[]{:S(2)}) %all-to-all-start) | async-done | bytes 655392 | tf_op jit(solution)/shard_map/all_to_all | solution.py:304
  38.6 0.7 reduce_sum.18
  39.2 16.6 %collective-permute-done.6 = bf16[272,512]{1,0:T(8,128)(2,1)} collective-permute-done((bf16[272,512]{1,0:T(8,128)(2,1)S(1)}, bf16[272,512]{1,0:T(8,128)(2,1)}, u32[]{:S(2)}, u32[]{:S(2)}) %collective-permute-start.6) | collective-permute-done | bytes 278560 | tf_op jit(solution)/shard_map/ppermute | solution.py:46
  55.9 3.3 %all-to-all-start.1 = ((f32[4,16,640]{2,1,0:T(8,128)}), f32[4,16,640]{2,1,0:T(8,128)S(1)}, u32[]{:S(2)}, u32[]{:S(2)}) async-start(f32[4,16,640]{2,1,0:T(8,128)} %bitcast.10), calls=%async_computation.1 | async-start | bytes 327680 | tf_op jit(solution)/shard_map/all_to_all | solution.py:304
  59.2 0.0 reduce-scatter.2.cloned.1.call-start
  59.2 1.0 broadcast_select_fusion.g0
  60.3 1.3 collective-permute-start.10
  61.6 1.0 collective-permute-start.8
  62.6 1.7 %collective-permute-start.9 = (bf16[272,512]{1,0:T(8,128)(2,1)S(1)}, bf16[272,512]{1,0:T(8,128)(2,1)S(1)}, u32[]{:S(2)}, u32[]{:S(2)}) collective-permute-start(bf16[272,512]{1,0:T(8,128)(2,1)S(1)} %broadcast_select_fusion.g0), channel_id=1, source_target_pairs={{0,2},{1,3},{2,0},{3,1},{4,6},{5,7},{6,4},{7,5},{8,10},{9,11},{10,... | collective-permute-start | bytes 835592 | tf_op jit(solution)/shard_map/ppermute | solution.py:46
  64.3 0.0 all-to-all-done.1
  64.3 1.3 collective-permute-start.7
  65.6 2.7 %collective-permute-done.10.g3 = bf16[272,512]{1,0:T(8,128)(2,1)S(1)} collective-permute-done((bf16[272,512]{1,0:T(8,128)(2,1)S(1)}, bf16[272,512]{1,0:T(8,128)(2,1)S(1)}, u32[]{:S(2)}, u32[]{:S(2)}) %collective-permute-start.10) | collective-permute-done | bytes 278560 | tf_op jit(solution)/shard_map/ppermute | solution.py:46
  68.4 1.1 collective-permute-done.8.g1
  69.5 6.3 %collective-permute-done.9.g2 = bf16[272,512]{1,0:T(8,128)(2,1)S(1)} collective-permute-done((bf16[272,512]{1,0:T(8,128)(2,1)S(1)}, bf16[272,512]{1,0:T(8,128)(2,1)S(1)}, u32[]{:S(2)}, u32[]{:S(2)}) %collective-permute-start.9) | collective-permute-done | bytes 278560 | tf_op jit(solution)/shard_map/ppermute | solution.py:46
  75.8 0.0 collective-permute-done.7
  75.8 0.0 copy-done.2
  75.8 5.9 %covariance.1 = f32[8,128,1024]{2,1,0:T(8,128)S(1)} custom-call(s32[6]{0:T(128)S(1)} %stack.39.pos, s32[3,64]{1,0:T(4,128)S(1)} %pad_add_fusion.table, bf16[1024,1024]{1,0:T(8,128)(2,1)S(1)} %copy-done.2, bf16[272,512]{1,0:T(8,128)(2,1)S(1)} %broadcast_select_fusion.g0, bf16[272,512]{1,0:T(8,128)(2,1)S(1)} %collective-permute-done.8.g1, ...), custom_call_target="tpu_custom_call" | custom-call | flops 5000000000 | bytes 1048576 | tf_op jit(solution)/shard_map/covariance/pallas_call | solution.py:56
  81.8 0.0 copy-start
  81.8 1.9 %copy-done = f32[8,128,1024]{2,1,0:T(8,128)} copy-done((f32[8,128,1024]{2,1,0:T(8,128)}, f32[8,128,1024]{2,1,0:T(8,128)S(1)}, u32[]{:S(2)}) %copy-start) | copy-done | bytes 4194328
  83.7 0.0 reduce-scatter.2.cloned.1.call-update
  83.8 7.4 %all_to_all.20 = f32[4,16,640]{2,1,0:T(8,128)S(1)} all-to-all(f32[4,16,640]{2,1,0:T(8,128)S(1)} %broadcast_in_dim.6), channel_id=1, replica_groups=mesh['z'=4,'y'=4,'c'=2,'w'=2,'x'=4] {'x'}, dimensions={0} | all-to-all | bytes 327680 | tf_op jit(solution)/shard_map/all_to_all | solution.py:304
  91.2 22.0 %all_to_all.21 = f32[16,16,640]{2,1,0:T(8,128)S(1)} all-to-all(f32[16,16,640]{2,1,0:T(8,128)S(1)} %broadcast_in_dim.15), channel_id=1, replica_groups=mesh['z'=4,'y'=4,'c'=2,'w'=2,'x'=4] {'y','z'}, dimensions={0} | all-to-all | bytes 1310720 | tf_op jit(solution)/shard_map/all_to_all | solution.py:304
  113.3 3.1 %collective-permute-start.11 = (f32[256,640]{1,0:T(8,128)S(1)}, f32[256,640]{1,0:T(8,128)S(1)}, u32[]{:S(2)}, u32[]{:S(2)}) collective-permute-start(f32[256,640]{1,0:T(8,128)S(1)} %bitcast.17), channel_id=1, source_target_pairs={{0,8},{1,9},{2,10},{3,11},{4,12},{5,13},{6,14},{7,15},{8,0},{9,1},... | collective-permute-start | bytes 1966088 | tf_op jit(solution)/shard_map/ppermute | solution.py:46
  116.4 1.7 %collective-permute-done.11.other = f32[256,640]{1,0:T(8,128)S(1)} collective-permute-done((f32[256,640]{1,0:T(8,128)S(1)}, f32[256,640]{1,0:T(8,128)S(1)}, u32[]{:S(2)}, u32[]{:S(2)}) %collective-permute-start.11) | collective-permute-done | bytes 655392 | tf_op jit(solution)/shard_map/ppermute | solution.py:46
  118.1 6.5 %factor0.1 = (f32[512,512]{1,0:T(8,128)S(1)}, f32[512,512]{1,0:T(8,128)S(1)}) custom-call(s32[6]{0:T(128)S(1)} %stack.39.pos, f32[256,640]{1,0:T(8,128)S(1)} %bitcast.18, f32[256,640]{1,0:T(8,128)S(1)} %collective-permute-done.11.other), custom_call_target="tpu_custom_call" | custom-call | flops 5000000000 | bytes 1048576 | tf_op jit(solution)/shard_map/factor0/pallas_call | solution.py:56
  124.6 6.0 %factor128.1.v = f32[512,512]{1,0:T(8,128)S(1)} custom-call(s32[6]{0:T(128)S(1)} %stack.39.pos, f32[512,512]{1,0:T(8,128)S(1)} %get-tuple-element.27.v), custom_call_target="tpu_custom_call" | custom-call | flops 5000000000 | bytes 1048576 | tf_op jit(solution)/shard_map/factor128/pallas_call | solution.py:56
  130.6 5.7 %factor256.1.v = f32[512,512]{1,0:T(8,128)S(1)} custom-call(s32[6]{0:T(128)S(1)} %stack.39.pos, f32[512,512]{1,0:T(8,128)S(1)} %factor128.1.v), custom_call_target="tpu_custom_call" | custom-call | flops 5000000000 | bytes 1048576 | tf_op jit(solution)/shard_map/factor256/pallas_call | solution.py:56
  136.2 0.0 reduce-scatter.2.cloned.1.call-done
  136.3 1.1 fusion.2
  137.4 1.0 collective-permute-start.12
  138.5 1.3 collective-permute-start.13
  139.7 0.2 collective-permute-start.14
  139.9 5.2 %factor384.1.inv = f32[512,512]{1,0:T(8,128)S(1)} custom-call(s32[6]{0:T(128)S(1)} %stack.39.pos, f32[512,512]{1,0:T(8,128)S(1)} %factor256.1.v), custom_call_target="tpu_custom_call" | custom-call | flops 5000000000 | bytes 1048576 | tf_op jit(solution)/shard_map/factor384/pallas_call | solution.py:56
  145.1 0.0 collective-permute-done.12.p1
  145.1 4.6 %collective-permute-done.13.p2 = f32[32,1024]{1,0:T(8,128)S(1)} collective-permute-done((f32[32,1024]{1,0:T(8,128)S(1)}, f32[32,1024]{1,0:T(8,128)S(1)}, u32[]{:S(2)}, u32[]{:S(2)}) %collective-permute-start.13) | collective-permute-done | bytes 131104 | tf_op jit(solution)/shard_map/ppermute | solution.py:46
  149.8 2.3 %collective-permute-done.14.p3 = f32[32,1024]{1,0:T(8,128)S(1)} collective-permute-done((f32[32,1024]{1,0:T(8,128)S(1)}, f32[32,1024]{1,0:T(8,128)S(1)}, u32[]{:S(2)}, u32[]{:S(2)}) %collective-permute-start.14) | collective-permute-done | bytes 131104 | tf_op jit(solution)/shard_map/ppermute | solution.py:46
  152.0 3.4 %whiten.1 = (f32[1,32,512]{2,1,0:T(8,128)}, f32[1,32,512]{2,1,0:T(8,128)}, f32[16,512]{1,0:T(8,128)}) custom-call(s32[6]{0:T(128)S(1)} %stack.39.pos, f32[512,512]{1,0:T(8,128)S(1)} %factor384.1.inv, f32[512,512]{1,0:T(8,128)S(1)} %get-tuple-element.28.up, f32[32,1024]{1,0:T(8,128)S(1)} %get-tuple-element.41.p0, f32[32,1024]{1,0:T(8,128)S(1)} %collective-permute-done.12.p1, ...), custom_call_target="tpu_custom_call" | custom-call | flops 2000000000 | bytes 1048576 | tf_op jit(solution)/shard_map/whiten/pallas_call | solution.py:56
  (6 shorter events, 0.1 us)
Async XLA Ops:
  7.9 4.9 %collective-permute-start = (bf16[16,512]{1,0:T(8,128)(2,1)S(1)}, bf16[16,512]{1,0:T(8,128)(2,1)S(1)}, u32[]{:S(2)}, u32[]{:S(2)}) collective-permute-start(bf16[16,512]{1,0:T(8,128)(2,1)S(1)} %get-tuple-element.37), channel_id=1, source_target_pairs={{0,8},{8,16},{16,24},{24,32},{32,40},{40,48},{48,56},{56,64},{64,7... | collective-permute-start | bytes 49160 | tf_op jit(solution)/shard_map/ppermute | solution.py:46
  8.6 4.3 %collective-permute-start.1 = (bf16[16,512]{1,0:T(8,128)(2,1)S(1)}, bf16[16,512]{1,0:T(8,128)(2,1)S(1)}, u32[]{:S(2)}, u32[]{:S(2)}) collective-permute-start(bf16[16,512]{1,0:T(8,128)(2,1)S(1)} %get-tuple-element.36), channel_id=1, source_target_pairs={{8,0},{16,8},{24,16},{32,24},{40,32},{48,40},{56,48},{64,56},{72,6... | collective-permute-start | bytes 49160 | tf_op jit(solution)/shard_map/ppermute | solution.py:46
  12.8 1.6 copy-start.1
  18.6 4.9 %collective-permute-start.2 = (f32[256,640]{1,0:T(8,128)S(1)}, f32[256,640]{1,0:T(8,128)S(1)}, u32[]{:S(2)}, u32[]{:S(2)}) collective-permute-start(f32[256,640]{1,0:T(8,128)S(1)} %get-tuple-element.20), channel_id=1, source_target_pairs={{0,8},{8,0},{16,24},{24,16},{32,40},{40,32},{48,56},{56,48},{64,72... | collective-permute-start | bytes 1966088 | tf_op jit(solution)/shard_map/ppermute | solution.py:46
  19.3 9.3 %collective-permute-start.3 = (bf16[272,512]{1,0:T(8,128)(2,1)}, bf16[272,512]{1,0:T(8,128)(2,1)}, u32[]{:S(2)}, u32[]{:S(2)}) collective-permute-start(bf16[272,512]{1,0:T(8,128)(2,1)} %get-tuple-element.21), channel_id=1, source_target_pairs={{0,2},{8,10},{16,18},{24,26},{32,34},{40,42},{48,50},{56,58},{64,6... | collective-permute-start | bytes 835592 | tf_op jit(solution)/shard_map/ppermute | solution.py:46
  20.7 7.9 %collective-permute-start.4 = (bf16[272,512]{1,0:T(8,128)(2,1)}, bf16[272,512]{1,0:T(8,128)(2,1)}, u32[]{:S(2)}, u32[]{:S(2)}) collective-permute-start(bf16[272,512]{1,0:T(8,128)(2,1)} %get-tuple-element.22), channel_id=1, source_target_pairs={{0,1},{8,9},{16,17},{24,25},{32,33},{40,41},{48,49},{56,57},{64,65... | collective-permute-start | bytes 835592 | tf_op jit(solution)/shard_map/ppermute | solution.py:46
  22.1 6.5 %collective-permute-start.5 = (bf16[272,512]{1,0:T(8,128)(2,1)S(1)}, bf16[272,512]{1,0:T(8,128)(2,1)}, u32[]{:S(2)}, u32[]{:S(2)}) collective-permute-start(bf16[272,512]{1,0:T(8,128)(2,1)S(1)} %get-tuple-element.23), channel_id=1, source_target_pairs={{0,3},{8,11},{16,19},{24,27},{32,35},{40,43},{48,51},{56,59},{64,6... | collective-permute-start | bytes 835592 | tf_op jit(solution)/shard_map/ppermute | solution.py:46
  24.4 14.1 %all-to-all-start = ((f32[4,64,640]{2,1,0:T(8,128)}), f32[4,64,640]{2,1,0:T(8,128)S(1)}, u32[]{:S(2)}, u32[]{:S(2)}) async-start(f32[4,64,640]{2,1,0:T(8,128)} %bitcast.9), calls=%async_computation | async-start | bytes 1310720 | tf_op jit(solution)/shard_map/all_to_all | solution.py:304
  28.6 47.3 %copy-start.2 = (bf16[1024,1024]{1,0:T(8,128)(2,1)S(1)}, bf16[1024,1024]{1,0:T(8,128)(2,1)}, u32[]{:S(2)}) copy-start(bf16[1024,1024]{1,0:T(8,128)(2,1)} %x.1) | copy-start | bytes 6291460
  30.0 25.8 %collective-permute-start.6 = (bf16[272,512]{1,0:T(8,128)(2,1)S(1)}, bf16[272,512]{1,0:T(8,128)(2,1)}, u32[]{:S(2)}, u32[]{:S(2)}) collective-permute-start(bf16[272,512]{1,0:T(8,128)(2,1)S(1)} %maximum_select_fusion), channel_id=1, source_target_pairs={{0,4},{1,5},{2,6},{3,7},{8,12},{9,13},{10,14},{11,15},{16,20},{17,... | collective-permute-start | bytes 835592 | tf_op jit(solution)/shard_map/ppermute | solution.py:46
  55.9 8.5 %all-to-all-start.1 = ((f32[4,16,640]{2,1,0:T(8,128)}), f32[4,16,640]{2,1,0:T(8,128)S(1)}, u32[]{:S(2)}, u32[]{:S(2)}) async-start(f32[4,16,640]{2,1,0:T(8,128)} %bitcast.10), calls=%async_computation.1 | async-start | bytes 327680 | tf_op jit(solution)/shard_map/all_to_all | solution.py:304
  59.2 77.1 %reduce-scatter.2.cloned.1.call-start = ((), (), s32[]{:S(2)}) async-start(), calls=%async_computation.5 | async-start | bytes 4718592 | tf_op jit(solution)/shard_map/reduce_scatter | solution.py:380
  60.3 8.1 %collective-permute-start.10 = (bf16[272,512]{1,0:T(8,128)(2,1)S(1)}, bf16[272,512]{1,0:T(8,128)(2,1)S(1)}, u32[]{:S(2)}, u32[]{:S(2)}) collective-permute-start(bf16[272,512]{1,0:T(8,128)(2,1)S(1)} %broadcast_select_fusion.g0), channel_id=1, source_target_pairs={{0,3},{1,0},{2,1},{3,2},{4,7},{5,4},{6,5},{7,6},{8,11},{9,8},{10,9... | collective-permute-start | bytes 835592 | tf_op jit(solution)/shard_map/ppermute | solution.py:46
  61.6 7.9 %collective-permute-start.8 = (bf16[272,512]{1,0:T(8,128)(2,1)S(1)}, bf16[272,512]{1,0:T(8,128)(2,1)S(1)}, u32[]{:S(2)}, u32[]{:S(2)}) collective-permute-start(bf16[272,512]{1,0:T(8,128)(2,1)S(1)} %broadcast_select_fusion.g0), channel_id=1, source_target_pairs={{0,1},{1,2},{2,3},{3,0},{4,5},{5,6},{6,7},{7,4},{8,9},{9,10},{10,1... | collective-permute-start | bytes 835592 | tf_op jit(solution)/shard_map/ppermute | solution.py:46
  62.6 13.2 %collective-permute-start.9 = (bf16[272,512]{1,0:T(8,128)(2,1)S(1)}, bf16[272,512]{1,0:T(8,128)(2,1)S(1)}, u32[]{:S(2)}, u32[]{:S(2)}) collective-permute-start(bf16[272,512]{1,0:T(8,128)(2,1)S(1)} %broadcast_select_fusion.g0), channel_id=1, source_target_pairs={{0,2},{1,3},{2,0},{3,1},{4,6},{5,7},{6,4},{7,5},{8,10},{9,11},{10,... | collective-permute-start | bytes 835592 | tf_op jit(solution)/shard_map/ppermute | solution.py:46
  64.3 11.5 %collective-permute-start.7 = (f32[16,640]{1,0:T(8,128)S(1)}, f32[16,640]{1,0:T(8,128)S(1)}, u32[]{:S(2)}, u32[]{:S(2)}) collective-permute-start(f32[16,640]{1,0:T(8,128)S(1)} %reduce_sum.19), channel_id=1, source_target_pairs={{0,4},{8,12},{16,20},{24,28},{32,36},{40,44},{48,52},{56,60},{64,6... | collective-permute-start | bytes 122888 | tf_op jit(solution)/shard_map/ppermute | solution.py:46
  81.8 1.9 %copy-start = (f32[8,128,1024]{2,1,0:T(8,128)}, f32[8,128,1024]{2,1,0:T(8,128)S(1)}, u32[]{:S(2)}) copy-start(f32[8,128,1024]{2,1,0:T(8,128)S(1)} %covariance.1) | copy-start | bytes 12582916
  113.3 4.8 %collective-permute-start.11 = (f32[256,640]{1,0:T(8,128)S(1)}, f32[256,640]{1,0:T(8,128)S(1)}, u32[]{:S(2)}, u32[]{:S(2)}) collective-permute-start(f32[256,640]{1,0:T(8,128)S(1)} %bitcast.17), channel_id=1, source_target_pairs={{0,8},{1,9},{2,10},{3,11},{4,12},{5,13},{6,14},{7,15},{8,0},{9,1},... | collective-permute-start | bytes 1966088 | tf_op jit(solution)/shard_map/ppermute | solution.py:46
  137.4 7.7 %collective-permute-start.12 = (f32[32,1024]{1,0:T(8,128)S(1)}, f32[32,1024]{1,0:T(8,128)S(1)}, u32[]{:S(2)}, u32[]{:S(2)}) collective-permute-start(f32[32,1024]{1,0:T(8,128)S(1)} %get-tuple-element.40), channel_id=1, source_target_pairs={{0,128},{1,129},{2,130},{3,131},{4,132},{5,133},{6,134},{7,135},{8... | collective-permute-start | bytes 393224 | tf_op jit(solution)/shard_map/ppermute | solution.py:46
  138.5 11.3 %collective-permute-start.13 = (f32[32,1024]{1,0:T(8,128)S(1)}, f32[32,1024]{1,0:T(8,128)S(1)}, u32[]{:S(2)}, u32[]{:S(2)}) collective-permute-start(f32[32,1024]{1,0:T(8,128)S(1)} %get-tuple-element.39), channel_id=1, source_target_pairs={{0,64},{1,65},{2,66},{3,67},{4,68},{5,69},{6,70},{7,71},{8,72},{9,... | collective-permute-start | bytes 393224 | tf_op jit(solution)/shard_map/ppermute | solution.py:46
  139.7 12.3 %collective-permute-start.14 = (f32[32,1024]{1,0:T(8,128)S(1)}, f32[32,1024]{1,0:T(8,128)S(1)}, u32[]{:S(2)}, u32[]{:S(2)}) collective-permute-start(f32[32,1024]{1,0:T(8,128)S(1)} %get-tuple-element.38), channel_id=1, source_target_pairs={{0,192},{1,193},{2,194},{3,195},{4,196},{5,197},{6,198},{7,199},{8... | collective-permute-start | bytes 393224 | tf_op jit(solution)/shard_map/ppermute | solution.py:46
Sparse Core Ops, SparseCore 0:
  83.9 43.3 reduce-scatter.1

commit v2 on v1

--- a/solution.py
+++ b/solution.py
@@ -11,6 +11,7 @@
 P_SIZE = 512
 RIM = 16
 NB = 128
+AHEAD = 3
 HI = lax.Precision.HIGHEST
 F32 = jnp.float32
 BF16 = jnp.bfloat16
@@ -46,7 +47,7 @@
     return lax.ppermute(value, AXES, pairs)
 
 
-def call(kernel, outs, args, name, scratch=(), flops=0, vmem=16, hbm=(), block=None):
+def call(kernel, outs, args, name, scratch=(), flops=0, vmem=16, hbm=(), block=None, out=pltpu.VMEM):
     specs = [pl.BlockSpec(memory_space=pltpu.VMEM)] * len(args)
     specs[0] = pl.BlockSpec(memory_space=pltpu.SMEM)
     for i in hbm:
@@ -58,7 +59,7 @@
         grid=(1,),
         out_shape=outs,
         in_specs=specs,
-        out_specs=[pl.BlockSpec(memory_space=pltpu.VMEM)] * len(outs),
+        out_specs=[pl.BlockSpec(memory_space=out)] * len(outs),
         scratch_shapes=list(scratch),
         compiler_params=pltpu.CompilerParams(vmem_limit_bytes=vmem * 2**20),
         cost_estimate=pl.CostEstimate(flops=flops, bytes_accessed=2**20, transcendentals=0),
@@ -156,9 +157,9 @@
         right[b : b + 256, 2 * n :] = zm
 
 
-def cov_kernel(pos, table, x, g0, g1, g2, g3, out, ext, right, sem):
-    rows, n = x.shape[0], P_SIZE
-    z, col = pos[3], pos[5]
+def select_kernel(pos, table, g0, g1, g2, g3, right, ext, sem):
+    rows, n = right.shape[0], P_SIZE
+    col = pos[5]
     for wait in (False, True):
         for k, g in enumerate((g0, g1, g2, g3)):
             q = lax.rem(col - k + 4, 4)
@@ -179,16 +180,35 @@
                 bring(g, ext.at[pl.ds(at, CHUNK), :], 0)
 
     fill_right(pos, table, ext, right, rows, n)
+
+
+def cov_kernel(pos, table, x, right, out, done, sent):
+    n = P_SIZE
+    z = pos[3]
     scale = 1.0 / pair_count(table)
+    leave = []
     for zz in range(4):
         left = x[:, 256 * zz : 256 * zz + 256]
         d0 = mm(left, right[:, :n]) * scale
         d1 = mm(left, right[:, n : 2 * n]) + mm(left, right[:, 2 * n :])
         d1 = d1 * (0.5 * scale)
         at = pl.multiple_of(lax.rem(zz - z + 4, 4) * 32, 32)
+        if zz >= 2:
+            leave[zz - 2].wait()
         for k in range(8):
-            out[k, pl.ds(at, 32), :n] = d0[32 * k : 32 * k + 32, :]
-            out[k, pl.ds(at, 32), n:] = d1[32 * k : 32 * k + 32, :]
+            done[zz % 2, k, :, :n] = d0[32 * k : 32 * k + 32, :]
+            done[zz % 2, k, :, n:] = d1[32 * k : 32 * k + 32, :]
+        leave.append(pltpu.make_async_copy(done.at[zz % 2], out.at[:, pl.ds(at, 32), :], sent.at[zz % 2]))
+        leave[zz].start()
+    leave[2].wait()
+    leave[3].wait()
+
+
+def parts(v):
+    hi = v.astype(BF16)
+    rest = v - hi.astype(F32)
+    mid = rest.astype(BF16)
+    return hi, mid, (rest - mid.astype(F32)).astype(BF16)
 
 
 def factor(s):
@@ -198,40 +218,42 @@
     lane = lax.broadcasted_iota(jnp.int32, (8, n), 1)
     for j in range(n // 8):
         r0 = 8 * j
-        look = j + 1 < n // 8
         block = (lane >= r0) & (lane < r0 + 8)
+        columns = lambda v: [jnp.broadcast_to(v[:, r0 + r : r0 + r + 1], (8, n)) for r in range(8)]
         rows = groups[j]
-        cols = [jnp.broadcast_to(rows[:, r0 + r : r0 + r + 1], (8, n)) for r in range(8)]
+        cols = columns(rows)
         rows = jnp.where(block, jnp.where(lane - r0 == sub, 1.0, 0.0), rows)
-        if look:
-            more = groups[j + 1]
-            below = [jnp.broadcast_to(more[:, r0 + r : r0 + r + 1], (8, n)) for r in range(8)]
-            more = jnp.where(block, 0.0, more)
+        far = min(j + 1 + AHEAD, n // 8)
+        near = range(j + 1, far)
+        below = {k: columns(groups[k]) for k in near}
+        more = {k: jnp.where(block, 0.0, groups[k]) for k in near}
         for r in range(8):
             rs = lax.rsqrt(cols[r][r : r + 1, :])
             l = cols[r] * rs
             lm = jnp.where(sub > r, l, 0.0)
             row = rows[r : r + 1, :] * rs
             rows = jnp.where(sub == r, row, rows - lm * row)
-            if look:
-                lq = below[r] * rs
-                more = more - lq * row
-            for s_ in range(r + 1, 8):
-                at = l[s_ : s_ + 1, :]
-                cols[s_] = cols[s_] - lm * at
-                if look:
-                    below[s_] = below[s_] - lq * at
+            lq = {k: below[k][r] * rs for k in near}
+            for k in near:
+                more[k] = more[k] - lq[k] * row
+            for t in range(r + 1, 8):
+                at = l[t : t + 1, :]
+                cols[t] = cols[t] - lm * at
+                for k in near:
+                    below[k][t] = below[k][t] - lq[k] * at
         groups[j] = rows
-        if look:
-            groups[j + 1] = more
-        if j + 2 < n // 8:
-            m = n - r0 - 16
-            rest = jnp.concatenate(groups[j + 2 :], axis=0)
-            lanes = lax.broadcasted_iota(jnp.int32, (m, n), 1)
+        for k in near:
+            groups[k] = more[k]
+        if far < n // 8:
+            rest = jnp.concatenate(groups[far:], axis=0)
+            lanes = lax.broadcasted_iota(jnp.int32, rest.shape, 1)
             rest = jnp.where((lanes >= r0) & (lanes < r0 + 8), 0.0, rest)
-            rest = rest - mm(rows, rows, HI)[r0 + 16 :, :]
-            for i in range(j + 2, n // 8):
-                groups[i] = rest[8 * (i - j - 2) : 8 * (i - j - 1), :]
+            hi, mid, lo = parts(rows)
+            left = jnp.concatenate([hi, hi, mid, hi, mid, lo], axis=0)
+            right = jnp.concatenate([hi, mid, hi, lo, mid, hi], axis=0)
+            rest = rest - mm(left, right)[8 * far :, :]
+            for k in range(far, n // 8):
+                groups[k] = rest[8 * (k - far) : 8 * (k - far) + 8, :]
     return lower_part(jnp.concatenate(groups, axis=0))
 
 
@@ -365,17 +387,18 @@
     gathered = [hold] + [
         move(hold, lambda z, y, c, w, x: (z, y, c, w, (x + k) % 4)) for k in (1, 2, 3)
     ]
-    over = move(rows16, lambda z, y, c, w, x: (z, y, c, 1, 0) if (w, x) == (0, 0) else None)
-    over, *gathered = together(over, *gathered)
-    own, other = diag_gather(spread(jnp.where(w == 0, rows16, over), "x", 4)[0])
+    rows16, *gathered = together(rows16, *gathered)
+    (right,) = call(
+        select_kernel, [jax.ShapeDtypeStruct((tok, 3 * P_SIZE), BF16)], (pos, table, *gathered), "select",
+        scratch=[pltpu.VMEM((tok + 2 * RIM, P_SIZE), BF16), pltpu.SemaphoreType.DMA((4, 3))],
+        flops=2 * 10**9, hbm=(2, 3, 4, 5),
+    )
+    rows16, right = together(spread(rows16, ("w", "x"), 8)[0], right)
+    own, other = diag_gather(rows16)
     (part,) = call(
-        cov_kernel, [jax.ShapeDtypeStruct((8, 128, 2 * P_SIZE), F32)], (pos, table, frames_data, *gathered), "covariance",
-        scratch=[
-            pltpu.VMEM((tok + 2 * RIM, P_SIZE), BF16),
-            pltpu.VMEM((tok, 3 * P_SIZE), BF16),
-            pltpu.SemaphoreType.DMA((4, 3)),
-        ],
-        flops=5 * 10**9, vmem=20, hbm=(3, 4, 5, 6),
+        cov_kernel, [jax.ShapeDtypeStruct((8, 128, 2 * P_SIZE), F32)], (pos, table, frames_data, right), "covariance",
+        scratch=[pltpu.VMEM((2, 8, 32, 2 * P_SIZE), F32), pltpu.SemaphoreType.DMA((2,))],
+        flops=4 * 10**9, vmem=56, out=pltpu.HBM,
     )
     t = lax.psum_scatter(part.reshape(1024, 2 * P_SIZE), ("y", "c"), scatter_dimension=0, tiled=True)
     rows = [t[:32]] + [

time: 163 us -> 166 us (1.018)
  the two profiles are of different devices: /device:TPU:161 before, /device:TPU:2 now
where the time goes in v2:
time: 166 us; the launch traced here: 165 us
  blocking collectives  41.6 us (25%)
  Pallas kernels  35.2 us (21%)
  waiting for transfers between devices  32.7 us (20%)
  starting transfers between devices  30.5 us (18%)
  between operations  14.3 us (9%)
  local copies, waits for them, and re-layouts  7.96 us (5%)
  other arithmetic  2.96 us (2%)
    all_to_all x2, blocking collectives, exchange(): return lax.all_to_all(v, axes, 0, 0, tiled=True)  41.6 us
    pallas_call x8, Pallas kernels, call(): pl.pallas_call(kernel, grid=(1,), out_shape=outs, in_specs=specs, out_spe...  35.2 us
    ppermute x14, waiting for transfers between devices, move(): return lax.ppermute(value, AXES, pairs)  25.8 us
    all_to_all x2, starting transfers between devices, exchange(): return lax.all_to_all(v, axes, 0, 0, tiled=True)  16.8 us
    ppermute x14, starting transfers between devices, move(): return lax.ppermute(value, AXES, pairs)  13.7 us
    all_to_all x2, waiting for transfers between devices, exchange(): return lax.all_to_all(v, axes, 0, 0, tiled=True)  5.29 us
  transfers between devices with their start and end apart: 17, of which 7 were waited for; matrix products, arithmetic and copies ran while one was open for 3% of the time, Pallas kernels for 12%

profile of v2, /device:TPU:2, one launch (start us, length us, event | category | flops | bytes accessed | tf_op | source)
XLA Modules:
  0.0 165.2 jit_solution(8401405887828397913)
XLA Ops:
  7.2 0.7 fusion.1
  7.9 0.7 collective-permute-start.1
  8.6 0.7 collective-permute-start
  9.2 1.2 fusion
  10.4 0.7 slice.43
  11.1 0.1 add_bitcast_fusion
  11.2 0.7 pad_add_fusion.table
  11.9 0.0 copy-start.1
  11.9 0.1 stack.39.pos
  12.0 0.0 collective-permute-done.1.after
  12.0 0.0 collective-permute-done.before
  12.0 0.0 copy-start
  12.0 1.6 copy-done
  13.6 4.2 %diagonal.1 = (f32[256,640]{1,0:T(8,128)S(1)}, f32[256,640]{1,0:T(8,128)S(1)}) custom-call(s32[6]{0:T(128)S(1)} %stack.39.pos, s32[3,64]{1,0:T(4,128)S(1)} %pad_add_fusion.table, bf16[1024,1024]{1,0:T(8,128)(2,1)S(1)} %copy-done, bf16[16,512]{1,0:T(8,128)(2,1)S(1)} %collective-permute-done.before, bf16[16,512]{1,0:T(8,128)(2,1)S(1)} %collective-permute-done.1.after), custom_call_target="tpu_custom_call" | custom-call | flops 3000000000 | bytes 1048576 | tf_op jit(solution)/shard_map/diagonal/pallas_call | solution.py:57
  17.8 0.7 collective-permute-start.2
  18.5 0.7 collective-permute-start.3
  19.2 1.3 collective-permute-start.4
  20.5 1.4 collective-permute-start.5
  21.9 0.0 collective-permute-done.2
  21.9 0.9 add.19
  22.9 4.5 %all-to-all-start = ((f32[4,64,640]{2,1,0:T(8,128)}), f32[4,64,640]{2,1,0:T(8,128)S(1)}, u32[]{:S(2)}, u32[]{:S(2)}) async-start(f32[4,64,640]{2,1,0:T(8,128)} %bitcast.9), calls=%async_computation | async-start | bytes 1310720 | tf_op jit(solution)/shard_map/all_to_all | solution.py:326
  27.3 0.0 collective-permute-done.3
  27.3 12.3 %collective-permute-done.4 = bf16[272,512]{1,0:T(8,128)(2,1)} collective-permute-done((bf16[272,512]{1,0:T(8,128)(2,1)S(1)}, bf16[272,512]{1,0:T(8,128)(2,1)}, u32[]{:S(2)}, u32[]{:S(2)}) %collective-permute-start.4) | collective-permute-done | bytes 278560 | tf_op jit(solution)/shard_map/ppermute | solution.py:47
  39.7 0.0 collective-permute-done.5
  39.7 1.2 maximum_select_fusion
  40.8 1.3 collective-permute-start.6
  42.2 0.0 all-to-all-done
  42.2 6.2 %collective-permute-done.6 = bf16[272,512]{1,0:T(8,128)(2,1)S(1)} collective-permute-done((bf16[272,512]{1,0:T(8,128)(2,1)S(1)}, bf16[272,512]{1,0:T(8,128)(2,1)S(1)}, u32[]{:S(2)}, u32[]{:S(2)}) %collective-permute-start.6) | collective-permute-done | bytes 278560 | tf_op jit(solution)/shard_map/ppermute | solution.py:47
  48.4 0.1 collective-permute-start.9
  48.5 0.1 collective-permute-start.8
  48.6 1.9 %collective-permute-start.7 = (bf16[272,512]{1,0:T(8,128)(2,1)S(1)}, bf16[272,512]{1,0:T(8,128)(2,1)S(1)}, u32[]{:S(2)}, u32[]{:S(2)}) collective-permute-start(bf16[272,512]{1,0:T(8,128)(2,1)S(1)} %broadcast_select_fusion.g0), channel_id=1, source_target_pairs={{0,1},{1,2},{2,3},{3,0},{4,5},{5,6},{6,7},{7,4},{8,9},{9,10},{10,1... | collective-permute-start | bytes 835592 | tf_op jit(solution)/shard_map/ppermute | solution.py:47
  50.6 17.9 %all_to_all.20 = f32[4,16,640]{2,1,0:T(8,128)S(1)} all-to-all(f32[4,16,640]{2,1,0:T(8,128)S(1)} %bitcast.19), channel_id=1, replica_groups=mesh['z'=4,'y'=4,'c'=2,'w'=2,'x'=4] {'z'}, dimensions={0} | all-to-all | bytes 327680 | tf_op jit(solution)/shard_map/all_to_all | solution.py:326
  68.5 0.0 collective-permute-done.9.g3
  68.5 0.0 collective-permute-done.8.g2
  68.5 0.0 collective-permute-done.7.g1
  68.5 0.7 broadcast_in_dim.4
  69.2 12.4 %all-to-all-start.2 = ((f32[8,16,640]{2,1,0:T(8,128)}), f32[8,16,640]{2,1,0:T(8,128)S(1)}, u32[]{:S(2)}, u32[]{:S(2)}) async-start(f32[8,16,640]{2,1,0:T(8,128)} %broadcast_in_dim.4), calls=%async_computation.2 | async-start | bytes 655360 | tf_op jit(solution)/shard_map/all_to_all | solution.py:326
  81.6 0.0 reduce-scatter.2.cloned.1.call-start
  81.6 0.0 copy-done.1
  81.6 0.0 copy-done.2
  81.6 2.6 %select.1.right = bf16[1024,1536]{1,0:T(8,128)(2,1)S(1)} custom-call(s32[6]{0:T(128)S(1)} %stack.39.pos, s32[3,64]{1,0:T(4,128)S(1)} %pad_add_fusion.table, bf16[272,512]{1,0:T(8,128)(2,1)S(1)} %broadcast_select_fusion.g0, bf16[272,512]{1,0:T(8,128)(2,1)S(1)} %collective-permute-done.7.g1, bf16[272,512]{1,0:T(8,128)(2,1)S(1)} %collective-permute-done.8.g2, ...), custom_call_target="tpu_custom_call" | custom-call | flops 2000000000 | bytes 1048576 | tf_op jit(solution)/shard_map/select/pallas_call | solution.py:57
  84.2 0.0 copy-start.4
  84.2 1.7 %copy-done.4 = bf16[1024,1536]{1,0:T(8,128)(2,1)} copy-done((bf16[1024,1536]{1,0:T(8,128)(2,1)}, bf16[1024,1536]{1,0:T(8,128)(2,1)S(1)}, u32[]{:S(2)}) %copy-start.4) | copy-done | bytes 3145752
  85.9 5.3 %all-to-all-done.2 = f32[8,16,640]{2,1,0:T(8,128)S(1)} async-done(((f32[8,16,640]{2,1,0:T(8,128)}), f32[8,16,640]{2,1,0:T(8,128)S(1)}, u32[]{:S(2)}, u32[]{:S(2)}) %all-to-all-start.2) | async-done | bytes 327712 | tf_op jit(solution)/shard_map/all_to_all | solution.py:326
  91.2 7.4 %covariance.1 = f32[8,128,1024]{2,1,0:T(8,128)} custom-call(s32[6]{0:T(128)} %copy-done.2, s32[3,64]{1,0:T(4,128)} %copy-done.1, bf16[1024,1024]{1,0:T(8,128)(2,1)} %x.1, bf16[1024,1536]{1,0:T(8,128)(2,1)} %copy-done.4), custom_call_target="tpu_custom_call" | custom-call | flops 4000000000 | bytes 1048576 | tf_op jit(solution)/shard_map/covariance/pallas_call | solution.py:57
  98.6 0.0 copy-start.3
  98.6 0.0 reduce-scatter.2.cloned.1.call-update
  98.7 23.7 %all_to_all.21 = f32[16,16,640]{2,1,0:T(8,128)S(1)} all-to-all(f32[16,16,640]{2,1,0:T(8,128)S(1)} %broadcast_in_dim.5), channel_id=1, replica_groups=mesh['z'=4,'y'=4,'c'=2,'w'=2,'x'=4] {'y','z'}, dimensions={0} | all-to-all | bytes 1310720 | tf_op jit(solution)/shard_map/all_to_all | solution.py:326
  122.4 0.0 collective-permute-start.10
  122.4 2.1 %collective-permute-done.10.other = f32[256,640]{1,0:T(8,128)S(1)} collective-permute-done((f32[256,640]{1,0:T(8,128)S(1)}, f32[256,640]{1,0:T(8,128)S(1)}, u32[]{:S(2)}, u32[]{:S(2)}) %collective-permute-start.10) | collective-permute-done | bytes 655392 | tf_op jit(solution)/shard_map/ppermute | solution.py:47
  124.5 0.0 copy-done.3
  124.5 5.0 %factor0.1 = (f32[512,512]{1,0:T(8,128)S(1)}, f32[512,512]{1,0:T(8,128)S(1)}) custom-call(s32[6]{0:T(128)S(1)} %copy-done.3, f32[256,640]{1,0:T(8,128)S(1)} %bitcast.17, f32[256,640]{1,0:T(8,128)S(1)} %collective-permute-done.10.other), custom_call_target="tpu_custom_call" | custom-call | flops 5000000000 | bytes 1048576 | tf_op jit(solution)/shard_map/factor0/pallas_call | solution.py:57
  129.4 4.5 %factor128.1.v = f32[512,512]{1,0:T(8,128)S(1)} custom-call(s32[6]{0:T(128)S(1)} %copy-done.3, f32[512,512]{1,0:T(8,128)S(1)} %get-tuple-element.34.v), custom_call_target="tpu_custom_call" | custom-call | flops 5000000000 | bytes 1048576 | tf_op jit(solution)/shard_map/factor128/pallas_call | solution.py:57
  134.0 4.3 %factor256.1.v = f32[512,512]{1,0:T(8,128)S(1)} custom-call(s32[6]{0:T(128)S(1)} %copy-done.3, f32[512,512]{1,0:T(8,128)S(1)} %factor128.1.v), custom_call_target="tpu_custom_call" | custom-call | flops 5000000000 | bytes 1048576 | tf_op jit(solution)/shard_map/factor256/pallas_call | solution.py:57
  138.3 1.6 reduce-scatter.2.cloned.1.call-done
  139.9 1.1 fusion.2
  141.1 3.5 %collective-permute-start.13 = (f32[32,1024]{1,0:T(8,128)S(1)}, f32[32,1024]{1,0:T(8,128)S(1)}, u32[]{:S(2)}, u32[]{:S(2)}) collective-permute-start(f32[32,1024]{1,0:T(8,128)S(1)} %get-tuple-element.42), channel_id=1, source_target_pairs={{0,192},{1,193},{2,194},{3,195},{4,196},{5,197},{6,198},{7,199},{8... | collective-permute-start | bytes 393224 | tf_op jit(solution)/shard_map/ppermute | solution.py:47
  144.6 0.0 collective-permute-start.12
  144.6 1.4 collective-permute-start.11
  146.0 3.9 %factor384.1.inv = f32[512,512]{1,0:T(8,128)S(1)} custom-call(s32[6]{0:T(128)S(1)} %copy-done.3, f32[512,512]{1,0:T(8,128)S(1)} %factor256.1.v), custom_call_target="tpu_custom_call" | custom-call | flops 5000000000 | bytes 1048576 | tf_op jit(solution)/shard_map/factor384/pallas_call | solution.py:57
  149.8 0.0 collective-permute-done.13.p3
  149.8 1.9 %collective-permute-done.12.p2 = f32[32,1024]{1,0:T(8,128)S(1)} collective-permute-done((f32[32,1024]{1,0:T(8,128)S(1)}, f32[32,1024]{1,0:T(8,128)S(1)}, u32[]{:S(2)}, u32[]{:S(2)}) %collective-permute-start.12) | collective-permute-done | bytes 131104 | tf_op jit(solution)/shard_map/ppermute | solution.py:47
  151.7 3.3 %collective-permute-done.11.p1 = f32[32,1024]{1,0:T(8,128)S(1)} collective-permute-done((f32[32,1024]{1,0:T(8,128)S(1)}, f32[32,1024]{1,0:T(8,128)S(1)}, u32[]{:S(2)}, u32[]{:S(2)}) %collective-permute-start.11) | collective-permute-done | bytes 131104 | tf_op jit(solution)/shard_map/ppermute | solution.py:47
  155.0 3.4 %whiten.1 = (f32[1,32,512]{2,1,0:T(8,128)}, f32[1,32,512]{2,1,0:T(8,128)}, f32[16,512]{1,0:T(8,128)}) custom-call(s32[6]{0:T(128)S(1)} %copy-done.3, f32[512,512]{1,0:T(8,128)S(1)} %factor384.1.inv, f32[512,512]{1,0:T(8,128)S(1)} %get-tuple-element.35.up, f32[32,1024]{1,0:T(8,128)S(1)} %get-tuple-element.45.p0, f32[32,1024]{1,0:T(8,128)S(1)} %collective-permute-done.11.p1, ...), custom_call_target="tpu_custom_call" | custom-call | flops 2000000000 | bytes 1048576 | tf_op jit(solution)/shard_map/whiten/pallas_call | solution.py:57
  (7 shorter events, 0.1 us)
Async XLA Ops:
  7.9 4.1 %collective-permute-start.1 = (bf16[16,512]{1,0:T(8,128)(2,1)S(1)}, bf16[16,512]{1,0:T(8,128)(2,1)S(1)}, u32[]{:S(2)}, u32[]{:S(2)}) collective-permute-start(bf16[16,512]{1,0:T(8,128)(2,1)S(1)} %get-tuple-element.40), channel_id=1, source_target_pairs={{8,0},{16,8},{24,16},{32,24},{40,32},{48,40},{56,48},{64,56},{72,6... | collective-permute-start | bytes 49160 | tf_op jit(solution)/shard_map/ppermute | solution.py:47
  8.6 3.5 %collective-permute-start = (bf16[16,512]{1,0:T(8,128)(2,1)S(1)}, bf16[16,512]{1,0:T(8,128)(2,1)S(1)}, u32[]{:S(2)}, u32[]{:S(2)}) collective-permute-start(bf16[16,512]{1,0:T(8,128)(2,1)S(1)} %get-tuple-element.41), channel_id=1, source_target_pairs={{0,8},{8,16},{16,24},{24,32},{32,40},{40,48},{48,56},{56,64},{64,7... | collective-permute-start | bytes 49160 | tf_op jit(solution)/shard_map/ppermute | solution.py:47
  11.9 69.7 %copy-start.1 = (s32[3,64]{1,0:T(4,128)}, s32[3,64]{1,0:T(4,128)S(1)}, u32[]{:S(2)}) copy-start(s32[3,64]{1,0:T(4,128)S(1)} %pad_add_fusion.table) | copy-start | bytes 2308
  12.0 69.6 %copy-start.2 = (s32[6]{0:T(128)}, s32[6]{0:T(128)S(1)}, u32[]{:S(2)}) copy-start(s32[6]{0:T(128)S(1)} %stack.39.pos) | copy-start | bytes 76
  12.0 1.6 copy-start
  17.8 4.1 %collective-permute-start.2 = (f32[256,640]{1,0:T(8,128)S(1)}, f32[256,640]{1,0:T(8,128)S(1)}, u32[]{:S(2)}, u32[]{:S(2)}) collective-permute-start(f32[256,640]{1,0:T(8,128)S(1)} %get-tuple-element.22), channel_id=1, source_target_pairs={{0,8},{8,0},{16,24},{24,16},{32,40},{40,32},{48,56},{56,48},{64,72... | collective-permute-start | bytes 1966088 | tf_op jit(solution)/shard_map/ppermute | solution.py:47
  18.5 8.8 %collective-permute-start.3 = (bf16[272,512]{1,0:T(8,128)(2,1)S(1)}, bf16[272,512]{1,0:T(8,128)(2,1)S(1)}, u32[]{:S(2)}, u32[]{:S(2)}) collective-permute-start(bf16[272,512]{1,0:T(8,128)(2,1)S(1)} %get-tuple-element.23), channel_id=1, source_target_pairs={{0,2},{8,10},{16,18},{24,26},{32,34},{40,42},{48,50},{56,58},{64,6... | collective-permute-start | bytes 835592 | tf_op jit(solution)/shard_map/ppermute | solution.py:47
  19.2 20.5 %collective-permute-start.4 = (bf16[272,512]{1,0:T(8,128)(2,1)S(1)}, bf16[272,512]{1,0:T(8,128)(2,1)}, u32[]{:S(2)}, u32[]{:S(2)}) collective-permute-start(bf16[272,512]{1,0:T(8,128)(2,1)S(1)} %get-tuple-element.24), channel_id=1, source_target_pairs={{0,1},{8,9},{16,17},{24,25},{32,33},{40,41},{48,49},{56,57},{64,65... | collective-permute-start | bytes 835592 | tf_op jit(solution)/shard_map/ppermute | solution.py:47
  20.5 19.2 %collective-permute-start.5 = (bf16[272,512]{1,0:T(8,128)(2,1)S(1)}, bf16[272,512]{1,0:T(8,128)(2,1)}, u32[]{:S(2)}, u32[]{:S(2)}) collective-permute-start(bf16[272,512]{1,0:T(8,128)(2,1)S(1)} %get-tuple-element.25), channel_id=1, source_target_pairs={{0,3},{8,11},{16,19},{24,27},{32,35},{40,43},{48,51},{56,59},{64,6... | collective-permute-start | bytes 835592 | tf_op jit(solution)/shard_map/ppermute | solution.py:47
  22.9 19.3 %all-to-all-start = ((f32[4,64,640]{2,1,0:T(8,128)}), f32[4,64,640]{2,1,0:T(8,128)S(1)}, u32[]{:S(2)}, u32[]{:S(2)}) async-start(f32[4,64,640]{2,1,0:T(8,128)} %bitcast.9), calls=%async_computation | async-start | bytes 1310720 | tf_op jit(solution)/shard_map/all_to_all | solution.py:326
  40.8 7.6 %collective-permute-start.6 = (bf16[272,512]{1,0:T(8,128)(2,1)S(1)}, bf16[272,512]{1,0:T(8,128)(2,1)S(1)}, u32[]{:S(2)}, u32[]{:S(2)}) collective-permute-start(bf16[272,512]{1,0:T(8,128)(2,1)S(1)} %maximum_select_fusion), channel_id=1, source_target_pairs={{0,4},{1,5},{2,6},{3,7},{8,12},{9,13},{10,14},{11,15},{16,20},{17,... | collective-permute-start | bytes 835592 | tf_op jit(solution)/shard_map/ppermute | solution.py:47
  48.4 20.0 %collective-permute-start.9 = (bf16[272,512]{1,0:T(8,128)(2,1)S(1)}, bf16[272,512]{1,0:T(8,128)(2,1)S(1)}, u32[]{:S(2)}, u32[]{:S(2)}) collective-permute-start(bf16[272,512]{1,0:T(8,128)(2,1)S(1)} %broadcast_select_fusion.g0), channel_id=1, source_target_pairs={{0,3},{1,0},{2,1},{3,2},{4,7},{5,4},{6,5},{7,6},{8,11},{9,8},{10,9... | collective-permute-start | bytes 835592 | tf_op jit(solution)/shard_map/ppermute | solution.py:47
  48.5 19.9 %collective-permute-start.8 = (bf16[272,512]{1,0:T(8,128)(2,1)S(1)}, bf16[272,512]{1,0:T(8,128)(2,1)S(1)}, u32[]{:S(2)}, u32[]{:S(2)}) collective-permute-start(bf16[272,512]{1,0:T(8,128)(2,1)S(1)} %broadcast_select_fusion.g0), channel_id=1, source_target_pairs={{0,2},{1,3},{2,0},{3,1},{4,6},{5,7},{6,4},{7,5},{8,10},{9,11},{10,... | collective-permute-start | bytes 835592 | tf_op jit(solution)/shard_map/ppermute | solution.py:47
  48.6 19.9 %collective-permute-start.7 = (bf16[272,512]{1,0:T(8,128)(2,1)S(1)}, bf16[272,512]{1,0:T(8,128)(2,1)S(1)}, u32[]{:S(2)}, u32[]{:S(2)}) collective-permute-start(bf16[272,512]{1,0:T(8,128)(2,1)S(1)} %broadcast_select_fusion.g0), channel_id=1, source_target_pairs={{0,1},{1,2},{2,3},{3,0},{4,5},{5,6},{6,7},{7,4},{8,9},{9,10},{10,1... | collective-permute-start | bytes 835592 | tf_op jit(solution)/shard_map/ppermute | solution.py:47
  69.2 22.0 %all-to-all-start.2 = ((f32[8,16,640]{2,1,0:T(8,128)}), f32[8,16,640]{2,1,0:T(8,128)S(1)}, u32[]{:S(2)}, u32[]{:S(2)}) async-start(f32[8,16,640]{2,1,0:T(8,128)} %broadcast_in_dim.4), calls=%async_computation.2 | async-start | bytes 655360 | tf_op jit(solution)/shard_map/all_to_all | solution.py:326
  81.6 58.3 %reduce-scatter.2.cloned.1.call-start = ((), (), s32[]{:S(2)}) async-start(), calls=%async_computation.5 | async-start | bytes 4718592 | tf_op jit(solution)/shard_map/reduce_scatter | solution.py:403
  84.2 1.7 %copy-start.4 = (bf16[1024,1536]{1,0:T(8,128)(2,1)}, bf16[1024,1536]{1,0:T(8,128)(2,1)S(1)}, u32[]{:S(2)}) copy-start(bf16[1024,1536]{1,0:T(8,128)(2,1)S(1)} %select.1.right) | copy-start | bytes 9437188
  98.6 25.9 %copy-start.3 = (s32[6]{0:T(128)S(1)}, s32[6]{0:T(128)}, u32[]{:S(2)}) copy-start(s32[6]{0:T(128)} %copy-done.2) | copy-start | bytes 76
  122.4 2.1 %collective-permute-start.10 = (f32[256,640]{1,0:T(8,128)S(1)}, f32[256,640]{1,0:T(8,128)S(1)}, u32[]{:S(2)}, u32[]{:S(2)}) collective-permute-start(f32[256,640]{1,0:T(8,128)S(1)} %bitcast.16), channel_id=1, source_target_pairs={{0,8},{1,9},{2,10},{3,11},{4,12},{5,13},{6,14},{7,15},{8,0},{9,1},... | collective-permute-start | bytes 1966088 | tf_op jit(solution)/shard_map/ppermute | solution.py:47
  141.1 8.8 %collective-permute-start.13 = (f32[32,1024]{1,0:T(8,128)S(1)}, f32[32,1024]{1,0:T(8,128)S(1)}, u32[]{:S(2)}, u32[]{:S(2)}) collective-permute-start(f32[32,1024]{1,0:T(8,128)S(1)} %get-tuple-element.42), channel_id=1, source_target_pairs={{0,192},{1,193},{2,194},{3,195},{4,196},{5,197},{6,198},{7,199},{8... | collective-permute-start | bytes 393224 | tf_op jit(solution)/shard_map/ppermute | solution.py:47
  144.6 7.2 %collective-permute-start.12 = (f32[32,1024]{1,0:T(8,128)S(1)}, f32[32,1024]{1,0:T(8,128)S(1)}, u32[]{:S(2)}, u32[]{:S(2)}) collective-permute-start(f32[32,1024]{1,0:T(8,128)S(1)} %get-tuple-element.43), channel_id=1, source_target_pairs={{0,64},{1,65},{2,66},{3,67},{4,68},{5,69},{6,70},{7,71},{8,72},{9,... | collective-permute-start | bytes 393224 | tf_op jit(solution)/shard_map/ppermute | solution.py:47
  144.6 10.4 %collective-permute-start.11 = (f32[32,1024]{1,0:T(8,128)S(1)}, f32[32,1024]{1,0:T(8,128)S(1)}, u32[]{:S(2)}, u32[]{:S(2)}) collective-permute-start(f32[32,1024]{1,0:T(8,128)S(1)} %get-tuple-element.44), channel_id=1, source_target_pairs={{0,128},{1,129},{2,130},{3,131},{4,132},{5,133},{6,134},{7,135},{8... | collective-permute-start | bytes 393224 | tf_op jit(solution)/shard_map/ppermute | solution.py:47
Sparse Core Ops, SparseCore 0:
  98.7 41.1 reduce-scatter.1

commit v3 on v2

--- a/solution.py
+++ b/solution.py
@@ -47,7 +47,7 @@
     return lax.ppermute(value, AXES, pairs)
 
 
-def call(kernel, outs, args, name, scratch=(), flops=0, vmem=16, hbm=(), block=None, out=pltpu.VMEM):
+def call(kernel, outs, args, name, scratch=(), flops=0, vmem=16, hbm=(), block=None):
     specs = [pl.BlockSpec(memory_space=pltpu.VMEM)] * len(args)
     specs[0] = pl.BlockSpec(memory_space=pltpu.SMEM)
     for i in hbm:
@@ -59,7 +59,7 @@
         grid=(1,),
         out_shape=outs,
         in_specs=specs,
-        out_specs=[pl.BlockSpec(memory_space=out)] * len(outs),
+        out_specs=[pl.BlockSpec(memory_space=pltpu.VMEM)] * len(outs),
         scratch_shapes=list(scratch),
         compiler_params=pltpu.CompilerParams(vmem_limit_bytes=vmem * 2**20),
         cost_estimate=pl.CostEstimate(flops=flops, bytes_accessed=2**20, transcendentals=0),
@@ -157,9 +157,9 @@
         right[b : b + 256, 2 * n :] = zm
 
 
-def select_kernel(pos, table, g0, g1, g2, g3, right, ext, sem):
-    rows, n = right.shape[0], P_SIZE
-    col = pos[5]
+def cov_kernel(pos, table, x, g0, g1, g2, g3, out, ext, right, sem):
+    rows, n = x.shape[0], P_SIZE
+    z, col = pos[3], pos[5]
     for wait in (False, True):
         for k, g in enumerate((g0, g1, g2, g3)):
             q = lax.rem(col - k + 4, 4)
@@ -180,28 +180,16 @@
                 bring(g, ext.at[pl.ds(at, CHUNK), :], 0)
 
     fill_right(pos, table, ext, right, rows, n)
-
-
-def cov_kernel(pos, table, x, right, out, done, sent):
-    n = P_SIZE
-    z = pos[3]
     scale = 1.0 / pair_count(table)
-    leave = []
     for zz in range(4):
         left = x[:, 256 * zz : 256 * zz + 256]
         d0 = mm(left, right[:, :n]) * scale
         d1 = mm(left, right[:, n : 2 * n]) + mm(left, right[:, 2 * n :])
         d1 = d1 * (0.5 * scale)
         at = pl.multiple_of(lax.rem(zz - z + 4, 4) * 32, 32)
-        if zz >= 2:
-            leave[zz - 2].wait()
         for k in range(8):
-            done[zz % 2, k, :, :n] = d0[32 * k : 32 * k + 32, :]
-            done[zz % 2, k, :, n:] = d1[32 * k : 32 * k + 32, :]
-        leave.append(pltpu.make_async_copy(done.at[zz % 2], out.at[:, pl.ds(at, 32), :], sent.at[zz % 2]))
-        leave[zz].start()
-    leave[2].wait()
-    leave[3].wait()
+            out[k, pl.ds(at, 32), :n] = d0[32 * k : 32 * k + 32, :]
+            out[k, pl.ds(at, 32), n:] = d1[32 * k : 32 * k + 32, :]
 
 
 def parts(v):
@@ -381,24 +369,27 @@
     first = jnp.concatenate([before, behind, panel[:FIRST]], axis=0)
     hold = jnp.where(x == 0, first, sent[0] + sent[1] + sent[2])
     over = move(hold, lambda z, y, c, w, x: (z, y, c, 1, x) if w == 0 else None)
-    quarter, over = together(diag_half(mine, theirs), over)
-    rows16 = diag_rows(quarter)
+    rows16 = diag_rows(diag_half(mine, theirs))
     hold = jnp.where(w == 0, hold, over)
     gathered = [hold] + [
         move(hold, lambda z, y, c, w, x: (z, y, c, w, (x + k) % 4)) for k in (1, 2, 3)
     ]
-    rows16, *gathered = together(rows16, *gathered)
-    (right,) = call(
-        select_kernel, [jax.ShapeDtypeStruct((tok, 3 * P_SIZE), BF16)], (pos, table, *gathered), "select",
-        scratch=[pltpu.VMEM((tok + 2 * RIM, P_SIZE), BF16), pltpu.SemaphoreType.DMA((4, 3))],
-        flops=2 * 10**9, hbm=(2, 3, 4, 5),
-    )
-    rows16, right = together(spread(rows16, ("w", "x"), 8)[0], right)
+    over = move(rows16, lambda z, y, c, w, x: (z, y, c, 1, 0) if (w, x) == (0, 0) else None)
+    over, *gathered = together(over, *gathered)
+    rows16 = jnp.where(w == 0, rows16, over)
+    copies = [
+        move(rows16, lambda z, y, c, w, x: (z, y, c, w, k) if x == 0 else None) for k in (2, 1, 3)
+    ]
+    rows16 = jnp.where(x == 0, rows16, copies[0] + copies[1] + copies[2])
     own, other = diag_gather(rows16)
     (part,) = call(
-        cov_kernel, [jax.ShapeDtypeStruct((8, 128, 2 * P_SIZE), F32)], (pos, table, frames_data, right), "covariance",
-        scratch=[pltpu.VMEM((2, 8, 32, 2 * P_SIZE), F32), pltpu.SemaphoreType.DMA((2,))],
-        flops=4 * 10**9, vmem=56, out=pltpu.HBM,
+        cov_kernel, [jax.ShapeDtypeStruct((8, 128, 2 * P_SIZE), F32)], (pos, table, frames_data, *gathered), "covariance",
+        scratch=[
+            pltpu.VMEM((tok + 2 * RIM, P_SIZE), BF16),
+            pltpu.VMEM((tok, 3 * P_SIZE), BF16),
+            pltpu.SemaphoreType.DMA((4, 3)),
+        ],
+        flops=5 * 10**9, vmem=20, hbm=(3, 4, 5, 6),
     )
     t = lax.psum_scatter(part.reshape(1024, 2 * P_SIZE), ("y", "c"), scatter_dimension=0, tiled=True)
     rows = [t[:32]] + [

time: 166 us -> 156 us (0.940)
  the two profiles are of different devices: /device:TPU:2 before, /device:TPU:167 now
where the time goes in v3:
time: 156 us
  waiting for transfers between devices  45.8 us (29%)
  Pallas kernels  31.2 us (20%)
  starting transfers between devices  28.8 us (18%)
  blocking collectives  22.5 us (14%)
  between operations  14.3 us (9%)
  local copies, waits for them, and re-layouts  8.28 us (5%)
  other arithmetic  4.83 us (3%)
    ppermute x18, waiting for transfers between devices, move(): return lax.ppermute(value, AXES, pairs)  38.6 us
    pallas_call x7, Pallas kernels, call(): pl.pallas_call(kernel, grid=(1,), out_shape=outs, in_specs=specs, out_spe...  31.2 us
    all_to_all x1, blocking collectives, exchange(): return lax.all_to_all(v, axes, 0, 0, tiled=True)  22.5 us
    ppermute x18, starting transfers between devices, move(): return lax.ppermute(value, AXES, pairs)  20.6 us
    all_to_all x2, starting transfers between devices, exchange(): return lax.all_to_all(v, axes, 0, 0, tiled=True)  8.22 us
    all_to_all x2, waiting for transfers between devices, exchange(): return lax.all_to_all(v, axes, 0, 0, tiled=True)  7.22 us
    unnamed x6, local copies, waits for them, and re-layouts  3.53 us
  transfers between devices with their start and end apart: 21, of which 10 were waited for; matrix products, arithmetic and copies ran while one was open for 5% of the time, Pallas kernels for 11%

profile of v3, /device:TPU:167, one launch (start us, length us, event | category | flops | bytes accessed | tf_op | source)
XLA Modules:
  0.0 155.7 jit_solution(4949712377173311287)
XLA Ops:
  7.2 0.7 fusion.1
  7.9 0.7 collective-permute-start
  8.6 0.7 collective-permute-start.1
  9.2 2.0 %fusion = (bf16[272,512]{1,0:T(8,128)(2,1)S(1)}, bf16[272,512]{1,0:T(8,128)(2,1)}, bf16[272,512]{1,0:T(8,128)(2,1)}) fusion(bf16[1024,1024]{1,0:T(8,128)(2,1)} %x.1), kind=kLoop, calls=%fused_computation.6 | loop fusion | bytes 1671168 | tf_op jit(solution)/shard_map/slice | solution.py:364
  11.2 0.7 slice.40
  12.0 0.1 add_bitcast_fusion
  12.0 0.7 pad_add_fusion.table
  12.7 0.1 stack.39.pos
  12.8 0.0 collective-permute-done.before
  12.8 0.0 collective-permute-done.1.after
  12.8 0.0 copy-start.1
  12.8 1.6 %copy-done.1 = bf16[1024,1024]{1,0:T(8,128)(2,1)S(1)} copy-done((bf16[1024,1024]{1,0:T(8,128)(2,1)S(1)}, bf16[1024,1024]{1,0:T(8,128)(2,1)}, u32[]{:S(2)}) %copy-start.1) | copy-done | bytes 2097176
  14.4 4.2 %diagonal.1 = (f32[256,640]{1,0:T(8,128)S(1)}, f32[256,640]{1,0:T(8,128)S(1)}) custom-call(s32[6]{0:T(128)S(1)} %stack.39.pos, s32[3,64]{1,0:T(4,128)S(1)} %pad_add_fusion.table, bf16[1024,1024]{1,0:T(8,128)(2,1)S(1)} %copy-done.1, bf16[16,512]{1,0:T(8,128)(2,1)S(1)} %collective-permute-done.before, bf16[16,512]{1,0:T(8,128)(2,1)S(1)} %collective-permute-done.1.after), custom_call_target="tpu_custom_call" | custom-call | flops 3000000000 | bytes 1048576 | tf_op jit(solution)/shard_map/diagonal/pallas_call | solution.py:57
  18.6 0.7 collective-permute-start.2
  19.3 1.4 collective-permute-start.4
  20.7 1.4 collective-permute-start.5
  22.0 1.4 collective-permute-start.6
  23.4 0.0 collective-permute-done.2
  23.4 0.9 add.25
  24.4 4.2 %all-to-all-start = ((f32[4,64,640]{2,1,0:T(8,128)}), f32[4,64,640]{2,1,0:T(8,128)S(1)}, u32[]{:S(2)}, u32[]{:S(2)}) async-start(f32[4,64,640]{2,1,0:T(8,128)} %bitcast.9), calls=%async_computation | async-start | bytes 1310720 | tf_op jit(solution)/shard_map/all_to_all | solution.py:314
  28.6 0.0 collective-permute-done.4
  28.6 0.0 collective-permute-done.5
  28.6 0.0 collective-permute-done.6
  28.6 1.4 maximum_select_fusion
  30.0 1.3 collective-permute-start.7
  31.3 7.2 %all-to-all-done = f32[4,64,640]{2,1,0:T(8,128)S(1)} async-done(((f32[4,64,640]{2,1,0:T(8,128)}), f32[4,64,640]{2,1,0:T(8,128)S(1)}, u32[]{:S(2)}, u32[]{:S(2)}) %all-to-all-start) | async-done | bytes 655392 | tf_op jit(solution)/shard_map/all_to_all | solution.py:314
  38.5 0.7 reduce_sum.18
  39.2 4.0 %all-to-all-start.1 = ((f32[4,16,640]{2,1,0:T(8,128)}), f32[4,16,640]{2,1,0:T(8,128)S(1)}, u32[]{:S(2)}, u32[]{:S(2)}) async-start(f32[4,16,640]{2,1,0:T(8,128)} %bitcast.10), calls=%async_computation.1 | async-start | bytes 327680 | tf_op jit(solution)/shard_map/all_to_all | solution.py:314
  43.3 13.1 %collective-permute-done.7 = bf16[272,512]{1,0:T(8,128)(2,1)} collective-permute-done((bf16[272,512]{1,0:T(8,128)(2,1)S(1)}, bf16[272,512]{1,0:T(8,128)(2,1)}, u32[]{:S(2)}, u32[]{:S(2)}) %collective-permute-start.7) | collective-permute-done | bytes 278560 | tf_op jit(solution)/shard_map/ppermute | solution.py:47
  56.3 1.0 broadcast_select_fusion.g0
  57.3 0.1 collective-permute-start.10
  57.4 2.7 %collective-permute-start.8 = (bf16[272,512]{1,0:T(8,128)(2,1)S(1)}, bf16[272,512]{1,0:T(8,128)(2,1)S(1)}, u32[]{:S(2)}, u32[]{:S(2)}) collective-permute-start(bf16[272,512]{1,0:T(8,128)(2,1)S(1)} %broadcast_select_fusion.g0), channel_id=1, source_target_pairs={{0,1},{1,2},{2,3},{3,0},{4,5},{5,6},{6,7},{7,4},{8,9},{9,10},{10,1... | collective-permute-start | bytes 835592 | tf_op jit(solution)/shard_map/ppermute | solution.py:47
  60.1 2.2 %collective-permute-start.9 = (bf16[272,512]{1,0:T(8,128)(2,1)S(1)}, bf16[272,512]{1,0:T(8,128)(2,1)S(1)}, u32[]{:S(2)}, u32[]{:S(2)}) collective-permute-start(bf16[272,512]{1,0:T(8,128)(2,1)S(1)} %broadcast_select_fusion.g0), channel_id=1, source_target_pairs={{0,2},{1,3},{2,0},{3,1},{4,6},{5,7},{6,4},{7,5},{8,10},{9,11},{10,... | collective-permute-start | bytes 835592 | tf_op jit(solution)/shard_map/ppermute | solution.py:47
  62.3 0.0 all-to-all-done.1
  62.3 0.7 collective-permute-start.3
  62.9 2.3 %collective-permute-done.10.g3 = bf16[272,512]{1,0:T(8,128)(2,1)S(1)} collective-permute-done((bf16[272,512]{1,0:T(8,128)(2,1)S(1)}, bf16[272,512]{1,0:T(8,128)(2,1)S(1)}, u32[]{:S(2)}, u32[]{:S(2)}) %collective-permute-start.10) | collective-permute-done | bytes 278560 | tf_op jit(solution)/shard_map/ppermute | solution.py:47
  65.2 0.4 collective-permute-done.8.g1
  65.6 6.6 %collective-permute-done.9.g2 = bf16[272,512]{1,0:T(8,128)(2,1)S(1)} collective-permute-done((bf16[272,512]{1,0:T(8,128)(2,1)S(1)}, bf16[272,512]{1,0:T(8,128)(2,1)S(1)}, u32[]{:S(2)}, u32[]{:S(2)}) %collective-permute-start.9) | collective-permute-done | bytes 278560 | tf_op jit(solution)/shard_map/ppermute | solution.py:47
  72.2 0.0 collective-permute-done.3
  72.2 5.9 %covariance.1 = f32[8,128,1024]{2,1,0:T(8,128)S(1)} custom-call(s32[6]{0:T(128)S(1)} %stack.39.pos, s32[3,64]{1,0:T(4,128)S(1)} %pad_add_fusion.table, bf16[1024,1024]{1,0:T(8,128)(2,1)S(1)} %copy-done.2, bf16[272,512]{1,0:T(8,128)(2,1)S(1)} %broadcast_select_fusion.g0, bf16[272,512]{1,0:T(8,128)(2,1)S(1)} %collective-permute-done.8.g1, ...), custom_call_target="tpu_custom_call" | custom-call | flops 5000000000 | bytes 1048576 | tf_op jit(solution)/shard_map/covariance/pallas_call | solution.py:57
  78.1 1.9 %copy-done = f32[8,128,1024]{2,1,0:T(8,128)} copy-done((f32[8,128,1024]{2,1,0:T(8,128)}, f32[8,128,1024]{2,1,0:T(8,128)S(1)}, u32[]{:S(2)}) %copy-start) | copy-done | bytes 4194328
  80.1 0.0 reduce-scatter.2.cloned.1.call-update
  80.1 0.7 collective-permute-start.11
  80.8 0.7 collective-permute-start.12
  81.4 1.3 collective-permute-start.13
  82.7 0.0 collective-permute-done.11
  82.7 0.0 collective-permute-done.12
  82.8 6.3 %collective-permute-done.13 = f32[16,640]{1,0:T(8,128)S(1)} collective-permute-done((f32[16,640]{1,0:T(8,128)S(1)}, f32[16,640]{1,0:T(8,128)S(1)}, u32[]{:S(2)}, u32[]{:S(2)}) %collective-permute-start.13) | collective-permute-done | bytes 40992 | tf_op jit(solution)/shard_map/ppermute | solution.py:47
  89.1 22.5 %all_to_all.15 = f32[16,16,640]{2,1,0:T(8,128)S(1)} all-to-all(f32[16,16,640]{2,1,0:T(8,128)S(1)} %broadcast_in_dim.2), channel_id=1, replica_groups=mesh['z'=4,'y'=4,'c'=2,'w'=2,'x'=4] {'y','z'}, dimensions={0} | all-to-all | bytes 1310720 | tf_op jit(solution)/shard_map/all_to_all | solution.py:314
  111.7 2.5 %collective-permute-start.14 = (f32[256,640]{1,0:T(8,128)S(1)}, f32[256,640]{1,0:T(8,128)S(1)}, u32[]{:S(2)}, u32[]{:S(2)}) collective-permute-start(f32[256,640]{1,0:T(8,128)S(1)} %bitcast.15), channel_id=1, source_target_pairs={{0,8},{1,9},{2,10},{3,11},{4,12},{5,13},{6,14},{7,15},{8,0},{9,1},... | collective-permute-start | bytes 1966088 | tf_op jit(solution)/shard_map/ppermute | solution.py:47
  114.1 1.7 %collective-permute-done.14.other = f32[256,640]{1,0:T(8,128)S(1)} collective-permute-done((f32[256,640]{1,0:T(8,128)S(1)}, f32[256,640]{1,0:T(8,128)S(1)}, u32[]{:S(2)}, u32[]{:S(2)}) %collective-permute-start.14) | collective-permute-done | bytes 655392 | tf_op jit(solution)/shard_map/ppermute | solution.py:47
  115.9 5.0 %factor0.1 = (f32[512,512]{1,0:T(8,128)S(1)}, f32[512,512]{1,0:T(8,128)S(1)}) custom-call(s32[6]{0:T(128)S(1)} %stack.39.pos, f32[256,640]{1,0:T(8,128)S(1)} %bitcast.16, f32[256,640]{1,0:T(8,128)S(1)} %collective-permute-done.14.other), custom_call_target="tpu_custom_call" | custom-call | flops 5000000000 | bytes 1048576 | tf_op jit(solution)/shard_map/factor0/pallas_call | solution.py:57
  120.8 4.5 %factor128.1.v = f32[512,512]{1,0:T(8,128)S(1)} custom-call(s32[6]{0:T(128)S(1)} %stack.39.pos, f32[512,512]{1,0:T(8,128)S(1)} %get-tuple-element.23.v), custom_call_target="tpu_custom_call" | custom-call | flops 5000000000 | bytes 1048576 | tf_op jit(solution)/shard_map/factor128/pallas_call | solution.py:57
  125.3 4.3 %factor256.1.v = f32[512,512]{1,0:T(8,128)S(1)} custom-call(s32[6]{0:T(128)S(1)} %stack.39.pos, f32[512,512]{1,0:T(8,128)S(1)} %factor128.1.v), custom_call_target="tpu_custom_call" | custom-call | flops 5000000000 | bytes 1048576 | tf_op jit(solution)/shard_map/factor256/pallas_call | solution.py:57
  129.7 0.0 reduce-scatter.2.cloned.1.call-done
  129.7 1.1 fusion.2
  130.9 1.1 collective-permute-start.15
  131.9 1.3 collective-permute-start.16
  133.2 0.2 collective-permute-start.17
  133.4 3.9 %factor384.1.inv = f32[512,512]{1,0:T(8,128)S(1)} custom-call(s32[6]{0:T(128)S(1)} %stack.39.pos, f32[512,512]{1,0:T(8,128)S(1)} %factor256.1.v), custom_call_target="tpu_custom_call" | custom-call | flops 5000000000 | bytes 1048576 | tf_op jit(solution)/shard_map/factor384/pallas_call | solution.py:57
  137.3 0.3 collective-permute-done.15.p1
  137.6 5.6 %collective-permute-done.16.p2 = f32[32,1024]{1,0:T(8,128)S(1)} collective-permute-done((f32[32,1024]{1,0:T(8,128)S(1)}, f32[32,1024]{1,0:T(8,128)S(1)}, u32[]{:S(2)}, u32[]{:S(2)}) %collective-permute-start.16) | collective-permute-done | bytes 131104 | tf_op jit(solution)/shard_map/ppermute | solution.py:47
  143.2 2.3 %collective-permute-done.17.p3 = f32[32,1024]{1,0:T(8,128)S(1)} collective-permute-done((f32[32,1024]{1,0:T(8,128)S(1)}, f32[32,1024]{1,0:T(8,128)S(1)}, u32[]{:S(2)}, u32[]{:S(2)}) %collective-permute-start.17) | collective-permute-done | bytes 131104 | tf_op jit(solution)/shard_map/ppermute | solution.py:47
  145.5 3.4 %whiten.1 = (f32[1,32,512]{2,1,0:T(8,128)}, f32[1,32,512]{2,1,0:T(8,128)}, f32[16,512]{1,0:T(8,128)}) custom-call(s32[6]{0:T(128)S(1)} %stack.39.pos, f32[512,512]{1,0:T(8,128)S(1)} %factor384.1.inv, f32[512,512]{1,0:T(8,128)S(1)} %get-tuple-element.24.up, f32[32,1024]{1,0:T(8,128)S(1)} %get-tuple-element.37.p0, f32[32,1024]{1,0:T(8,128)S(1)} %collective-permute-done.15.p1, ...), custom_call_target="tpu_custom_call" | custom-call | flops 2000000000 | bytes 1048576 | tf_op jit(solution)/shard_map/whiten/pallas_call | solution.py:57
  (9 shorter events, 0.1 us)
Async XLA Ops:
  7.9 4.9 %collective-permute-start = (bf16[16,512]{1,0:T(8,128)(2,1)S(1)}, bf16[16,512]{1,0:T(8,128)(2,1)S(1)}, u32[]{:S(2)}, u32[]{:S(2)}) collective-permute-start(bf16[16,512]{1,0:T(8,128)(2,1)S(1)} %get-tuple-element.33), channel_id=1, source_target_pairs={{0,8},{8,16},{16,24},{24,32},{32,40},{40,48},{48,56},{56,64},{64,7... | collective-permute-start | bytes 49160 | tf_op jit(solution)/shard_map/ppermute | solution.py:47
  8.6 4.3 %collective-permute-start.1 = (bf16[16,512]{1,0:T(8,128)(2,1)S(1)}, bf16[16,512]{1,0:T(8,128)(2,1)S(1)}, u32[]{:S(2)}, u32[]{:S(2)}) collective-permute-start(bf16[16,512]{1,0:T(8,128)(2,1)S(1)} %get-tuple-element.32), channel_id=1, source_target_pairs={{8,0},{16,8},{24,16},{32,24},{40,32},{48,40},{56,48},{64,56},{72,6... | collective-permute-start | bytes 49160 | tf_op jit(solution)/shard_map/ppermute | solution.py:47
  12.8 1.6 %copy-start.1 = (bf16[1024,1024]{1,0:T(8,128)(2,1)S(1)}, bf16[1024,1024]{1,0:T(8,128)(2,1)}, u32[]{:S(2)}) copy-start(bf16[1024,1024]{1,0:T(8,128)(2,1)} %x.1) | copy-start | bytes 6291460
  18.6 4.8 %collective-permute-start.2 = (f32[256,640]{1,0:T(8,128)S(1)}, f32[256,640]{1,0:T(8,128)S(1)}, u32[]{:S(2)}, u32[]{:S(2)}) collective-permute-start(f32[256,640]{1,0:T(8,128)S(1)} %get-tuple-element.18), channel_id=1, source_target_pairs={{0,8},{8,0},{16,24},{24,16},{32,40},{40,32},{48,56},{56,48},{64,72... | collective-permute-start | bytes 1966088 | tf_op jit(solution)/shard_map/ppermute | solution.py:47
  19.3 9.3 %collective-permute-start.4 = (bf16[272,512]{1,0:T(8,128)(2,1)}, bf16[272,512]{1,0:T(8,128)(2,1)}, u32[]{:S(2)}, u32[]{:S(2)}) collective-permute-start(bf16[272,512]{1,0:T(8,128)(2,1)} %get-tuple-element.19), channel_id=1, source_target_pairs={{0,2},{8,10},{16,18},{24,26},{32,34},{40,42},{48,50},{56,58},{64,6... | collective-permute-start | bytes 835592 | tf_op jit(solution)/shard_map/ppermute | solution.py:47
  20.7 7.9 %collective-permute-start.5 = (bf16[272,512]{1,0:T(8,128)(2,1)}, bf16[272,512]{1,0:T(8,128)(2,1)}, u32[]{:S(2)}, u32[]{:S(2)}) collective-permute-start(bf16[272,512]{1,0:T(8,128)(2,1)} %get-tuple-element.20), channel_id=1, source_target_pairs={{0,1},{8,9},{16,17},{24,25},{32,33},{40,41},{48,49},{56,57},{64,65... | collective-permute-start | bytes 835592 | tf_op jit(solution)/shard_map/ppermute | solution.py:47
  22.0 6.5 %collective-permute-start.6 = (bf16[272,512]{1,0:T(8,128)(2,1)S(1)}, bf16[272,512]{1,0:T(8,128)(2,1)}, u32[]{:S(2)}, u32[]{:S(2)}) collective-permute-start(bf16[272,512]{1,0:T(8,128)(2,1)S(1)} %get-tuple-element.21), channel_id=1, source_target_pairs={{0,3},{8,11},{16,19},{24,27},{32,35},{40,43},{48,51},{56,59},{64,6... | collective-permute-start | bytes 835592 | tf_op jit(solution)/shard_map/ppermute | solution.py:47
  24.4 14.1 %all-to-all-start = ((f32[4,64,640]{2,1,0:T(8,128)}), f32[4,64,640]{2,1,0:T(8,128)S(1)}, u32[]{:S(2)}, u32[]{:S(2)}) async-start(f32[4,64,640]{2,1,0:T(8,128)} %bitcast.9), calls=%async_computation | async-start | bytes 1310720 | tf_op jit(solution)/shard_map/all_to_all | solution.py:314
  28.6 43.6 %copy-start.2 = (bf16[1024,1024]{1,0:T(8,128)(2,1)S(1)}, bf16[1024,1024]{1,0:T(8,128)(2,1)}, u32[]{:S(2)}) copy-start(bf16[1024,1024]{1,0:T(8,128)(2,1)} %x.1) | copy-start | bytes 6291460
  30.0 26.3 %collective-permute-start.7 = (bf16[272,512]{1,0:T(8,128)(2,1)S(1)}, bf16[272,512]{1,0:T(8,128)(2,1)}, u32[]{:S(2)}, u32[]{:S(2)}) collective-permute-start(bf16[272,512]{1,0:T(8,128)(2,1)S(1)} %maximum_select_fusion), channel_id=1, source_target_pairs={{0,4},{1,5},{2,6},{3,7},{8,12},{9,13},{10,14},{11,15},{16,20},{17,... | collective-permute-start | bytes 835592 | tf_op jit(solution)/shard_map/ppermute | solution.py:47
  39.2 23.0 %all-to-all-start.1 = ((f32[4,16,640]{2,1,0:T(8,128)}), f32[4,16,640]{2,1,0:T(8,128)S(1)}, u32[]{:S(2)}, u32[]{:S(2)}) async-start(f32[4,16,640]{2,1,0:T(8,128)} %bitcast.10), calls=%async_computation.1 | async-start | bytes 327680 | tf_op jit(solution)/shard_map/all_to_all | solution.py:314
  43.3 86.5 %reduce-scatter.2.cloned.1.call-start = ((), (), s32[]{:S(2)}) async-start(), calls=%async_computation.4 | async-start | bytes 4718592 | tf_op jit(solution)/shard_map/reduce_scatter | solution.py:394
  57.3 7.9 %collective-permute-start.10 = (bf16[272,512]{1,0:T(8,128)(2,1)S(1)}, bf16[272,512]{1,0:T(8,128)(2,1)S(1)}, u32[]{:S(2)}, u32[]{:S(2)}) collective-permute-start(bf16[272,512]{1,0:T(8,128)(2,1)S(1)} %broadcast_select_fusion.g0), channel_id=1, source_target_pairs={{0,3},{1,0},{2,1},{3,2},{4,7},{5,4},{6,5},{7,6},{8,11},{9,8},{10,9... | collective-permute-start | bytes 835592 | tf_op jit(solution)/shard_map/ppermute | solution.py:47
  57.4 8.2 %collective-permute-start.8 = (bf16[272,512]{1,0:T(8,128)(2,1)S(1)}, bf16[272,512]{1,0:T(8,128)(2,1)S(1)}, u32[]{:S(2)}, u32[]{:S(2)}) collective-permute-start(bf16[272,512]{1,0:T(8,128)(2,1)S(1)} %broadcast_select_fusion.g0), channel_id=1, source_target_pairs={{0,1},{1,2},{2,3},{3,0},{4,5},{5,6},{6,7},{7,4},{8,9},{9,10},{10,1... | collective-permute-start | bytes 835592 | tf_op jit(solution)/shard_map/ppermute | solution.py:47
  60.1 12.1 %collective-permute-start.9 = (bf16[272,512]{1,0:T(8,128)(2,1)S(1)}, bf16[272,512]{1,0:T(8,128)(2,1)S(1)}, u32[]{:S(2)}, u32[]{:S(2)}) collective-permute-start(bf16[272,512]{1,0:T(8,128)(2,1)S(1)} %broadcast_select_fusion.g0), channel_id=1, source_target_pairs={{0,2},{1,3},{2,0},{3,1},{4,6},{5,7},{6,4},{7,5},{8,10},{9,11},{10,... | collective-permute-start | bytes 835592 | tf_op jit(solution)/shard_map/ppermute | solution.py:47
  62.3 9.9 %collective-permute-start.3 = (f32[16,640]{1,0:T(8,128)S(1)}, f32[16,640]{1,0:T(8,128)S(1)}, u32[]{:S(2)}, u32[]{:S(2)}) collective-permute-start(f32[16,640]{1,0:T(8,128)S(1)} %reduce_sum.19), channel_id=1, source_target_pairs={{0,4},{8,12},{16,20},{24,28},{32,36},{40,44},{48,52},{56,60},{64,6... | collective-permute-start | bytes 122888 | tf_op jit(solution)/shard_map/ppermute | solution.py:47
  78.1 1.9 %copy-start = (f32[8,128,1024]{2,1,0:T(8,128)}, f32[8,128,1024]{2,1,0:T(8,128)S(1)}, u32[]{:S(2)}) copy-start(f32[8,128,1024]{2,1,0:T(8,128)S(1)} %covariance.1) | copy-start | bytes 12582916
  80.1 2.6 %collective-permute-start.11 = (f32[16,640]{1,0:T(8,128)S(1)}, f32[16,640]{1,0:T(8,128)S(1)}, u32[]{:S(2)}, u32[]{:S(2)}) collective-permute-start(f32[16,640]{1,0:T(8,128)S(1)} %broadcast_select_fusion.1), channel_id=1, source_target_pairs={{0,2},{4,6},{8,10},{12,14},{16,18},{20,22},{24,26},{28,30},{32,34}... | collective-permute-start | bytes 122888 | tf_op jit(solution)/shard_map/ppermute | solution.py:47
  80.8 2.0 %collective-permute-start.12 = (f32[16,640]{1,0:T(8,128)S(1)}, f32[16,640]{1,0:T(8,128)S(1)}, u32[]{:S(2)}, u32[]{:S(2)}) collective-permute-start(f32[16,640]{1,0:T(8,128)S(1)} %broadcast_select_fusion.1), channel_id=1, source_target_pairs={{0,1},{4,5},{8,9},{12,13},{16,17},{20,21},{24,25},{28,29},{32,33},... | collective-permute-start | bytes 122888 | tf_op jit(solution)/shard_map/ppermute | solution.py:47
  81.4 7.6 %collective-permute-start.13 = (f32[16,640]{1,0:T(8,128)S(1)}, f32[16,640]{1,0:T(8,128)S(1)}, u32[]{:S(2)}, u32[]{:S(2)}) collective-permute-start(f32[16,640]{1,0:T(8,128)S(1)} %broadcast_select_fusion.1), channel_id=1, source_target_pairs={{0,3},{4,7},{8,11},{12,15},{16,19},{20,23},{24,27},{28,31},{32,35}... | collective-permute-start | bytes 122888 | tf_op jit(solution)/shard_map/ppermute | solution.py:47
  111.7 4.2 %collective-permute-start.14 = (f32[256,640]{1,0:T(8,128)S(1)}, f32[256,640]{1,0:T(8,128)S(1)}, u32[]{:S(2)}, u32[]{:S(2)}) collective-permute-start(f32[256,640]{1,0:T(8,128)S(1)} %bitcast.15), channel_id=1, source_target_pairs={{0,8},{1,9},{2,10},{3,11},{4,12},{5,13},{6,14},{7,15},{8,0},{9,1},... | collective-permute-start | bytes 1966088 | tf_op jit(solution)/shard_map/ppermute | solution.py:47
  130.9 6.7 %collective-permute-start.15 = (f32[32,1024]{1,0:T(8,128)S(1)}, f32[32,1024]{1,0:T(8,128)S(1)}, u32[]{:S(2)}, u32[]{:S(2)}) collective-permute-start(f32[32,1024]{1,0:T(8,128)S(1)} %get-tuple-element.36), channel_id=1, source_target_pairs={{0,128},{1,129},{2,130},{3,131},{4,132},{5,133},{6,134},{7,135},{8... | collective-permute-start | bytes 393224 | tf_op jit(solution)/shard_map/ppermute | solution.py:47
  131.9 11.3 %collective-permute-start.16 = (f32[32,1024]{1,0:T(8,128)S(1)}, f32[32,1024]{1,0:T(8,128)S(1)}, u32[]{:S(2)}, u32[]{:S(2)}) collective-permute-start(f32[32,1024]{1,0:T(8,128)S(1)} %get-tuple-element.35), channel_id=1, source_target_pairs={{0,64},{1,65},{2,66},{3,67},{4,68},{5,69},{6,70},{7,71},{8,72},{9,... | collective-permute-start | bytes 393224 | tf_op jit(solution)/shard_map/ppermute | solution.py:47
  133.2 12.3 %collective-permute-start.17 = (f32[32,1024]{1,0:T(8,128)S(1)}, f32[32,1024]{1,0:T(8,128)S(1)}, u32[]{:S(2)}, u32[]{:S(2)}) collective-permute-start(f32[32,1024]{1,0:T(8,128)S(1)} %get-tuple-element.34), channel_id=1, source_target_pairs={{0,192},{1,193},{2,194},{3,195},{4,196},{5,197},{6,198},{7,199},{8... | collective-permute-start | bytes 393224 | tf_op jit(solution)/shard_map/ppermute | solution.py:47
Sparse Core Ops, SparseCore 0:
  80.2 44.7 reduce-scatter.1

commit v4 on v3

--- a/solution.py
+++ b/solution.py
@@ -290,20 +290,33 @@
     inverse_step(o, w)
 
 
-def whiten_kernel(pos, inv, up, p0, p1, p2, p3, panel, cross, tau, left):
-    m = inv[...]
-    s = (p0[...] + p1[...]) + (p2[...] + p3[...])
-    left[0:32, :] = s[:, :P_SIZE]
-    left[32:64, :] = s[:, P_SIZE:]
+def mt_parts(a, b):
+    n = a.shape[0]
+    a0, a1, a2 = parts(a)
+    dims = (((1,), (1,)), ((), ()))
+    by = [
+        lax.dot_general(jnp.concatenate(rows, axis=0), p, dims, preferred_element_type=F32)
+        for rows, p in zip(((a0, a1, a2), (a0, a1), (a0,)), parts(b))
+    ]
+    low = by[0][2 * n :] + by[1][n:] + by[2]
+    return by[0][:n] + ((by[0][n : 2 * n] + by[1][:n]) + low)
+
+
+def tau_kernel(pos, inv, up, tau):
     rows = inv[pl.ds(pl.multiple_of(pos[2], 16), 16), :]
     u = up[...]
     r = lax.broadcasted_iota(jnp.int32, u.shape, 0)
     l = lax.broadcasted_iota(jnp.int32, u.shape, 1)
-    left[64:80, :] = mn(rows, u) + mt(rows, jnp.where(l > r, u, 0.0))
-    res = mt(left[...], m)
+    tau[...] = mt(mn(rows, u) + mt(rows, jnp.where(l > r, u, 0.0)), inv[...])
+
+
+def whiten_kernel(pos, inv, p0, p1, p2, p3, panel, cross, left):
+    s = (p0[...] + p1[...]) + (p2[...] + p3[...])
+    left[0:32, :] = s[:, :P_SIZE]
+    left[32:64, :] = s[:, P_SIZE:]
+    res = mt_parts(left[...], inv[...])
     panel[0] = res[0:32, :]
     cross[0] = res[32:64, :]
-    tau[...] = res[64:80, :]
 
 
 def swap_core(v, only=None):
@@ -400,13 +413,15 @@
     inv, up = call(unpack_kernel, [full, full], (pos, own, other), "factor0", flops=5 * 10**9, vmem=8)
     for o in range(NB, P_SIZE, NB):
         (inv,) = call(functools.partial(inverse_kernel, o), [full], (pos, inv), "factor%d" % o, flops=5 * 10**9, vmem=8)
+    (tau,) = call(
+        tau_kernel, [jax.ShapeDtypeStruct((16, P_SIZE), F32)], (pos, inv, up), "tau", flops=10**9, vmem=8
+    )
     own = jax.ShapeDtypeStruct((1, 32, P_SIZE), F32)
-    return tuple(
-        call(
-            whiten_kernel, [own, own, jax.ShapeDtypeStruct((16, P_SIZE), F32)],
-            (pos, inv, up, *rows), "whiten", scratch=[pltpu.VMEM((80, P_SIZE), F32)], flops=2 * 10**9,
-        )
-    )
+    panel, cross = call(
+        whiten_kernel, [own, own], (pos, inv, *rows), "whiten",
+        scratch=[pltpu.VMEM((64, P_SIZE), F32)], flops=10**9, vmem=8,
+    )
+    return panel, cross, tau
 
 
 def solution(mesh):

time: 156 us -> 155 us (level)
  the two profiles are of different devices: /device:TPU:167 before, /device:TPU:2 now
where the time goes in v4:
time: 155 us; the launch traced here: 153 us
  starting transfers between devices  33.9 us (22%)
  waiting for transfers between devices  33.8 us (22%)
  Pallas kernels  32.8 us (21%)
  blocking collectives  26.3 us (17%)
  between operations  14.2 us (9%)
  local copies, waits for them, and re-layouts  8.28 us (5%)
  other arithmetic  3.73 us (2%)
    pallas_call x8, Pallas kernels, call(): pl.pallas_call(kernel, grid=(1,), out_shape=outs, in_specs=specs, out_spe...  32.8 us
    ppermute x18, waiting for transfers between devices, move(): return lax.ppermute(value, AXES, pairs)  29.5 us
    all_to_all x1, blocking collectives, exchange(): return lax.all_to_all(v, axes, 0, 0, tiled=True)  26.3 us
    ppermute x18, starting transfers between devices, move(): return lax.ppermute(value, AXES, pairs)  22.1 us
    all_to_all x2, starting transfers between devices, exchange(): return lax.all_to_all(v, axes, 0, 0, tiled=True)  11.8 us
    all_to_all x2, waiting for transfers between devices, exchange(): return lax.all_to_all(v, axes, 0, 0, tiled=True)  4.16 us
    unnamed x6, local copies, waits for them, and re-layouts  3.53 us
  transfers between devices with their start and end apart: 21, of which 9 were waited for; matrix products, arithmetic and copies ran while one was open for 4% of the time, Pallas kernels for 14%

profile of v4, /device:TPU:2, one launch (start us, length us, event | category | flops | bytes accessed | tf_op | source)
XLA Modules:
  0.0 153.1 jit_solution(9457715226974703375)
XLA Ops:
  7.2 0.7 fusion.1
  7.9 0.7 collective-permute-start.1
  8.6 0.7 collective-permute-start
  9.2 2.0 %fusion = (bf16[272,512]{1,0:T(8,128)(2,1)S(1)}, bf16[272,512]{1,0:T(8,128)(2,1)}, bf16[272,512]{1,0:T(8,128)(2,1)}) fusion(bf16[1024,1024]{1,0:T(8,128)(2,1)} %x.1), kind=kLoop, calls=%fused_computation.6 | loop fusion | bytes 1671168 | tf_op jit(solution)/shard_map/slice | solution.py:377
  11.2 0.7 slice.40
  12.0 0.1 add_bitcast_fusion
  12.0 0.7 pad_add_fusion.table
  12.7 0.1 stack.39.pos
  12.8 0.0 collective-permute-done.1.after
  12.8 0.0 collective-permute-done.before
  12.8 0.0 copy-start.1
  12.8 1.6 %copy-done.1 = bf16[1024,1024]{1,0:T(8,128)(2,1)S(1)} copy-done((bf16[1024,1024]{1,0:T(8,128)(2,1)S(1)}, bf16[1024,1024]{1,0:T(8,128)(2,1)}, u32[]{:S(2)}) %copy-start.1) | copy-done | bytes 2097176
  14.4 4.2 %diagonal.1 = (f32[256,640]{1,0:T(8,128)S(1)}, f32[256,640]{1,0:T(8,128)S(1)}) custom-call(s32[6]{0:T(128)S(1)} %stack.39.pos, s32[3,64]{1,0:T(4,128)S(1)} %pad_add_fusion.table, bf16[1024,1024]{1,0:T(8,128)(2,1)S(1)} %copy-done.1, bf16[16,512]{1,0:T(8,128)(2,1)S(1)} %collective-permute-done.before, bf16[16,512]{1,0:T(8,128)(2,1)S(1)} %collective-permute-done.1.after), custom_call_target="tpu_custom_call" | custom-call | flops 3000000000 | bytes 1048576 | tf_op jit(solution)/shard_map/diagonal/pallas_call | solution.py:57
  18.6 0.7 collective-permute-start.2
  19.3 1.4 collective-permute-start.4
  20.7 1.3 collective-permute-start.5
  22.0 1.4 collective-permute-start.6
  23.4 0.0 collective-permute-done.2
  23.4 0.9 add.25
  24.3 4.5 %all-to-all-start = ((f32[4,64,640]{2,1,0:T(8,128)}), f32[4,64,640]{2,1,0:T(8,128)S(1)}, u32[]{:S(2)}, u32[]{:S(2)}) async-start(f32[4,64,640]{2,1,0:T(8,128)} %bitcast.9), calls=%async_computation | async-start | bytes 1310720 | tf_op jit(solution)/shard_map/all_to_all | solution.py:327
  28.8 0.0 collective-permute-done.4
  28.8 11.9 %collective-permute-done.5 = bf16[272,512]{1,0:T(8,128)(2,1)} collective-permute-done((bf16[272,512]{1,0:T(8,128)(2,1)}, bf16[272,512]{1,0:T(8,128)(2,1)}, u32[]{:S(2)}, u32[]{:S(2)}) %collective-permute-start.5) | collective-permute-done | bytes 278560 | tf_op jit(solution)/shard_map/ppermute | solution.py:47
  40.7 0.0 collective-permute-done.6
  40.7 1.3 maximum_select_fusion
  41.9 2.0 %collective-permute-start.7 = (bf16[272,512]{1,0:T(8,128)(2,1)S(1)}, bf16[272,512]{1,0:T(8,128)(2,1)}, u32[]{:S(2)}, u32[]{:S(2)}) collective-permute-start(bf16[272,512]{1,0:T(8,128)(2,1)S(1)} %maximum_select_fusion), channel_id=1, source_target_pairs={{0,4},{1,5},{2,6},{3,7},{8,12},{9,13},{10,14},{11,15},{16,20},{17,... | collective-permute-start | bytes 835592 | tf_op jit(solution)/shard_map/ppermute | solution.py:47
  44.0 0.0 all-to-all-done
  44.0 0.7 reduce_sum.18
  44.7 7.3 %all-to-all-start.1 = ((f32[4,16,640]{2,1,0:T(8,128)}), f32[4,16,640]{2,1,0:T(8,128)S(1)}, u32[]{:S(2)}, u32[]{:S(2)}) async-start(f32[4,16,640]{2,1,0:T(8,128)} %bitcast.10), calls=%async_computation.1 | async-start | bytes 327680 | tf_op jit(solution)/shard_map/all_to_all | solution.py:327
  52.0 0.0 collective-permute-done.7
  52.0 0.1 broadcast_select_fusion.g0
  52.0 4.1 %collective-permute-start.10 = (bf16[272,512]{1,0:T(8,128)(2,1)S(1)}, bf16[272,512]{1,0:T(8,128)(2,1)S(1)}, u32[]{:S(2)}, u32[]{:S(2)}) collective-permute-start(bf16[272,512]{1,0:T(8,128)(2,1)S(1)} %broadcast_select_fusion.g0), channel_id=1, source_target_pairs={{0,3},{1,0},{2,1},{3,2},{4,7},{5,4},{6,5},{7,6},{8,11},{9,8},{10,9... | collective-permute-start | bytes 835592 | tf_op jit(solution)/shard_map/ppermute | solution.py:47
  56.2 0.0 collective-permute-start.9
  56.2 1.6 %collective-permute-start.8 = (bf16[272,512]{1,0:T(8,128)(2,1)S(1)}, bf16[272,512]{1,0:T(8,128)(2,1)S(1)}, u32[]{:S(2)}, u32[]{:S(2)}) collective-permute-start(bf16[272,512]{1,0:T(8,128)(2,1)S(1)} %broadcast_select_fusion.g0), channel_id=1, source_target_pairs={{0,1},{1,2},{2,3},{3,0},{4,5},{5,6},{6,7},{7,4},{8,9},{9,10},{10,1... | collective-permute-start | bytes 835592 | tf_op jit(solution)/shard_map/ppermute | solution.py:47
  57.7 4.2 %all-to-all-done.1 = f32[4,16,640]{2,1,0:T(8,128)S(1)} async-done(((f32[4,16,640]{2,1,0:T(8,128)}), f32[4,16,640]{2,1,0:T(8,128)S(1)}, u32[]{:S(2)}, u32[]{:S(2)}) %all-to-all-start.1) | async-done | bytes 163872 | tf_op jit(solution)/shard_map/all_to_all | solution.py:327
  61.9 0.7 collective-permute-start.3
  62.6 3.7 %collective-permute-done.10.g3 = bf16[272,512]{1,0:T(8,128)(2,1)S(1)} collective-permute-done((bf16[272,512]{1,0:T(8,128)(2,1)S(1)}, bf16[272,512]{1,0:T(8,128)(2,1)S(1)}, u32[]{:S(2)}, u32[]{:S(2)}) %collective-permute-start.10) | collective-permute-done | bytes 278560 | tf_op jit(solution)/shard_map/ppermute | solution.py:47
  66.3 1.4 collective-permute-done.9.g2
  67.7 0.9 collective-permute-done.8.g1
  68.5 0.0 collective-permute-done.3
  68.5 5.9 %covariance.1 = f32[8,128,1024]{2,1,0:T(8,128)S(1)} custom-call(s32[6]{0:T(128)S(1)} %stack.39.pos, s32[3,64]{1,0:T(4,128)S(1)} %pad_add_fusion.table, bf16[1024,1024]{1,0:T(8,128)(2,1)S(1)} %copy-done.2, bf16[272,512]{1,0:T(8,128)(2,1)S(1)} %broadcast_select_fusion.g0, bf16[272,512]{1,0:T(8,128)(2,1)S(1)} %collective-permute-done.8.g1, ...), custom_call_target="tpu_custom_call" | custom-call | flops 5000000000 | bytes 1048576 | tf_op jit(solution)/shard_map/covariance/pallas_call | solution.py:57
  74.5 1.9 %copy-done = f32[8,128,1024]{2,1,0:T(8,128)} copy-done((f32[8,128,1024]{2,1,0:T(8,128)}, f32[8,128,1024]{2,1,0:T(8,128)S(1)}, u32[]{:S(2)}) %copy-start) | copy-done | bytes 4194328
  76.4 0.0 reduce-scatter.2.cloned.1.call-update
  76.4 0.7 collective-permute-start.13
  77.1 1.3 collective-permute-start.12
  78.4 0.7 collective-permute-start.11
  79.1 0.0 collective-permute-done.13
  79.1 6.8 %collective-permute-done.12 = f32[16,640]{1,0:T(8,128)S(1)} collective-permute-done((f32[16,640]{1,0:T(8,128)S(1)}, f32[16,640]{1,0:T(8,128)S(1)}, u32[]{:S(2)}, u32[]{:S(2)}) %collective-permute-start.12) | collective-permute-done | bytes 40992 | tf_op jit(solution)/shard_map/ppermute | solution.py:47
  85.9 0.0 collective-permute-done.11
  86.0 26.3 %all_to_all.15 = f32[16,16,640]{2,1,0:T(8,128)S(1)} all-to-all(f32[16,16,640]{2,1,0:T(8,128)S(1)} %broadcast_in_dim.2), channel_id=1, replica_groups=mesh['z'=4,'y'=4,'c'=2,'w'=2,'x'=4] {'y','z'}, dimensions={0} | all-to-all | bytes 1310720 | tf_op jit(solution)/shard_map/all_to_all | solution.py:327
  112.3 0.0 collective-permute-start.14
  112.3 2.1 %collective-permute-done.14.other = f32[256,640]{1,0:T(8,128)S(1)} collective-permute-done((f32[256,640]{1,0:T(8,128)S(1)}, f32[256,640]{1,0:T(8,128)S(1)}, u32[]{:S(2)}, u32[]{:S(2)}) %collective-permute-start.14) | collective-permute-done | bytes 655392 | tf_op jit(solution)/shard_map/ppermute | solution.py:47
  114.4 5.0 %factor0.1 = (f32[512,512]{1,0:T(8,128)S(1)}, f32[512,512]{1,0:T(8,128)S(1)}) custom-call(s32[6]{0:T(128)S(1)} %stack.39.pos, f32[256,640]{1,0:T(8,128)S(1)} %bitcast.16, f32[256,640]{1,0:T(8,128)S(1)} %collective-permute-done.14.other), custom_call_target="tpu_custom_call" | custom-call | flops 5000000000 | bytes 1048576 | tf_op jit(solution)/shard_map/factor0/pallas_call | solution.py:57
  119.3 4.5 %factor128.1.v = f32[512,512]{1,0:T(8,128)S(1)} custom-call(s32[6]{0:T(128)S(1)} %stack.39.pos, f32[512,512]{1,0:T(8,128)S(1)} %get-tuple-element.25.v), custom_call_target="tpu_custom_call" | custom-call | flops 5000000000 | bytes 1048576 | tf_op jit(solution)/shard_map/factor128/pallas_call | solution.py:57
  123.9 4.3 %factor256.1.v = f32[512,512]{1,0:T(8,128)S(1)} custom-call(s32[6]{0:T(128)S(1)} %stack.39.pos, f32[512,512]{1,0:T(8,128)S(1)} %factor128.1.v), custom_call_target="tpu_custom_call" | custom-call | flops 5000000000 | bytes 1048576 | tf_op jit(solution)/shard_map/factor256/pallas_call | solution.py:57
  128.2 0.2 reduce-scatter.2.cloned.1.call-done
  128.4 1.1 fusion.2
  129.5 4.4 %collective-permute-start.17 = (f32[32,1024]{1,0:T(8,128)S(1)}, f32[32,1024]{1,0:T(8,128)S(1)}, u32[]{:S(2)}, u32[]{:S(2)}) collective-permute-start(f32[32,1024]{1,0:T(8,128)S(1)} %get-tuple-element.38), channel_id=1, source_target_pairs={{0,192},{1,193},{2,194},{3,195},{4,196},{5,197},{6,198},{7,199},{8... | collective-permute-start | bytes 393224 | tf_op jit(solution)/shard_map/ppermute | solution.py:47
  133.9 0.7 collective-permute-start.15
  134.6 3.9 %factor384.1.inv = f32[512,512]{1,0:T(8,128)S(1)} custom-call(s32[6]{0:T(128)S(1)} %stack.39.pos, f32[512,512]{1,0:T(8,128)S(1)} %factor256.1.v), custom_call_target="tpu_custom_call" | custom-call | flops 5000000000 | bytes 1048576 | tf_op jit(solution)/shard_map/factor384/pallas_call | solution.py:57
  138.5 3.2 %tau.1 = f32[16,512]{1,0:T(8,128)} custom-call(s32[6]{0:T(128)S(1)} %stack.39.pos, f32[512,512]{1,0:T(8,128)S(1)} %factor384.1.inv, f32[512,512]{1,0:T(8,128)S(1)} %get-tuple-element.32.up), custom_call_target="tpu_custom_call" | custom-call | flops 1000000000 | bytes 1048576 | tf_op jit(solution)/shard_map/tau/pallas_call | solution.py:57
  141.7 0.0 collective-permute-done.17.p3
  141.7 0.0 collective-permute-done.16.p2
  141.7 2.7 %collective-permute-done.15.p1 = f32[32,1024]{1,0:T(8,128)S(1)} collective-permute-done((f32[32,1024]{1,0:T(8,128)S(1)}, f32[32,1024]{1,0:T(8,128)S(1)}, u32[]{:S(2)}, u32[]{:S(2)}) %collective-permute-start.15) | collective-permute-done | bytes 131104 | tf_op jit(solution)/shard_map/ppermute | solution.py:47
  144.4 1.8 %whiten.1 = (f32[1,32,512]{2,1,0:T(8,128)}, f32[1,32,512]{2,1,0:T(8,128)}) custom-call(s32[6]{0:T(128)S(1)} %stack.39.pos, f32[512,512]{1,0:T(8,128)S(1)} %factor384.1.inv, f32[32,1024]{1,0:T(8,128)S(1)} %get-tuple-element.41.p0, f32[32,1024]{1,0:T(8,128)S(1)} %collective-permute-done.15.p1, f32[32,1024]{1,0:T(8,128)S(1)} %collective-permute-done.16.p2, ...), custom_call_target="tpu_custom_call" | custom-call | flops 1000000000 | bytes 1048576 | tf_op jit(solution)/shard_map/whiten/pallas_call | solution.py:57
  (10 shorter events, 0.1 us)
Async XLA Ops:
  7.9 4.9 %collective-permute-start.1 = (bf16[16,512]{1,0:T(8,128)(2,1)S(1)}, bf16[16,512]{1,0:T(8,128)(2,1)S(1)}, u32[]{:S(2)}, u32[]{:S(2)}) collective-permute-start(bf16[16,512]{1,0:T(8,128)(2,1)S(1)} %get-tuple-element.36), channel_id=1, source_target_pairs={{8,0},{16,8},{24,16},{32,24},{40,32},{48,40},{56,48},{64,56},{72,6... | collective-permute-start | bytes 49160 | tf_op jit(solution)/shard_map/ppermute | solution.py:47
  8.6 4.3 %collective-permute-start = (bf16[16,512]{1,0:T(8,128)(2,1)S(1)}, bf16[16,512]{1,0:T(8,128)(2,1)S(1)}, u32[]{:S(2)}, u32[]{:S(2)}) collective-permute-start(bf16[16,512]{1,0:T(8,128)(2,1)S(1)} %get-tuple-element.37), channel_id=1, source_target_pairs={{0,8},{8,16},{16,24},{24,32},{32,40},{40,48},{48,56},{56,64},{64,7... | collective-permute-start | bytes 49160 | tf_op jit(solution)/shard_map/ppermute | solution.py:47
  12.8 1.6 %copy-start.1 = (bf16[1024,1024]{1,0:T(8,128)(2,1)S(1)}, bf16[1024,1024]{1,0:T(8,128)(2,1)}, u32[]{:S(2)}) copy-start(bf16[1024,1024]{1,0:T(8,128)(2,1)} %x.1) | copy-start | bytes 6291460
  18.6 4.8 %collective-permute-start.2 = (f32[256,640]{1,0:T(8,128)S(1)}, f32[256,640]{1,0:T(8,128)S(1)}, u32[]{:S(2)}, u32[]{:S(2)}) collective-permute-start(f32[256,640]{1,0:T(8,128)S(1)} %get-tuple-element.20), channel_id=1, source_target_pairs={{0,8},{8,0},{16,24},{24,16},{32,40},{40,32},{48,56},{56,48},{64,72... | collective-permute-start | bytes 1966088 | tf_op jit(solution)/shard_map/ppermute | solution.py:47
  19.3 9.5 %collective-permute-start.4 = (bf16[272,512]{1,0:T(8,128)(2,1)}, bf16[272,512]{1,0:T(8,128)(2,1)}, u32[]{:S(2)}, u32[]{:S(2)}) collective-permute-start(bf16[272,512]{1,0:T(8,128)(2,1)} %get-tuple-element.21), channel_id=1, source_target_pairs={{0,2},{8,10},{16,18},{24,26},{32,34},{40,42},{48,50},{56,58},{64,6... | collective-permute-start | bytes 835592 | tf_op jit(solution)/shard_map/ppermute | solution.py:47
  20.7 20.0 %collective-permute-start.5 = (bf16[272,512]{1,0:T(8,128)(2,1)}, bf16[272,512]{1,0:T(8,128)(2,1)}, u32[]{:S(2)}, u32[]{:S(2)}) collective-permute-start(bf16[272,512]{1,0:T(8,128)(2,1)} %get-tuple-element.22), channel_id=1, source_target_pairs={{0,1},{8,9},{16,17},{24,25},{32,33},{40,41},{48,49},{56,57},{64,65... | collective-permute-start | bytes 835592 | tf_op jit(solution)/shard_map/ppermute | solution.py:47
  22.0 18.7 %collective-permute-start.6 = (bf16[272,512]{1,0:T(8,128)(2,1)S(1)}, bf16[272,512]{1,0:T(8,128)(2,1)}, u32[]{:S(2)}, u32[]{:S(2)}) collective-permute-start(bf16[272,512]{1,0:T(8,128)(2,1)S(1)} %get-tuple-element.23), channel_id=1, source_target_pairs={{0,3},{8,11},{16,19},{24,27},{32,35},{40,43},{48,51},{56,59},{64,6... | collective-permute-start | bytes 835592 | tf_op jit(solution)/shard_map/ppermute | solution.py:47
  24.3 19.7 %all-to-all-start = ((f32[4,64,640]{2,1,0:T(8,128)}), f32[4,64,640]{2,1,0:T(8,128)S(1)}, u32[]{:S(2)}, u32[]{:S(2)}) async-start(f32[4,64,640]{2,1,0:T(8,128)} %bitcast.9), calls=%async_computation | async-start | bytes 1310720 | tf_op jit(solution)/shard_map/all_to_all | solution.py:327
  28.8 39.8 %copy-start.2 = (bf16[1024,1024]{1,0:T(8,128)(2,1)S(1)}, bf16[1024,1024]{1,0:T(8,128)(2,1)}, u32[]{:S(2)}) copy-start(bf16[1024,1024]{1,0:T(8,128)(2,1)} %x.1) | copy-start | bytes 6291460
  41.9 10.0 %collective-permute-start.7 = (bf16[272,512]{1,0:T(8,128)(2,1)S(1)}, bf16[272,512]{1,0:T(8,128)(2,1)}, u32[]{:S(2)}, u32[]{:S(2)}) collective-permute-start(bf16[272,512]{1,0:T(8,128)(2,1)S(1)} %maximum_select_fusion), channel_id=1, source_target_pairs={{0,4},{1,5},{2,6},{3,7},{8,12},{9,13},{10,14},{11,15},{16,20},{17,... | collective-permute-start | bytes 835592 | tf_op jit(solution)/shard_map/ppermute | solution.py:47
  44.7 17.2 %all-to-all-start.1 = ((f32[4,16,640]{2,1,0:T(8,128)}), f32[4,16,640]{2,1,0:T(8,128)S(1)}, u32[]{:S(2)}, u32[]{:S(2)}) async-start(f32[4,16,640]{2,1,0:T(8,128)} %bitcast.10), calls=%async_computation.1 | async-start | bytes 327680 | tf_op jit(solution)/shard_map/all_to_all | solution.py:327
  52.0 76.4 %reduce-scatter.2.cloned.1.call-start = ((), (), s32[]{:S(2)}) async-start(), calls=%async_computation.4 | async-start | bytes 4718592 | tf_op jit(solution)/shard_map/reduce_scatter | solution.py:407
  52.0 14.2 %collective-permute-start.10 = (bf16[272,512]{1,0:T(8,128)(2,1)S(1)}, bf16[272,512]{1,0:T(8,128)(2,1)S(1)}, u32[]{:S(2)}, u32[]{:S(2)}) collective-permute-start(bf16[272,512]{1,0:T(8,128)(2,1)S(1)} %broadcast_select_fusion.g0), channel_id=1, source_target_pairs={{0,3},{1,0},{2,1},{3,2},{4,7},{5,4},{6,5},{7,6},{8,11},{9,8},{10,9... | collective-permute-start | bytes 835592 | tf_op jit(solution)/shard_map/ppermute | solution.py:47
  56.2 11.5 %collective-permute-start.9 = (bf16[272,512]{1,0:T(8,128)(2,1)S(1)}, bf16[272,512]{1,0:T(8,128)(2,1)S(1)}, u32[]{:S(2)}, u32[]{:S(2)}) collective-permute-start(bf16[272,512]{1,0:T(8,128)(2,1)S(1)} %broadcast_select_fusion.g0), channel_id=1, source_target_pairs={{0,2},{1,3},{2,0},{3,1},{4,6},{5,7},{6,4},{7,5},{8,10},{9,11},{10,... | collective-permute-start | bytes 835592 | tf_op jit(solution)/shard_map/ppermute | solution.py:47
  56.2 12.4 %collective-permute-start.8 = (bf16[272,512]{1,0:T(8,128)(2,1)S(1)}, bf16[272,512]{1,0:T(8,128)(2,1)S(1)}, u32[]{:S(2)}, u32[]{:S(2)}) collective-permute-start(bf16[272,512]{1,0:T(8,128)(2,1)S(1)} %broadcast_select_fusion.g0), channel_id=1, source_target_pairs={{0,1},{1,2},{2,3},{3,0},{4,5},{5,6},{6,7},{7,4},{8,9},{9,10},{10,1... | collective-permute-start | bytes 835592 | tf_op jit(solution)/shard_map/ppermute | solution.py:47
  61.9 6.6 %collective-permute-start.3 = (f32[16,640]{1,0:T(8,128)S(1)}, f32[16,640]{1,0:T(8,128)S(1)}, u32[]{:S(2)}, u32[]{:S(2)}) collective-permute-start(f32[16,640]{1,0:T(8,128)S(1)} %reduce_sum.19), channel_id=1, source_target_pairs={{0,4},{8,12},{16,20},{24,28},{32,36},{40,44},{48,52},{56,60},{64,6... | collective-permute-start | bytes 122888 | tf_op jit(solution)/shard_map/ppermute | solution.py:47
  74.5 1.9 %copy-start = (f32[8,128,1024]{2,1,0:T(8,128)}, f32[8,128,1024]{2,1,0:T(8,128)S(1)}, u32[]{:S(2)}) copy-start(f32[8,128,1024]{2,1,0:T(8,128)S(1)} %covariance.1) | copy-start | bytes 12582916
  76.4 2.6 %collective-permute-start.13 = (f32[16,640]{1,0:T(8,128)S(1)}, f32[16,640]{1,0:T(8,128)S(1)}, u32[]{:S(2)}, u32[]{:S(2)}) collective-permute-start(f32[16,640]{1,0:T(8,128)S(1)} %broadcast_select_fusion.1), channel_id=1, source_target_pairs={{0,3},{4,7},{8,11},{12,15},{16,19},{20,23},{24,27},{28,31},{32,35}... | collective-permute-start | bytes 122888 | tf_op jit(solution)/shard_map/ppermute | solution.py:47
  77.1 8.8 %collective-permute-start.12 = (f32[16,640]{1,0:T(8,128)S(1)}, f32[16,640]{1,0:T(8,128)S(1)}, u32[]{:S(2)}, u32[]{:S(2)}) collective-permute-start(f32[16,640]{1,0:T(8,128)S(1)} %broadcast_select_fusion.1), channel_id=1, source_target_pairs={{0,1},{4,5},{8,9},{12,13},{16,17},{20,21},{24,25},{28,29},{32,33},... | collective-permute-start | bytes 122888 | tf_op jit(solution)/shard_map/ppermute | solution.py:47
  78.4 7.5 %collective-permute-start.11 = (f32[16,640]{1,0:T(8,128)S(1)}, f32[16,640]{1,0:T(8,128)S(1)}, u32[]{:S(2)}, u32[]{:S(2)}) collective-permute-start(f32[16,640]{1,0:T(8,128)S(1)} %broadcast_select_fusion.1), channel_id=1, source_target_pairs={{0,2},{4,6},{8,10},{12,14},{16,18},{20,22},{24,26},{28,30},{32,34}... | collective-permute-start | bytes 122888 | tf_op jit(solution)/shard_map/ppermute | solution.py:47
  112.3 2.1 %collective-permute-start.14 = (f32[256,640]{1,0:T(8,128)S(1)}, f32[256,640]{1,0:T(8,128)S(1)}, u32[]{:S(2)}, u32[]{:S(2)}) collective-permute-start(f32[256,640]{1,0:T(8,128)S(1)} %bitcast.15), channel_id=1, source_target_pairs={{0,8},{1,9},{2,10},{3,11},{4,12},{5,13},{6,14},{7,15},{8,0},{9,1},... | collective-permute-start | bytes 1966088 | tf_op jit(solution)/shard_map/ppermute | solution.py:47
  129.5 12.2 %collective-permute-start.17 = (f32[32,1024]{1,0:T(8,128)S(1)}, f32[32,1024]{1,0:T(8,128)S(1)}, u32[]{:S(2)}, u32[]{:S(2)}) collective-permute-start(f32[32,1024]{1,0:T(8,128)S(1)} %get-tuple-element.38), channel_id=1, source_target_pairs={{0,192},{1,193},{2,194},{3,195},{4,196},{5,197},{6,198},{7,199},{8... | collective-permute-start | bytes 393224 | tf_op jit(solution)/shard_map/ppermute | solution.py:47
  133.9 7.8 %collective-permute-start.16 = (f32[32,1024]{1,0:T(8,128)S(1)}, f32[32,1024]{1,0:T(8,128)S(1)}, u32[]{:S(2)}, u32[]{:S(2)}) collective-permute-start(f32[32,1024]{1,0:T(8,128)S(1)} %get-tuple-element.39), channel_id=1, source_target_pairs={{0,64},{1,65},{2,66},{3,67},{4,68},{5,69},{6,70},{7,71},{8,72},{9,... | collective-permute-start | bytes 393224 | tf_op jit(solution)/shard_map/ppermute | solution.py:47
  133.9 10.5 %collective-permute-start.15 = (f32[32,1024]{1,0:T(8,128)S(1)}, f32[32,1024]{1,0:T(8,128)S(1)}, u32[]{:S(2)}, u32[]{:S(2)}) collective-permute-start(f32[32,1024]{1,0:T(8,128)S(1)} %get-tuple-element.40), channel_id=1, source_target_pairs={{0,128},{1,129},{2,130},{3,131},{4,132},{5,133},{6,134},{7,135},{8... | collective-permute-start | bytes 393224 | tf_op jit(solution)/shard_map/ppermute | solution.py:47
Sparse Core Ops, SparseCore 0:
  76.5 51.7 reduce-scatter.1

commit v5 on v4

--- a/solution.py
+++ b/solution.py
@@ -251,16 +251,20 @@
     return jnp.where(r >= c, v, 0.0)
 
 
-def unpack_kernel(pos, own, other, w, up):
+def unpack_kernel(pos, own, other, w, up, buf):
     c = pos[1]
     r = lax.broadcasted_iota(jnp.int32, (P_SIZE // 2, P_SIZE), 0)
     l = lax.broadcasted_iota(jnp.int32, (P_SIZE // 2, P_SIZE), 1)
     for half in range(2):
+        for k in range(16):
+            for q in range(4):
+                at = 16 * k + 4 * q
+                buf[at : at + 4, :] = jnp.where(c == half, own[q, k], other[q, k])
         at = slice(256 * half, 256 * half + 256)
-        v = jnp.where(c == half, own[:, :P_SIZE], other[:, :P_SIZE])
-        d = jnp.where(c == half, own[:, P_SIZE : P_SIZE + 1], other[:, P_SIZE : P_SIZE + 1])
+        v = buf[:, :P_SIZE]
         w[at, :] = v
-        up[at, :] = jnp.where(l > r + 256 * half, v, jnp.where(l == r + 256 * half, d, 0.0))
+        diag = buf[:, P_SIZE : P_SIZE + 1]
+        up[at, :] = jnp.where(l > r + 256 * half, v, jnp.where(l == r + 256 * half, diag, 0.0))
     r = lax.broadcasted_iota(jnp.int32, (NB, NB), 0)
     l = lax.broadcasted_iota(jnp.int32, (NB, NB), 1)
     for o in range(0, P_SIZE, NB):
@@ -345,7 +349,7 @@
 
 
 def diag_gather(own):
-    half = spread(own, ("y", "z"), 16).reshape(256, own.shape[1])
+    half = spread(spread(own, ("y", "z"), 16), "x", 4)
     return half, swap_core(half)
 
 
@@ -391,10 +395,9 @@
     over, *gathered = together(over, *gathered)
     rows16 = jnp.where(w == 0, rows16, over)
     copies = [
-        move(rows16, lambda z, y, c, w, x: (z, y, c, w, k) if x == 0 else None) for k in (2, 1, 3)
+        move(rows16[4 * k : 4 * k + 4], lambda z, y, c, w, x: (z, y, c, w, k) if x == 0 else None) for k in (2, 1, 3)
     ]
-    rows16 = jnp.where(x == 0, rows16, copies[0] + copies[1] + copies[2])
-    own, other = diag_gather(rows16)
+    own, other = diag_gather(jnp.where(x == 0, rows16[:4], copies[0] + copies[1] + copies[2]))
     (part,) = call(
         cov_kernel, [jax.ShapeDtypeStruct((8, 128, 2 * P_SIZE), F32)], (pos, table, frames_data, *gathered), "covariance",
         scratch=[
@@ -410,7 +413,10 @@
     ]
 
     full = jax.ShapeDtypeStruct((P_SIZE, P_SIZE), F32)
-    inv, up = call(unpack_kernel, [full, full], (pos, own, other), "factor0", flops=5 * 10**9, vmem=8)
+    inv, up = call(
+        unpack_kernel, [full, full], (pos, own, other), "factor0",
+        scratch=[pltpu.VMEM((P_SIZE // 2, P_SIZE + NB), F32)], flops=5 * 10**9, vmem=8,
+    )
     for o in range(NB, P_SIZE, NB):
         (inv,) = call(functools.partial(inverse_kernel, o), [full], (pos, inv), "factor%d" % o, flops=5 * 10**9, vmem=8)
     (tau,) = call(

time: 155 us -> 160 us (1.032)
  blocking collectives: 26.3 us -> 34.2 us
  starting transfers between devices: 33.9 us -> 31.7 us
  waiting for transfers between devices: 33.8 us -> 32 us
    all_to_all x1 -> x2, blocking collectives: 26.3 us -> 34.2 us  [exchange(): return lax.all_to_all(v, axes, 0, 0, tiled=True)]
    ppermute x18, starting transfers between devices: 22.1 us -> 20 us  [move(): return lax.ppermute(value, AXES, pairs)]
    ppermute x18, waiting for transfers between devices: 29.5 us -> 27.8 us  [move(): return lax.ppermute(value, AXES, pairs)]
  transfers between devices with their start and end apart: 21 -> 21, of which waited for: 9 -> 8; matrix products, arithmetic and copies ran while one was open for 4% -> 4% of each run, Pallas kernels for 14% -> 13%
where the time goes in v5:
time: 160 us; the launch traced here: 157 us
  blocking collectives  34.2 us (21%)
  Pallas kernels  33 us (21%)
  waiting for transfers between devices  32 us (20%)
  starting transfers between devices  31.7 us (20%)
  between operations  14.2 us (9%)
  local copies, waits for them, and re-layouts  8.35 us (5%)
  other arithmetic  3.74 us (2%)
    all_to_all x2, blocking collectives, exchange(): return lax.all_to_all(v, axes, 0, 0, tiled=True)  34.2 us
    pallas_call x8, Pallas kernels, call(): pl.pallas_call(kernel, grid=(1,), out_shape=outs, in_specs=specs, out_spe...  33 us
    ppermute x18, waiting for transfers between devices, move(): return lax.ppermute(value, AXES, pairs)  27.8 us
    ppermute x18, starting transfers between devices, move(): return lax.ppermute(value, AXES, pairs)  20 us
    all_to_all x2, starting transfers between devices, exchange(): return lax.all_to_all(v, axes, 0, 0, tiled=True)  11.8 us
    all_to_all x2, waiting for transfers between devices, exchange(): return lax.all_to_all(v, axes, 0, 0, tiled=True)  4.16 us
    unnamed x6, local copies, waits for them, and re-layouts  3.52 us
  transfers between devices with their start and end apart: 21, of which 8 were waited for; matrix products, arithmetic and copies ran while one was open for 4% of the time, Pallas kernels for 13%

profile of v5, /device:TPU:2, one launch (start us, length us, event | category | flops | bytes accessed | tf_op | source)
XLA Modules:
  0.0 157.3 jit_solution(5221220448029209472)
XLA Ops:
  7.2 0.7 fusion.1
  7.9 0.7 collective-permute-start.1
  8.6 0.7 collective-permute-start
  9.2 2.0 %fusion = (bf16[272,512]{1,0:T(8,128)(2,1)S(1)}, bf16[272,512]{1,0:T(8,128)(2,1)}, bf16[272,512]{1,0:T(8,128)(2,1)}) fusion(bf16[1024,1024]{1,0:T(8,128)(2,1)} %x.1), kind=kLoop, calls=%fused_computation.6 | loop fusion | bytes 1671168 | tf_op jit(solution)/shard_map/slice | solution.py:381
  11.2 0.7 slice.52
  12.0 0.1 add_bitcast_fusion
  12.1 0.7 pad_add_fusion.table
  12.7 0.1 stack.39.pos
  12.8 0.0 collective-permute-done.1.after
  12.8 0.0 collective-permute-done.before
  12.8 0.0 copy-start.1
  12.8 1.6 %copy-done.1 = bf16[1024,1024]{1,0:T(8,128)(2,1)S(1)} copy-done((bf16[1024,1024]{1,0:T(8,128)(2,1)S(1)}, bf16[1024,1024]{1,0:T(8,128)(2,1)}, u32[]{:S(2)}) %copy-start.1) | copy-done | bytes 2097176
  14.4 4.2 %diagonal.1 = (f32[256,640]{1,0:T(8,128)S(1)}, f32[256,640]{1,0:T(8,128)S(1)}) custom-call(s32[6]{0:T(128)S(1)} %stack.39.pos, s32[3,64]{1,0:T(4,128)S(1)} %pad_add_fusion.table, bf16[1024,1024]{1,0:T(8,128)(2,1)S(1)} %copy-done.1, bf16[16,512]{1,0:T(8,128)(2,1)S(1)} %collective-permute-done.before, bf16[16,512]{1,0:T(8,128)(2,1)S(1)} %collective-permute-done.1.after), custom_call_target="tpu_custom_call" | custom-call | flops 3000000000 | bytes 1048576 | tf_op jit(solution)/shard_map/diagonal/pallas_call | solution.py:57
  18.6 0.7 collective-permute-start.2
  19.3 1.4 collective-permute-start.4
  20.7 1.3 collective-permute-start.5
  22.0 1.4 collective-permute-start.6
  23.4 0.0 collective-permute-done.2
  23.4 0.9 add.25
  24.3 4.5 %all-to-all-start = ((f32[4,64,640]{2,1,0:T(8,128)}), f32[4,64,640]{2,1,0:T(8,128)S(1)}, u32[]{:S(2)}, u32[]{:S(2)}) async-start(f32[4,64,640]{2,1,0:T(8,128)} %bitcast.9), calls=%async_computation | async-start | bytes 1310720 | tf_op jit(solution)/shard_map/all_to_all | solution.py:331
  28.8 0.0 collective-permute-done.4
  28.8 11.9 %collective-permute-done.5 = bf16[272,512]{1,0:T(8,128)(2,1)} collective-permute-done((bf16[272,512]{1,0:T(8,128)(2,1)}, bf16[272,512]{1,0:T(8,128)(2,1)}, u32[]{:S(2)}, u32[]{:S(2)}) %collective-permute-start.5) | collective-permute-done | bytes 278560 | tf_op jit(solution)/shard_map/ppermute | solution.py:47
  40.7 0.0 collective-permute-done.6
  40.7 1.3 maximum_select_fusion
  42.0 2.0 %collective-permute-start.7 = (bf16[272,512]{1,0:T(8,128)(2,1)S(1)}, bf16[272,512]{1,0:T(8,128)(2,1)}, u32[]{:S(2)}, u32[]{:S(2)}) collective-permute-start(bf16[272,512]{1,0:T(8,128)(2,1)S(1)} %maximum_select_fusion), channel_id=1, source_target_pairs={{0,4},{1,5},{2,6},{3,7},{8,12},{9,13},{10,14},{11,15},{16,20},{17,... | collective-permute-start | bytes 835592 | tf_op jit(solution)/shard_map/ppermute | solution.py:47
  44.0 0.0 all-to-all-done
  44.0 0.7 reduce_sum.18
  44.7 7.3 %all-to-all-start.1 = ((f32[4,16,640]{2,1,0:T(8,128)}), f32[4,16,640]{2,1,0:T(8,128)S(1)}, u32[]{:S(2)}, u32[]{:S(2)}) async-start(f32[4,16,640]{2,1,0:T(8,128)} %bitcast.10), calls=%async_computation.1 | async-start | bytes 327680 | tf_op jit(solution)/shard_map/all_to_all | solution.py:331
  52.0 0.0 collective-permute-done.7
  52.0 0.1 broadcast_select_fusion.g0
  52.0 4.1 %collective-permute-start.10 = (bf16[272,512]{1,0:T(8,128)(2,1)S(1)}, bf16[272,512]{1,0:T(8,128)(2,1)S(1)}, u32[]{:S(2)}, u32[]{:S(2)}) collective-permute-start(bf16[272,512]{1,0:T(8,128)(2,1)S(1)} %broadcast_select_fusion.g0), channel_id=1, source_target_pairs={{0,3},{1,0},{2,1},{3,2},{4,7},{5,4},{6,5},{7,6},{8,11},{9,8},{10,9... | collective-permute-start | bytes 835592 | tf_op jit(solution)/shard_map/ppermute | solution.py:47
  56.2 0.0 collective-permute-start.9
  56.2 1.6 collective-permute-start.8
  57.7 4.2 %all-to-all-done.1 = f32[4,16,640]{2,1,0:T(8,128)S(1)} async-done(((f32[4,16,640]{2,1,0:T(8,128)}), f32[4,16,640]{2,1,0:T(8,128)S(1)}, u32[]{:S(2)}, u32[]{:S(2)}) %all-to-all-start.1) | async-done | bytes 163872 | tf_op jit(solution)/shard_map/all_to_all | solution.py:331
  61.9 0.7 collective-permute-start.3
  62.6 3.7 %collective-permute-done.10.g3 = bf16[272,512]{1,0:T(8,128)(2,1)S(1)} collective-permute-done((bf16[272,512]{1,0:T(8,128)(2,1)S(1)}, bf16[272,512]{1,0:T(8,128)(2,1)S(1)}, u32[]{:S(2)}, u32[]{:S(2)}) %collective-permute-start.10) | collective-permute-done | bytes 278560 | tf_op jit(solution)/shard_map/ppermute | solution.py:47
  66.3 1.4 collective-permute-done.9.g2
  67.7 0.9 collective-permute-done.8.g1
  68.5 0.0 collective-permute-done.3
  68.5 5.9 %covariance.1 = f32[8,128,1024]{2,1,0:T(8,128)S(1)} custom-call(s32[6]{0:T(128)S(1)} %stack.39.pos, s32[3,64]{1,0:T(4,128)S(1)} %pad_add_fusion.table, bf16[1024,1024]{1,0:T(8,128)(2,1)S(1)} %copy-done.2, bf16[272,512]{1,0:T(8,128)(2,1)S(1)} %broadcast_select_fusion.g0, bf16[272,512]{1,0:T(8,128)(2,1)S(1)} %collective-permute-done.8.g1, ...), custom_call_target="tpu_custom_call" | custom-call | flops 5000000000 | bytes 1048576 | tf_op jit(solution)/shard_map/covariance/pallas_call | solution.py:57
  74.5 1.9 %copy-done = f32[8,128,1024]{2,1,0:T(8,128)} copy-done((f32[8,128,1024]{2,1,0:T(8,128)}, f32[8,128,1024]{2,1,0:T(8,128)S(1)}, u32[]{:S(2)}) %copy-start) | copy-done | bytes 4194328
  76.4 0.0 reduce-scatter.2.cloned.1.call-update
  76.5 1.3 collective-permute-start.12
  77.8 0.7 collective-permute-start.13
  78.5 0.7 collective-permute-start.11
  79.1 3.5 %collective-permute-done.12 = f32[4,640]{1,0:T(4,128)S(1)} collective-permute-done((f32[4,640]{1,0:T(4,128)S(1)}, f32[4,640]{1,0:T(4,128)S(1)}, u32[]{:S(2)}, u32[]{:S(2)}) %collective-permute-start.12) | collective-permute-done | bytes 10272 | tf_op jit(solution)/shard_map/ppermute | solution.py:47
  82.6 0.0 collective-permute-done.13
  82.6 0.0 collective-permute-done.11
  82.7 19.7 %all_to_all.20 = f32[16,4,640]{2,1,0:T(4,128)S(1)} all-to-all(f32[16,4,640]{2,1,0:T(4,128)S(1)} %broadcast_in_dim.4), channel_id=1, replica_groups=mesh['z'=4,'y'=4,'c'=2,'w'=2,'x'=4] {'y','z'}, dimensions={0} | all-to-all | bytes 327680 | tf_op jit(solution)/shard_map/all_to_all | solution.py:331
  102.4 0.1 broadcast_in_dim.5
  102.4 14.5 %all_to_all.21.own = f32[4,16,4,640]{3,2,1,0:T(4,128)S(1)} all-to-all(f32[4,16,4,640]{3,2,1,0:T(4,128)S(1)} %broadcast_in_dim.5), channel_id=1, replica_groups=mesh['z'=4,'y'=4,'c'=2,'w'=2,'x'=4] {'x'}, dimensions={0} | all-to-all | bytes 1310720 | tf_op jit(solution)/shard_map/all_to_all | solution.py:331
  117.0 2.2 %collective-permute-done.14.other = f32[4,16,4,640]{3,2,1,0:T(4,128)S(1)} collective-permute-done((f32[4,16,4,640]{3,2,1,0:T(4,128)S(1)}, f32[4,16,4,640]{3,2,1,0:T(4,128)S(1)}, u32[]{:S(2)}, u32[]{:S(2)}) %collective-permute-start.14) | collective-permute-done | bytes 655392 | tf_op jit(solution)/shard_map/ppermute | solution.py:47
  119.1 5.1 %factor0.1 = (f32[512,512]{1,0:T(8,128)S(1)}, f32[512,512]{1,0:T(8,128)S(1)}) custom-call(s32[6]{0:T(128)S(1)} %stack.39.pos, f32[4,16,4,640]{3,2,1,0:T(4,128)S(1)} %all_to_all.21.own, f32[4,16,4,640]{3,2,1,0:T(4,128)S(1)} %collective-permute-done.14.other), custom_call_target="tpu_custom_call" | custom-call | flops 5000000000 | bytes 1048576 | tf_op jit(solution)/shard_map/factor0/pallas_call | solution.py:57
  124.3 4.5 %factor128.1.v = f32[512,512]{1,0:T(8,128)S(1)} custom-call(s32[6]{0:T(128)S(1)} %stack.39.pos, f32[512,512]{1,0:T(8,128)S(1)} %get-tuple-element.25.v), custom_call_target="tpu_custom_call" | custom-call | flops 5000000000 | bytes 1048576 | tf_op jit(solution)/shard_map/factor128/pallas_call | solution.py:57
  128.8 4.3 %factor256.1.v = f32[512,512]{1,0:T(8,128)S(1)} custom-call(s32[6]{0:T(128)S(1)} %stack.39.pos, f32[512,512]{1,0:T(8,128)S(1)} %factor128.1.v), custom_call_target="tpu_custom_call" | custom-call | flops 5000000000 | bytes 1048576 | tf_op jit(solution)/shard_map/factor256/pallas_call | solution.py:57
  133.2 0.0 reduce-scatter.2.cloned.1.call-done
  133.2 1.1 fusion.2
  134.3 1.0 collective-permute-start.17
  135.3 1.1 collective-permute-start.16
  136.4 0.8 collective-permute-start.15
  137.3 3.9 %factor384.1.inv = f32[512,512]{1,0:T(8,128)S(1)} custom-call(s32[6]{0:T(128)S(1)} %stack.39.pos, f32[512,512]{1,0:T(8,128)S(1)} %factor256.1.v), custom_call_target="tpu_custom_call" | custom-call | flops 5000000000 | bytes 1048576 | tf_op jit(solution)/shard_map/factor384/pallas_call | solution.py:57
  141.1 3.2 %tau.1 = f32[16,512]{1,0:T(8,128)} custom-call(s32[6]{0:T(128)S(1)} %stack.39.pos, f32[512,512]{1,0:T(8,128)S(1)} %factor384.1.inv, f32[512,512]{1,0:T(8,128)S(1)} %get-tuple-element.32.up), custom_call_target="tpu_custom_call" | custom-call | flops 1000000000 | bytes 1048576 | tf_op jit(solution)/shard_map/tau/pallas_call | solution.py:57
  144.4 4.3 %collective-permute-done.15.p1 = f32[32,1024]{1,0:T(8,128)S(1)} collective-permute-done((f32[32,1024]{1,0:T(8,128)S(1)}, f32[32,1024]{1,0:T(8,128)S(1)}, u32[]{:S(2)}, u32[]{:S(2)}) %collective-permute-start.15) | collective-permute-done | bytes 131104 | tf_op jit(solution)/shard_map/ppermute | solution.py:47
  148.6 1.8 %whiten.1 = (f32[1,32,512]{2,1,0:T(8,128)}, f32[1,32,512]{2,1,0:T(8,128)}) custom-call(s32[6]{0:T(128)S(1)} %stack.39.pos, f32[512,512]{1,0:T(8,128)S(1)} %factor384.1.inv, f32[32,1024]{1,0:T(8,128)S(1)} %get-tuple-element.41.p0, f32[32,1024]{1,0:T(8,128)S(1)} %collective-permute-done.15.p1, f32[32,1024]{1,0:T(8,128)S(1)} %collective-permute-done.16.p2, ...), custom_call_target="tpu_custom_call" | custom-call | flops 1000000000 | bytes 1048576 | tf_op jit(solution)/shard_map/whiten/pallas_call | solution.py:57
  (13 shorter events, 0.1 us)
Async XLA Ops:
  7.9 4.9 %collective-permute-start.1 = (bf16[16,512]{1,0:T(8,128)(2,1)S(1)}, bf16[16,512]{1,0:T(8,128)(2,1)S(1)}, u32[]{:S(2)}, u32[]{:S(2)}) collective-permute-start(bf16[16,512]{1,0:T(8,128)(2,1)S(1)} %get-tuple-element.36), channel_id=1, source_target_pairs={{8,0},{16,8},{24,16},{32,24},{40,32},{48,40},{56,48},{64,56},{72,6... | collective-permute-start | bytes 49160 | tf_op jit(solution)/shard_map/ppermute | solution.py:47
  8.6 4.3 %collective-permute-start = (bf16[16,512]{1,0:T(8,128)(2,1)S(1)}, bf16[16,512]{1,0:T(8,128)(2,1)S(1)}, u32[]{:S(2)}, u32[]{:S(2)}) collective-permute-start(bf16[16,512]{1,0:T(8,128)(2,1)S(1)} %get-tuple-element.37), channel_id=1, source_target_pairs={{0,8},{8,16},{16,24},{24,32},{32,40},{40,48},{48,56},{56,64},{64,7... | collective-permute-start | bytes 49160 | tf_op jit(solution)/shard_map/ppermute | solution.py:47
  12.8 1.6 %copy-start.1 = (bf16[1024,1024]{1,0:T(8,128)(2,1)S(1)}, bf16[1024,1024]{1,0:T(8,128)(2,1)}, u32[]{:S(2)}) copy-start(bf16[1024,1024]{1,0:T(8,128)(2,1)} %x.1) | copy-start | bytes 6291460
  18.6 4.8 %collective-permute-start.2 = (f32[256,640]{1,0:T(8,128)S(1)}, f32[256,640]{1,0:T(8,128)S(1)}, u32[]{:S(2)}, u32[]{:S(2)}) collective-permute-start(f32[256,640]{1,0:T(8,128)S(1)} %get-tuple-element.20), channel_id=1, source_target_pairs={{0,8},{8,0},{16,24},{24,16},{32,40},{40,32},{48,56},{56,48},{64,72... | collective-permute-start | bytes 1966088 | tf_op jit(solution)/shard_map/ppermute | solution.py:47
  19.3 9.5 %collective-permute-start.4 = (bf16[272,512]{1,0:T(8,128)(2,1)}, bf16[272,512]{1,0:T(8,128)(2,1)}, u32[]{:S(2)}, u32[]{:S(2)}) collective-permute-start(bf16[272,512]{1,0:T(8,128)(2,1)} %get-tuple-element.21), channel_id=1, source_target_pairs={{0,2},{8,10},{16,18},{24,26},{32,34},{40,42},{48,50},{56,58},{64,6... | collective-permute-start | bytes 835592 | tf_op jit(solution)/shard_map/ppermute | solution.py:47
  20.7 20.0 %collective-permute-start.5 = (bf16[272,512]{1,0:T(8,128)(2,1)}, bf16[272,512]{1,0:T(8,128)(2,1)}, u32[]{:S(2)}, u32[]{:S(2)}) collective-permute-start(bf16[272,512]{1,0:T(8,128)(2,1)} %get-tuple-element.22), channel_id=1, source_target_pairs={{0,1},{8,9},{16,17},{24,25},{32,33},{40,41},{48,49},{56,57},{64,65... | collective-permute-start | bytes 835592 | tf_op jit(solution)/shard_map/ppermute | solution.py:47
  22.0 18.7 %collective-permute-start.6 = (bf16[272,512]{1,0:T(8,128)(2,1)S(1)}, bf16[272,512]{1,0:T(8,128)(2,1)}, u32[]{:S(2)}, u32[]{:S(2)}) collective-permute-start(bf16[272,512]{1,0:T(8,128)(2,1)S(1)} %get-tuple-element.23), channel_id=1, source_target_pairs={{0,3},{8,11},{16,19},{24,27},{32,35},{40,43},{48,51},{56,59},{64,6... | collective-permute-start | bytes 835592 | tf_op jit(solution)/shard_map/ppermute | solution.py:47
  24.3 19.7 %all-to-all-start = ((f32[4,64,640]{2,1,0:T(8,128)}), f32[4,64,640]{2,1,0:T(8,128)S(1)}, u32[]{:S(2)}, u32[]{:S(2)}) async-start(f32[4,64,640]{2,1,0:T(8,128)} %bitcast.9), calls=%async_computation | async-start | bytes 1310720 | tf_op jit(solution)/shard_map/all_to_all | solution.py:331
  28.8 39.8 %copy-start.2 = (bf16[1024,1024]{1,0:T(8,128)(2,1)S(1)}, bf16[1024,1024]{1,0:T(8,128)(2,1)}, u32[]{:S(2)}) copy-start(bf16[1024,1024]{1,0:T(8,128)(2,1)} %x.1) | copy-start | bytes 6291460
  42.0 10.0 %collective-permute-start.7 = (bf16[272,512]{1,0:T(8,128)(2,1)S(1)}, bf16[272,512]{1,0:T(8,128)(2,1)}, u32[]{:S(2)}, u32[]{:S(2)}) collective-permute-start(bf16[272,512]{1,0:T(8,128)(2,1)S(1)} %maximum_select_fusion), channel_id=1, source_target_pairs={{0,4},{1,5},{2,6},{3,7},{8,12},{9,13},{10,14},{11,15},{16,20},{17,... | collective-permute-start | bytes 835592 | tf_op jit(solution)/shard_map/ppermute | solution.py:47
  44.7 17.2 %all-to-all-start.1 = ((f32[4,16,640]{2,1,0:T(8,128)}), f32[4,16,640]{2,1,0:T(8,128)S(1)}, u32[]{:S(2)}, u32[]{:S(2)}) async-start(f32[4,16,640]{2,1,0:T(8,128)} %bitcast.10), calls=%async_computation.1 | async-start | bytes 327680 | tf_op jit(solution)/shard_map/all_to_all | solution.py:331
  52.0 81.2 %reduce-scatter.2.cloned.1.call-start = ((), (), s32[]{:S(2)}) async-start(), calls=%async_computation.5 | async-start | bytes 4718592 | tf_op jit(solution)/shard_map/reduce_scatter | solution.py:410
  52.0 14.2 %collective-permute-start.10 = (bf16[272,512]{1,0:T(8,128)(2,1)S(1)}, bf16[272,512]{1,0:T(8,128)(2,1)S(1)}, u32[]{:S(2)}, u32[]{:S(2)}) collective-permute-start(bf16[272,512]{1,0:T(8,128)(2,1)S(1)} %broadcast_select_fusion.g0), channel_id=1, source_target_pairs={{0,3},{1,0},{2,1},{3,2},{4,7},{5,4},{6,5},{7,6},{8,11},{9,8},{10,9... | collective-permute-start | bytes 835592 | tf_op jit(solution)/shard_map/ppermute | solution.py:47
  56.2 11.5 %collective-permute-start.9 = (bf16[272,512]{1,0:T(8,128)(2,1)S(1)}, bf16[272,512]{1,0:T(8,128)(2,1)S(1)}, u32[]{:S(2)}, u32[]{:S(2)}) collective-permute-start(bf16[272,512]{1,0:T(8,128)(2,1)S(1)} %broadcast_select_fusion.g0), channel_id=1, source_target_pairs={{0,2},{1,3},{2,0},{3,1},{4,6},{5,7},{6,4},{7,5},{8,10},{9,11},{10,... | collective-permute-start | bytes 835592 | tf_op jit(solution)/shard_map/ppermute | solution.py:47
  56.2 12.4 %collective-permute-start.8 = (bf16[272,512]{1,0:T(8,128)(2,1)S(1)}, bf16[272,512]{1,0:T(8,128)(2,1)S(1)}, u32[]{:S(2)}, u32[]{:S(2)}) collective-permute-start(bf16[272,512]{1,0:T(8,128)(2,1)S(1)} %broadcast_select_fusion.g0), channel_id=1, source_target_pairs={{0,1},{1,2},{2,3},{3,0},{4,5},{5,6},{6,7},{7,4},{8,9},{9,10},{10,1... | collective-permute-start | bytes 835592 | tf_op jit(solution)/shard_map/ppermute | solution.py:47
  61.9 6.6 %collective-permute-start.3 = (f32[16,640]{1,0:T(8,128)S(1)}, f32[16,640]{1,0:T(8,128)S(1)}, u32[]{:S(2)}, u32[]{:S(2)}) collective-permute-start(f32[16,640]{1,0:T(8,128)S(1)} %reduce_sum.19), channel_id=1, source_target_pairs={{0,4},{8,12},{16,20},{24,28},{32,36},{40,44},{48,52},{56,60},{64,6... | collective-permute-start | bytes 122888 | tf_op jit(solution)/shard_map/ppermute | solution.py:47
  74.5 1.9 %copy-start = (f32[8,128,1024]{2,1,0:T(8,128)}, f32[8,128,1024]{2,1,0:T(8,128)S(1)}, u32[]{:S(2)}) copy-start(f32[8,128,1024]{2,1,0:T(8,128)S(1)} %covariance.1) | copy-start | bytes 12582916
  76.5 6.1 %collective-permute-start.12 = (f32[4,640]{1,0:T(4,128)S(1)}, f32[4,640]{1,0:T(4,128)S(1)}, u32[]{:S(2)}, u32[]{:S(2)}) collective-permute-start(f32[4,640]{1,0:T(4,128)S(1)} %get-tuple-element.42), channel_id=1, source_target_pairs={{0,1},{4,5},{8,9},{12,13},{16,17},{20,21},{24,25},{28,29},{32,33},... | collective-permute-start | bytes 30728 | tf_op jit(solution)/shard_map/ppermute | solution.py:47
  77.8 4.8 %collective-permute-start.13 = (f32[4,640]{1,0:T(4,128)S(1)}, f32[4,640]{1,0:T(4,128)S(1)}, u32[]{:S(2)}, u32[]{:S(2)}) collective-permute-start(f32[4,640]{1,0:T(4,128)S(1)} %get-tuple-element.43), channel_id=1, source_target_pairs={{0,3},{4,7},{8,11},{12,15},{16,19},{20,23},{24,27},{28,31},{32,35}... | collective-permute-start | bytes 30728 | tf_op jit(solution)/shard_map/ppermute | solution.py:47
  78.5 4.2 %collective-permute-start.11 = (f32[4,640]{1,0:T(4,128)S(1)}, f32[4,640]{1,0:T(4,128)S(1)}, u32[]{:S(2)}, u32[]{:S(2)}) collective-permute-start(f32[4,640]{1,0:T(4,128)S(1)} %get-tuple-element.44), channel_id=1, source_target_pairs={{0,2},{4,6},{8,10},{12,14},{16,18},{20,22},{24,26},{28,30},{32,34}... | collective-permute-start | bytes 30728 | tf_op jit(solution)/shard_map/ppermute | solution.py:47
  117.0 2.2 %collective-permute-start.14 = (f32[4,16,4,640]{3,2,1,0:T(4,128)S(1)}, f32[4,16,4,640]{3,2,1,0:T(4,128)S(1)}, u32[]{:S(2)}, u32[]{:S(2)}) collective-permute-start(f32[4,16,4,640]{3,2,1,0:T(4,128)S(1)} %all_to_all.21.own), channel_id=1, source_target_pairs={{0,8},{1,9},{2,10},{3,11},{4,12},{5,13},{6,14},{7,15},{8,0},{9,1},... | collective-permute-start | bytes 1966088 | tf_op jit(solution)/shard_map/ppermute | solution.py:47
  134.3 10.0 %collective-permute-start.17 = (f32[32,1024]{1,0:T(8,128)S(1)}, f32[32,1024]{1,0:T(8,128)S(1)}, u32[]{:S(2)}, u32[]{:S(2)}) collective-permute-start(f32[32,1024]{1,0:T(8,128)S(1)} %get-tuple-element.38), channel_id=1, source_target_pairs={{0,192},{1,193},{2,194},{3,195},{4,196},{5,197},{6,198},{7,199},{8... | collective-permute-start | bytes 393224 | tf_op jit(solution)/shard_map/ppermute | solution.py:47
  135.3 9.1 %collective-permute-start.16 = (f32[32,1024]{1,0:T(8,128)S(1)}, f32[32,1024]{1,0:T(8,128)S(1)}, u32[]{:S(2)}, u32[]{:S(2)}) collective-permute-start(f32[32,1024]{1,0:T(8,128)S(1)} %get-tuple-element.39), channel_id=1, source_target_pairs={{0,64},{1,65},{2,66},{3,67},{4,68},{5,69},{6,70},{7,71},{8,72},{9,... | collective-permute-start | bytes 393224 | tf_op jit(solution)/shard_map/ppermute | solution.py:47
  136.4 12.2 %collective-permute-start.15 = (f32[32,1024]{1,0:T(8,128)S(1)}, f32[32,1024]{1,0:T(8,128)S(1)}, u32[]{:S(2)}, u32[]{:S(2)}) collective-permute-start(f32[32,1024]{1,0:T(8,128)S(1)} %get-tuple-element.40), channel_id=1, source_target_pairs={{0,128},{1,129},{2,130},{3,131},{4,132},{5,133},{6,134},{7,135},{8... | collective-permute-start | bytes 393224 | tf_op jit(solution)/shard_map/ppermute | solution.py:47
Sparse Core Ops, SparseCore 0:
  76.6 48.5 reduce-scatter.1

commit v6 on v3

--- a/solution.py
+++ b/solution.py
@@ -290,8 +290,19 @@
     inverse_step(o, w)
 
 
+def mt_parts(a, b):
+    n = a.shape[0]
+    a0, a1, a2 = parts(a)
+    dims = (((1,), (1,)), ((), ()))
+    by = [
+        lax.dot_general(jnp.concatenate(rows, axis=0), p, dims, preferred_element_type=F32)
+        for rows, p in zip(((a0, a1, a2), (a0, a1), (a0,)), parts(b))
+    ]
+    low = by[0][2 * n :] + by[1][n:] + by[2]
+    return by[0][:n] + ((by[0][n : 2 * n] + by[1][:n]) + low)
+
+
 def whiten_kernel(pos, inv, up, p0, p1, p2, p3, panel, cross, tau, left):
-    m = inv[...]
     s = (p0[...] + p1[...]) + (p2[...] + p3[...])
     left[0:32, :] = s[:, :P_SIZE]
     left[32:64, :] = s[:, P_SIZE:]
@@ -300,7 +311,7 @@
     r = lax.broadcasted_iota(jnp.int32, u.shape, 0)
     l = lax.broadcasted_iota(jnp.int32, u.shape, 1)
     left[64:80, :] = mn(rows, u) + mt(rows, jnp.where(l > r, u, 0.0))
-    res = mt(left[...], m)
+    res = mt_parts(left[...], inv[...])
     panel[0] = res[0:32, :]
     cross[0] = res[32:64, :]
     tau[...] = res[64:80, :]
@@ -322,9 +333,10 @@
     return lax.optimization_barrier(values)
 
 
-def diag_half(mine, theirs):
+def diag_half(mine, theirs, first):
     half = (mine + swap_core(theirs, (0, 0))).reshape(4, 64, mine.shape[1])
-    return jnp.sum(exchange(half, "y"), axis=0)
+    half, first = together(half, first)
+    return jnp.sum(exchange(half, "y"), axis=0), first
 
 
 def diag_rows(quarter):
@@ -361,21 +373,23 @@
         scratch=[pltpu.VMEM((tok + 2 * RIM, P_SIZE), BF16), pltpu.VMEM((tok, 3 * P_SIZE), BF16)],
         flops=3 * 10**9, block={2: (tok, P_SIZE)},
     )
-    theirs, *chunks = together(theirs, *(panel[STEP0 + CHUNK * (k - 1) : STEP0 + CHUNK * k] for k in (2, 1, 3)))
+    chunks = [panel[STEP0 + CHUNK * (k - 1) : STEP0 + CHUNK * k] for k in (2, 1, 3)]
     sent = [
         move(v, lambda z, y, c, w, x: (z, y, c, w, k) if (w, x) == (0, 0) else None)
         for k, v in zip((2, 1, 3), chunks)
     ]
     first = jnp.concatenate([before, behind, panel[:FIRST]], axis=0)
     hold = jnp.where(x == 0, first, sent[0] + sent[1] + sent[2])
+    theirs, hold = together(theirs, hold)
     over = move(hold, lambda z, y, c, w, x: (z, y, c, 1, x) if w == 0 else None)
-    rows16 = diag_rows(diag_half(mine, theirs))
+    quarter, over = diag_half(mine, theirs, over)
     hold = jnp.where(w == 0, hold, over)
     gathered = [hold] + [
         move(hold, lambda z, y, c, w, x: (z, y, c, w, (x + k) % 4)) for k in (1, 2, 3)
     ]
+    quarter, gathered[1] = together(quarter, gathered[1])
+    rows16 = diag_rows(quarter)
     over = move(rows16, lambda z, y, c, w, x: (z, y, c, 1, 0) if (w, x) == (0, 0) else None)
-    over, *gathered = together(over, *gathered)
     rows16 = jnp.where(w == 0, rows16, over)
     copies = [
         move(rows16, lambda z, y, c, w, x: (z, y, c, w, k) if x == 0 else None) for k in (2, 1, 3)
@@ -392,19 +406,19 @@
         flops=5 * 10**9, vmem=20, hbm=(3, 4, 5, 6),
     )
     t = lax.psum_scatter(part.reshape(1024, 2 * P_SIZE), ("y", "c"), scatter_dimension=0, tiled=True)
+    full = jax.ShapeDtypeStruct((P_SIZE, P_SIZE), F32)
+    inv, up = call(unpack_kernel, [full, full], (pos, own, other), "factor0", flops=5 * 10**9, vmem=8)
+    inv, t = together(inv, t)
     rows = [t[:32]] + [
         move(t[32 * k : 32 * k + 32], lambda z, y, c, w, x: ((z + k) % 4, y, c, w, x)) for k in (2, 1, 3)
     ]
-
-    full = jax.ShapeDtypeStruct((P_SIZE, P_SIZE), F32)
-    inv, up = call(unpack_kernel, [full, full], (pos, own, other), "factor0", flops=5 * 10**9, vmem=8)
     for o in range(NB, P_SIZE, NB):
         (inv,) = call(functools.partial(inverse_kernel, o), [full], (pos, inv), "factor%d" % o, flops=5 * 10**9, vmem=8)
     own = jax.ShapeDtypeStruct((1, 32, P_SIZE), F32)
     return tuple(
         call(
             whiten_kernel, [own, own, jax.ShapeDtypeStruct((16, P_SIZE), F32)],
-            (pos, inv, up, *rows), "whiten", scratch=[pltpu.VMEM((80, P_SIZE), F32)], flops=2 * 10**9,
+            (pos, inv, up, *rows), "whiten", scratch=[pltpu.VMEM((80, P_SIZE), F32)], flops=2 * 10**9, vmem=8,
         )
     )
 

time: 156 us -> 166 us (1.064)
  the two profiles are of different devices: /device:TPU:167 before, /device:TPU:37 now
where the time goes in v6:
time: 166 us; the launch traced here: 165 us
  waiting for transfers between devices  42.3 us (25%)
  starting transfers between devices  36.3 us (22%)
  Pallas kernels  31.3 us (19%)
  blocking collectives  26.4 us (16%)
  between operations  14.3 us (9%)
  local copies, waits for them, and re-layouts  7.5 us (5%)
  other arithmetic  6.92 us (4%)
    ppermute x18, waiting for transfers between devices, move(): return lax.ppermute(value, AXES, pairs)  40.2 us
    ppermute x18, starting transfers between devices, move(): return lax.ppermute(value, AXES, pairs)  32.1 us
    pallas_call x7, Pallas kernels, call(): pl.pallas_call(kernel, grid=(1,), out_shape=outs, in_specs=specs, out_spe...  31.3 us
    all_to_all x2, blocking collectives, exchange(): return lax.all_to_all(v, axes, 0, 0, tiled=True)  26.4 us
    all_to_all x1, starting transfers between devices, exchange(): return lax.all_to_all(v, axes, 0, 0, tiled=True)  4.2 us
  transfers between devices with their start and end apart: 20, of which 9 were waited for; matrix products, arithmetic and copies ran while one was open for 6% of the time, Pallas kernels for 8%

profile of v6, /device:TPU:37, one launch (start us, length us, event | category | flops | bytes accessed | tf_op | source)
XLA Modules:
  0.0 165.1 jit_solution(14166788878472978975)
XLA Ops:
  7.2 0.0 copy-start.1
  7.2 0.9 fusion.1
  8.1 0.7 collective-permute-start
  8.7 0.7 collective-permute-start.1
  9.4 2.1 %fusion = (bf16[272,512]{1,0:T(8,128)(2,1)}, bf16[272,512]{1,0:T(8,128)(2,1)}, bf16[272,512]{1,0:T(8,128)(2,1)}) fusion(bf16[1024,1024]{1,0:T(8,128)(2,1)} %x.1), kind=kLoop, calls=%fused_computation.6 | loop fusion | bytes 1671168 | tf_op jit(solution)/shard_map/slice | solution.py:376
  11.5 1.3 collective-permute-start.2
  12.8 1.4 collective-permute-start.3
  14.1 1.4 collective-permute-start.4
  15.5 0.7 slice.40
  16.2 0.1 add_bitcast_fusion
  16.3 0.7 pad_add_fusion.table
  17.0 1.7 %slice.43 = bf16[240,512]{1,0:T(8,128)(2,1)} slice(bf16[1024,1024]{1,0:T(8,128)(2,1)} %x.1), slice={[0:240], [0:512]} | slice | bytes 491520 | tf_op jit(solution)/shard_map/slice | solution.py:381
  18.7 0.1 stack.39.pos
  18.8 0.0 collective-permute-done.before
  18.8 0.0 collective-permute-done.1.after
  18.8 4.2 %diagonal.1 = (f32[256,640]{1,0:T(8,128)S(1)}, f32[256,640]{1,0:T(8,128)S(1)}) custom-call(s32[6]{0:T(128)S(1)} %stack.39.pos, s32[3,64]{1,0:T(4,128)S(1)} %pad_add_fusion.table, bf16[1024,1024]{1,0:T(8,128)(2,1)S(1)} %copy-done.1, bf16[16,512]{1,0:T(8,128)(2,1)S(1)} %collective-permute-done.before, bf16[16,512]{1,0:T(8,128)(2,1)S(1)} %collective-permute-done.1.after), custom_call_target="tpu_custom_call" | custom-call | flops 3000000000 | bytes 1048576 | tf_op jit(solution)/shard_map/diagonal/pallas_call | solution.py:57
  23.0 0.0 collective-permute-done.2
  23.0 0.0 collective-permute-done.3
  23.0 0.0 collective-permute-done.4
  23.0 0.0 copy-done.2
  23.0 2.0 %maximum_select_fusion = bf16[272,512]{1,0:T(8,128)(2,1)} fusion(bf16[240,512]{1,0:T(8,128)(2,1)S(1)} %copy-done.2, bf16[16,512]{1,0:T(8,128)(2,1)S(1)} %collective-permute-done.1.after, bf16[16,512]{1,0:T(8,128)(2,1)S(1)} %collective-permute-done.before, bf16[272,512]{1,0:T(8,128)(2,1)} %collective-permute-done.4, bf16[272,512]{1,0:T(8,128)(2,1)} %collective-permute-done.2, ...), kind=kLoop, calls=%fused_computation | loop fusion | flops 1810432 | bytes 1392641 | tf_op jit(solution)/shard_map/jit(_where)/select_n | solution.py:382
  25.0 1.5 collective-permute-start.5
  26.5 8.7 %collective-permute-start.6 = (bf16[272,512]{1,0:T(8,128)(2,1)}, bf16[272,512]{1,0:T(8,128)(2,1)}, u32[]{:S(2)}, u32[]{:S(2)}) collective-permute-start(bf16[272,512]{1,0:T(8,128)(2,1)} %maximum_select_fusion), channel_id=1, source_target_pairs={{0,4},{1,5},{2,6},{3,7},{8,12},{9,13},{10,14},{11,15},{16,20},{17,... | collective-permute-start | bytes 835592 | tf_op jit(solution)/shard_map/ppermute | solution.py:47
  35.2 0.0 collective-permute-done.5
  35.2 2.0 %add.27 = f32[256,640]{1,0:T(8,128)} add(f32[256,640]{1,0:T(8,128)S(1)} %get-tuple-element.15, f32[256,640]{1,0:T(8,128)} %collective-permute-done.5) | non-fusion elementwise | flops 163840 | bytes 1966080 | tf_op jit(solution)/shard_map/add | solution.py:337
  37.2 9.0 %collective-permute-done.6 = bf16[272,512]{1,0:T(8,128)(2,1)} collective-permute-done((bf16[272,512]{1,0:T(8,128)(2,1)}, bf16[272,512]{1,0:T(8,128)(2,1)}, u32[]{:S(2)}, u32[]{:S(2)}) %collective-permute-start.6) | collective-permute-done | bytes 278560 | tf_op jit(solution)/shard_map/ppermute | solution.py:47
  46.2 4.2 %all-to-all-start = ((f32[4,64,640]{2,1,0:T(8,128)}), f32[4,64,640]{2,1,0:T(8,128)}, u32[]{:S(2)}, u32[]{:S(2)}) async-start(f32[4,64,640]{2,1,0:T(8,128)} %bitcast.9), calls=%async_computation | async-start | bytes 1310720 | tf_op jit(solution)/shard_map/all_to_all | solution.py:325
  50.4 0.0 reduce-scatter.2.cloned.1.call-start
  50.4 1.0 broadcast_select_fusion.g0
  51.4 1.0 collective-permute-start.7
  52.4 2.9 %collective-permute-start.13 = (bf16[272,512]{1,0:T(8,128)(2,1)S(1)}, bf16[272,512]{1,0:T(8,128)(2,1)S(1)}, u32[]{:S(2)}, u32[]{:S(2)}) collective-permute-start(bf16[272,512]{1,0:T(8,128)(2,1)S(1)} %broadcast_select_fusion.g0), channel_id=1, source_target_pairs={{0,2},{1,3},{2,0},{3,1},{4,6},{5,7},{6,4},{7,5},{8,10},{9,11},{10,... | collective-permute-start | bytes 835592 | tf_op jit(solution)/shard_map/ppermute | solution.py:47
  55.3 2.0 %collective-permute-start.14 = (bf16[272,512]{1,0:T(8,128)(2,1)S(1)}, bf16[272,512]{1,0:T(8,128)(2,1)S(1)}, u32[]{:S(2)}, u32[]{:S(2)}) collective-permute-start(bf16[272,512]{1,0:T(8,128)(2,1)S(1)} %broadcast_select_fusion.g0), channel_id=1, source_target_pairs={{0,3},{1,0},{2,1},{3,2},{4,7},{5,4},{6,5},{7,6},{8,11},{9,8},{10,9... | collective-permute-start | bytes 835592 | tf_op jit(solution)/shard_map/ppermute | solution.py:47
  57.3 2.1 %all-to-all-done = f32[4,64,640]{2,1,0:T(8,128)} async-done(((f32[4,64,640]{2,1,0:T(8,128)}), f32[4,64,640]{2,1,0:T(8,128)}, u32[]{:S(2)}, u32[]{:S(2)}) %all-to-all-start) | async-done | bytes 655392 | tf_op jit(solution)/shard_map/all_to_all | solution.py:325
  59.4 1.1 reduce_sum.18
  60.6 0.0 collective-permute-done.7.g1
  60.6 7.1 %collective-permute-done.13.g2 = bf16[272,512]{1,0:T(8,128)(2,1)S(1)} collective-permute-done((bf16[272,512]{1,0:T(8,128)(2,1)S(1)}, bf16[272,512]{1,0:T(8,128)(2,1)S(1)}, u32[]{:S(2)}, u32[]{:S(2)}) %collective-permute-start.13) | collective-permute-done | bytes 278560 | tf_op jit(solution)/shard_map/ppermute | solution.py:47
  67.7 0.6 collective-permute-done.14.g3
  68.3 5.8 %covariance.1 = f32[8,128,1024]{2,1,0:T(8,128)S(1)} custom-call(s32[6]{0:T(128)S(1)} %stack.39.pos, s32[3,64]{1,0:T(4,128)S(1)} %pad_add_fusion.table, bf16[1024,1024]{1,0:T(8,128)(2,1)S(1)} %copy-done.1, bf16[272,512]{1,0:T(8,128)(2,1)S(1)} %broadcast_select_fusion.g0, bf16[272,512]{1,0:T(8,128)(2,1)S(1)} %collective-permute-done.7.g1, ...), custom_call_target="tpu_custom_call" | custom-call | flops 5000000000 | bytes 1048576 | tf_op jit(solution)/shard_map/covariance/pallas_call | solution.py:57
  74.1 1.9 %copy-done = f32[8,128,1024]{2,1,0:T(8,128)} copy-done((f32[8,128,1024]{2,1,0:T(8,128)}, f32[8,128,1024]{2,1,0:T(8,128)S(1)}, u32[]{:S(2)}) %copy-start) | copy-done | bytes 4194328
  76.1 0.0 reduce-scatter.2.cloned.1.call-update
  76.1 7.1 %all_to_all.15 = f32[4,16,640]{2,1,0:T(8,128)S(1)} all-to-all(f32[4,16,640]{2,1,0:T(8,128)S(1)} %bitcast.17), channel_id=1, replica_groups=mesh['z'=4,'y'=4,'c'=2,'w'=2,'x'=4] {'z'}, dimensions={0} | all-to-all | bytes 327680 | tf_op jit(solution)/shard_map/all_to_all | solution.py:325
  83.2 0.7 collective-permute-start.8
  83.9 0.0 collective-permute-done.8
  83.9 0.7 collective-permute-start.10
  84.6 0.7 collective-permute-start.11
  85.2 1.3 collective-permute-start.9
  86.5 0.0 collective-permute-done.10
  86.5 0.0 collective-permute-done.11
  86.6 13.5 %collective-permute-done.9 = f32[16,640]{1,0:T(8,128)S(1)} collective-permute-done((f32[16,640]{1,0:T(8,128)S(1)}, f32[16,640]{1,0:T(8,128)S(1)}, u32[]{:S(2)}, u32[]{:S(2)}) %collective-permute-start.9) | collective-permute-done | bytes 40992 | tf_op jit(solution)/shard_map/ppermute | solution.py:47
  100.1 19.3 %all_to_all.16 = f32[16,16,640]{2,1,0:T(8,128)S(1)} all-to-all(f32[16,16,640]{2,1,0:T(8,128)S(1)} %broadcast_in_dim.2), channel_id=1, replica_groups=mesh['z'=4,'y'=4,'c'=2,'w'=2,'x'=4] {'y','z'}, dimensions={0} | all-to-all | bytes 1310720 | tf_op jit(solution)/shard_map/all_to_all | solution.py:325
  119.4 4.9 %collective-permute-start.12 = (f32[256,640]{1,0:T(8,128)S(1)}, f32[256,640]{1,0:T(8,128)S(1)}, u32[]{:S(2)}, u32[]{:S(2)}) collective-permute-start(f32[256,640]{1,0:T(8,128)S(1)} %bitcast.15), channel_id=1, source_target_pairs={{0,8},{1,9},{2,10},{3,11},{4,12},{5,13},{6,14},{7,15},{8,0},{9,1},... | collective-permute-start | bytes 1966088 | tf_op jit(solution)/shard_map/ppermute | solution.py:47
  124.3 1.7 %collective-permute-done.12.other = f32[256,640]{1,0:T(8,128)S(1)} collective-permute-done((f32[256,640]{1,0:T(8,128)S(1)}, f32[256,640]{1,0:T(8,128)S(1)}, u32[]{:S(2)}, u32[]{:S(2)}) %collective-permute-start.12) | collective-permute-done | bytes 655392 | tf_op jit(solution)/shard_map/ppermute | solution.py:47
  126.0 5.0 %factor0.1 = (f32[512,512]{1,0:T(8,128)S(1)}, f32[512,512]{1,0:T(8,128)S(1)}) custom-call(s32[6]{0:T(128)S(1)} %stack.39.pos, f32[256,640]{1,0:T(8,128)S(1)} %bitcast.16, f32[256,640]{1,0:T(8,128)S(1)} %collective-permute-done.12.other), custom_call_target="tpu_custom_call" | custom-call | flops 5000000000 | bytes 1048576 | tf_op jit(solution)/shard_map/factor0/pallas_call | solution.py:57
  131.0 0.0 reduce-scatter.2.cloned.1.call-done
  131.0 4.5 %factor128.1.v = f32[512,512]{1,0:T(8,128)S(1)} custom-call(s32[6]{0:T(128)S(1)} %stack.39.pos, f32[512,512]{1,0:T(8,128)S(1)} %get-tuple-element.24.v), custom_call_target="tpu_custom_call" | custom-call | flops 5000000000 | bytes 1048576 | tf_op jit(solution)/shard_map/factor128/pallas_call | solution.py:57
  135.6 4.3 %factor256.1.v = f32[512,512]{1,0:T(8,128)S(1)} custom-call(s32[6]{0:T(128)S(1)} %stack.39.pos, f32[512,512]{1,0:T(8,128)S(1)} %factor128.1.v), custom_call_target="tpu_custom_call" | custom-call | flops 5000000000 | bytes 1048576 | tf_op jit(solution)/shard_map/factor256/pallas_call | solution.py:57
  140.0 1.1 collective-permute-start.15
  141.0 1.3 collective-permute-start.16
  142.3 0.2 collective-permute-start.17
  142.5 3.9 %factor384.1.inv = f32[512,512]{1,0:T(8,128)S(1)} custom-call(s32[6]{0:T(128)S(1)} %stack.39.pos, f32[512,512]{1,0:T(8,128)S(1)} %factor256.1.v), custom_call_target="tpu_custom_call" | custom-call | flops 5000000000 | bytes 1048576 | tf_op jit(solution)/shard_map/factor384/pallas_call | solution.py:57
  146.4 0.4 collective-permute-done.15.p1
  146.7 5.6 %collective-permute-done.16.p2 = f32[32,1024]{1,0:T(8,128)S(1)} collective-permute-done((f32[32,1024]{1,0:T(8,128)S(1)}, f32[32,1024]{1,0:T(8,128)S(1)}, u32[]{:S(2)}, u32[]{:S(2)}) %collective-permute-start.16) | collective-permute-done | bytes 131104 | tf_op jit(solution)/shard_map/ppermute | solution.py:47
  152.3 2.2 %collective-permute-done.17.p3 = f32[32,1024]{1,0:T(8,128)S(1)} collective-permute-done((f32[32,1024]{1,0:T(8,128)S(1)}, f32[32,1024]{1,0:T(8,128)S(1)}, u32[]{:S(2)}, u32[]{:S(2)}) %collective-permute-start.17) | collective-permute-done | bytes 131104 | tf_op jit(solution)/shard_map/ppermute | solution.py:47
  154.6 3.6 %whiten.1 = (f32[1,32,512]{2,1,0:T(8,128)}, f32[1,32,512]{2,1,0:T(8,128)}, f32[16,512]{1,0:T(8,128)}) custom-call(s32[6]{0:T(128)S(1)} %stack.39.pos, f32[512,512]{1,0:T(8,128)S(1)} %factor384.1.inv, f32[512,512]{1,0:T(8,128)S(1)} %get-tuple-element.25.up, f32[32,1024]{1,0:T(8,128)S(1)} %get-tuple-element.35.p0, f32[32,1024]{1,0:T(8,128)S(1)} %collective-permute-done.15.p1, ...), custom_call_target="tpu_custom_call" | custom-call | flops 2000000000 | bytes 1048576 | tf_op jit(solution)/shard_map/whiten/pallas_call | solution.py:57
  (10 shorter events, 0.1 us)
Async XLA Ops:
  7.2 11.6 %copy-start.1 = (bf16[1024,1024]{1,0:T(8,128)(2,1)S(1)}, bf16[1024,1024]{1,0:T(8,128)(2,1)}, u32[]{:S(2)}) copy-start(bf16[1024,1024]{1,0:T(8,128)(2,1)} %x.1) | copy-start | bytes 6291460
  8.1 10.7 %collective-permute-start = (bf16[16,512]{1,0:T(8,128)(2,1)S(1)}, bf16[16,512]{1,0:T(8,128)(2,1)S(1)}, u32[]{:S(2)}, u32[]{:S(2)}) collective-permute-start(bf16[16,512]{1,0:T(8,128)(2,1)S(1)} %get-tuple-element.31), channel_id=1, source_target_pairs={{0,8},{8,16},{16,24},{24,32},{32,40},{40,48},{48,56},{56,64},{64,7... | collective-permute-start | bytes 49160 | tf_op jit(solution)/shard_map/ppermute | solution.py:47
  8.7 10.1 %collective-permute-start.1 = (bf16[16,512]{1,0:T(8,128)(2,1)S(1)}, bf16[16,512]{1,0:T(8,128)(2,1)S(1)}, u32[]{:S(2)}, u32[]{:S(2)}) collective-permute-start(bf16[16,512]{1,0:T(8,128)(2,1)S(1)} %get-tuple-element.30), channel_id=1, source_target_pairs={{8,0},{16,8},{24,16},{32,24},{40,32},{48,40},{56,48},{64,56},{72,6... | collective-permute-start | bytes 49160 | tf_op jit(solution)/shard_map/ppermute | solution.py:47
  11.5 11.5 %collective-permute-start.2 = (bf16[272,512]{1,0:T(8,128)(2,1)}, bf16[272,512]{1,0:T(8,128)(2,1)}, u32[]{:S(2)}, u32[]{:S(2)}) collective-permute-start(bf16[272,512]{1,0:T(8,128)(2,1)} %get-tuple-element.28), channel_id=1, source_target_pairs={{0,2},{8,10},{16,18},{24,26},{32,34},{40,42},{48,50},{56,58},{64,6... | collective-permute-start | bytes 835592 | tf_op jit(solution)/shard_map/ppermute | solution.py:47
  12.8 10.2 %collective-permute-start.3 = (bf16[272,512]{1,0:T(8,128)(2,1)}, bf16[272,512]{1,0:T(8,128)(2,1)}, u32[]{:S(2)}, u32[]{:S(2)}) collective-permute-start(bf16[272,512]{1,0:T(8,128)(2,1)} %get-tuple-element.27), channel_id=1, source_target_pairs={{0,1},{8,9},{16,17},{24,25},{32,33},{40,41},{48,49},{56,57},{64,65... | collective-permute-start | bytes 835592 | tf_op jit(solution)/shard_map/ppermute | solution.py:47
  14.1 8.8 %collective-permute-start.4 = (bf16[272,512]{1,0:T(8,128)(2,1)}, bf16[272,512]{1,0:T(8,128)(2,1)}, u32[]{:S(2)}, u32[]{:S(2)}) collective-permute-start(bf16[272,512]{1,0:T(8,128)(2,1)} %get-tuple-element.29), channel_id=1, source_target_pairs={{0,3},{8,11},{16,19},{24,27},{32,35},{40,43},{48,51},{56,59},{64,6... | collective-permute-start | bytes 835592 | tf_op jit(solution)/shard_map/ppermute | solution.py:47
  18.8 4.2 %copy-start.2 = (bf16[240,512]{1,0:T(8,128)(2,1)S(1)}, bf16[240,512]{1,0:T(8,128)(2,1)}, u32[]{:S(2)}) copy-start(bf16[240,512]{1,0:T(8,128)(2,1)} %slice.43) | copy-start | bytes 737284
  25.0 10.2 %collective-permute-start.5 = (f32[256,640]{1,0:T(8,128)S(1)}, f32[256,640]{1,0:T(8,128)}, u32[]{:S(2)}, u32[]{:S(2)}) collective-permute-start(f32[256,640]{1,0:T(8,128)S(1)} %get-tuple-element.17), channel_id=1, source_target_pairs={{0,8},{8,0},{16,24},{24,16},{32,40},{40,32},{48,56},{56,48},{64,72... | collective-permute-start | bytes 1966088 | tf_op jit(solution)/shard_map/ppermute | solution.py:47
  26.5 19.7 %collective-permute-start.6 = (bf16[272,512]{1,0:T(8,128)(2,1)}, bf16[272,512]{1,0:T(8,128)(2,1)}, u32[]{:S(2)}, u32[]{:S(2)}) collective-permute-start(bf16[272,512]{1,0:T(8,128)(2,1)} %maximum_select_fusion), channel_id=1, source_target_pairs={{0,4},{1,5},{2,6},{3,7},{8,12},{9,13},{10,14},{11,15},{16,20},{17,... | collective-permute-start | bytes 835592 | tf_op jit(solution)/shard_map/ppermute | solution.py:47
  46.2 13.2 %all-to-all-start = ((f32[4,64,640]{2,1,0:T(8,128)}), f32[4,64,640]{2,1,0:T(8,128)}, u32[]{:S(2)}, u32[]{:S(2)}) async-start(f32[4,64,640]{2,1,0:T(8,128)} %bitcast.9), calls=%async_computation | async-start | bytes 1310720 | tf_op jit(solution)/shard_map/all_to_all | solution.py:325
  50.4 80.6 %reduce-scatter.2.cloned.1.call-start = ((), (), s32[]{:S(2)}) async-start(), calls=%async_computation.4 | async-start | bytes 4718592 | tf_op jit(solution)/shard_map/reduce_scatter | solution.py:408
  51.4 9.2 %collective-permute-start.7 = (bf16[272,512]{1,0:T(8,128)(2,1)S(1)}, bf16[272,512]{1,0:T(8,128)(2,1)S(1)}, u32[]{:S(2)}, u32[]{:S(2)}) collective-permute-start(bf16[272,512]{1,0:T(8,128)(2,1)S(1)} %broadcast_select_fusion.g0), channel_id=1, source_target_pairs={{0,1},{1,2},{2,3},{3,0},{4,5},{5,6},{6,7},{7,4},{8,9},{9,10},{10,1... | collective-permute-start | bytes 835592 | tf_op jit(solution)/shard_map/ppermute | solution.py:47
  52.4 15.3 %collective-permute-start.13 = (bf16[272,512]{1,0:T(8,128)(2,1)S(1)}, bf16[272,512]{1,0:T(8,128)(2,1)S(1)}, u32[]{:S(2)}, u32[]{:S(2)}) collective-permute-start(bf16[272,512]{1,0:T(8,128)(2,1)S(1)} %broadcast_select_fusion.g0), channel_id=1, source_target_pairs={{0,2},{1,3},{2,0},{3,1},{4,6},{5,7},{6,4},{7,5},{8,10},{9,11},{10,... | collective-permute-start | bytes 835592 | tf_op jit(solution)/shard_map/ppermute | solution.py:47
  55.3 13.0 %collective-permute-start.14 = (bf16[272,512]{1,0:T(8,128)(2,1)S(1)}, bf16[272,512]{1,0:T(8,128)(2,1)S(1)}, u32[]{:S(2)}, u32[]{:S(2)}) collective-permute-start(bf16[272,512]{1,0:T(8,128)(2,1)S(1)} %broadcast_select_fusion.g0), channel_id=1, source_target_pairs={{0,3},{1,0},{2,1},{3,2},{4,7},{5,4},{6,5},{7,6},{8,11},{9,8},{10,9... | collective-permute-start | bytes 835592 | tf_op jit(solution)/shard_map/ppermute | solution.py:47
  74.1 1.9 %copy-start = (f32[8,128,1024]{2,1,0:T(8,128)}, f32[8,128,1024]{2,1,0:T(8,128)S(1)}, u32[]{:S(2)}) copy-start(f32[8,128,1024]{2,1,0:T(8,128)S(1)} %covariance.1) | copy-start | bytes 12582916
  83.2 0.7 collective-permute-start.8
  83.9 2.6 %collective-permute-start.10 = (f32[16,640]{1,0:T(8,128)S(1)}, f32[16,640]{1,0:T(8,128)S(1)}, u32[]{:S(2)}, u32[]{:S(2)}) collective-permute-start(f32[16,640]{1,0:T(8,128)S(1)} %broadcast_select_fusion.1), channel_id=1, source_target_pairs={{0,1},{4,5},{8,9},{12,13},{16,17},{20,21},{24,25},{28,29},{32,33},... | collective-permute-start | bytes 122888 | tf_op jit(solution)/shard_map/ppermute | solution.py:47
  84.6 2.0 %collective-permute-start.11 = (f32[16,640]{1,0:T(8,128)S(1)}, f32[16,640]{1,0:T(8,128)S(1)}, u32[]{:S(2)}, u32[]{:S(2)}) collective-permute-start(f32[16,640]{1,0:T(8,128)S(1)} %broadcast_select_fusion.1), channel_id=1, source_target_pairs={{0,3},{4,7},{8,11},{12,15},{16,19},{20,23},{24,27},{28,31},{32,35}... | collective-permute-start | bytes 122888 | tf_op jit(solution)/shard_map/ppermute | solution.py:47
  85.2 14.8 %collective-permute-start.9 = (f32[16,640]{1,0:T(8,128)S(1)}, f32[16,640]{1,0:T(8,128)S(1)}, u32[]{:S(2)}, u32[]{:S(2)}) collective-permute-start(f32[16,640]{1,0:T(8,128)S(1)} %broadcast_select_fusion.1), channel_id=1, source_target_pairs={{0,2},{4,6},{8,10},{12,14},{16,18},{20,22},{24,26},{28,30},{32,34}... | collective-permute-start | bytes 122888 | tf_op jit(solution)/shard_map/ppermute | solution.py:47
  119.4 6.6 %collective-permute-start.12 = (f32[256,640]{1,0:T(8,128)S(1)}, f32[256,640]{1,0:T(8,128)S(1)}, u32[]{:S(2)}, u32[]{:S(2)}) collective-permute-start(f32[256,640]{1,0:T(8,128)S(1)} %bitcast.15), channel_id=1, source_target_pairs={{0,8},{1,9},{2,10},{3,11},{4,12},{5,13},{6,14},{7,15},{8,0},{9,1},... | collective-permute-start | bytes 1966088 | tf_op jit(solution)/shard_map/ppermute | solution.py:47
  135.6 4.4 %copy-start.3 = (f32[128,1024]{1,0:T(8,128)S(1)}, f32[128,1024]{1,0:T(8,128)}, u32[]{:S(2)}) copy-start(f32[128,1024]{1,0:T(8,128)} %reduce-scatter.2.cloned.1.call-done) | copy-start | bytes 1572868
  140.0 6.8 %collective-permute-start.15 = (f32[32,1024]{1,0:T(8,128)S(1)}, f32[32,1024]{1,0:T(8,128)S(1)}, u32[]{:S(2)}, u32[]{:S(2)}) collective-permute-start(f32[32,1024]{1,0:T(8,128)S(1)} %get-tuple-element.34), channel_id=1, source_target_pairs={{0,128},{1,129},{2,130},{3,131},{4,132},{5,133},{6,134},{7,135},{8... | collective-permute-start | bytes 393224 | tf_op jit(solution)/shard_map/ppermute | solution.py:47
  141.0 11.3 %collective-permute-start.16 = (f32[32,1024]{1,0:T(8,128)S(1)}, f32[32,1024]{1,0:T(8,128)S(1)}, u32[]{:S(2)}, u32[]{:S(2)}) collective-permute-start(f32[32,1024]{1,0:T(8,128)S(1)} %get-tuple-element.33), channel_id=1, source_target_pairs={{0,64},{1,65},{2,66},{3,67},{4,68},{5,69},{6,70},{7,71},{8,72},{9,... | collective-permute-start | bytes 393224 | tf_op jit(solution)/shard_map/ppermute | solution.py:47
  142.3 12.3 %collective-permute-start.17 = (f32[32,1024]{1,0:T(8,128)S(1)}, f32[32,1024]{1,0:T(8,128)S(1)}, u32[]{:S(2)}, u32[]{:S(2)}) collective-permute-start(f32[32,1024]{1,0:T(8,128)S(1)} %get-tuple-element.32), channel_id=1, source_target_pairs={{0,192},{1,193},{2,194},{3,195},{4,196},{5,197},{6,198},{7,199},{8... | collective-permute-start | bytes 393224 | tf_op jit(solution)/shard_map/ppermute | solution.py:47
Sparse Core Ops, SparseCore 0:
  76.2 48.5 reduce-scatter.1

commit v7 on v4

--- a/solution.py
+++ b/solution.py
@@ -345,7 +345,8 @@
 
 
 def diag_gather(own):
-    half = spread(own, ("y", "z"), 16).reshape(256, own.shape[1])
+    column = spread(own, "z", 4).reshape(64, own.shape[1])
+    half = spread(column, "y", 4).reshape(256, own.shape[1])
     return half, swap_core(half)
 
 

time: 155 us -> 160 us (1.032)
  blocking collectives: 26.3 us -> 30.6 us
  starting transfers between devices: 33.9 us -> 31.4 us
  waiting for transfers between devices: 33.8 us -> 35.4 us
    all_to_all x1 -> x2, blocking collectives: 26.3 us -> 30.6 us  [exchange(): return lax.all_to_all(v, axes, 0, 0, tiled=True)]
    ppermute x18, starting transfers between devices: 22.1 us -> 19.7 us  [move(): return lax.ppermute(value, AXES, pairs)]
    ppermute x18, waiting for transfers between devices: 29.5 us -> 31.3 us  [move(): return lax.ppermute(value, AXES, pairs)]
  transfers between devices with their start and end apart: 21 -> 21, of which waited for: 9 -> 8; matrix products, arithmetic and copies ran while one was open for 4% -> 4% of each run, Pallas kernels for 14% -> 13%
where the time goes in v7:
time: 160 us; the launch traced here: 157 us
  waiting for transfers between devices  35.4 us (22%)
  Pallas kernels  32.8 us (20%)
  starting transfers between devices  31.4 us (20%)
  blocking collectives  30.6 us (19%)
  between operations  14.2 us (9%)
  local copies, waits for them, and re-layouts  8.29 us (5%)
  other arithmetic  3.73 us (2%)
    pallas_call x8, Pallas kernels, call(): pl.pallas_call(kernel, grid=(1,), out_shape=outs, in_specs=specs, out_spe...  32.8 us
    ppermute x18, waiting for transfers between devices, move(): return lax.ppermute(value, AXES, pairs)  31.3 us
    all_to_all x2, blocking collectives, exchange(): return lax.all_to_all(v, axes, 0, 0, tiled=True)  30.6 us
    ppermute x18, starting transfers between devices, move(): return lax.ppermute(value, AXES, pairs)  19.7 us
    all_to_all x2, starting transfers between devices, exchange(): return lax.all_to_all(v, axes, 0, 0, tiled=True)  11.8 us
    all_to_all x2, waiting for transfers between devices, exchange(): return lax.all_to_all(v, axes, 0, 0, tiled=True)  4.16 us
    unnamed x6, local copies, waits for them, and re-layouts  3.53 us
  transfers between devices with their start and end apart: 21, of which 8 were waited for; matrix products, arithmetic and copies ran while one was open for 4% of the time, Pallas kernels for 13%

profile of v7, /device:TPU:2, one launch (start us, length us, event | category | flops | bytes accessed | tf_op | source)
XLA Modules:
  0.0 156.5 jit_solution(3286068910673043868)
XLA Ops:
  7.2 0.7 fusion.1
  7.9 0.7 collective-permute-start.1
  8.6 0.7 collective-permute-start
  9.2 2.0 %fusion = (bf16[272,512]{1,0:T(8,128)(2,1)S(1)}, bf16[272,512]{1,0:T(8,128)(2,1)}, bf16[272,512]{1,0:T(8,128)(2,1)}) fusion(bf16[1024,1024]{1,0:T(8,128)(2,1)} %x.1), kind=kLoop, calls=%fused_computation.6 | loop fusion | bytes 1671168 | tf_op jit(solution)/shard_map/slice | solution.py:378
  11.2 0.7 slice.40
  12.0 0.1 add_bitcast_fusion
  12.0 0.7 pad_add_fusion.table
  12.7 0.1 stack.39.pos
  12.8 0.0 collective-permute-done.1.after
  12.8 0.0 collective-permute-done.before
  12.8 0.0 copy-start.1
  12.8 1.6 %copy-done.1 = bf16[1024,1024]{1,0:T(8,128)(2,1)S(1)} copy-done((bf16[1024,1024]{1,0:T(8,128)(2,1)S(1)}, bf16[1024,1024]{1,0:T(8,128)(2,1)}, u32[]{:S(2)}) %copy-start.1) | copy-done | bytes 2097176
  14.4 4.2 %diagonal.1 = (f32[256,640]{1,0:T(8,128)S(1)}, f32[256,640]{1,0:T(8,128)S(1)}) custom-call(s32[6]{0:T(128)S(1)} %stack.39.pos, s32[3,64]{1,0:T(4,128)S(1)} %pad_add_fusion.table, bf16[1024,1024]{1,0:T(8,128)(2,1)S(1)} %copy-done.1, bf16[16,512]{1,0:T(8,128)(2,1)S(1)} %collective-permute-done.before, bf16[16,512]{1,0:T(8,128)(2,1)S(1)} %collective-permute-done.1.after), custom_call_target="tpu_custom_call" | custom-call | flops 3000000000 | bytes 1048576 | tf_op jit(solution)/shard_map/diagonal/pallas_call | solution.py:57
  18.6 0.7 collective-permute-start.2
  19.3 1.4 collective-permute-start.4
  20.7 1.3 collective-permute-start.5
  22.0 1.4 collective-permute-start.6
  23.4 0.0 collective-permute-done.2
  23.4 0.9 add.25
  24.3 4.5 %all-to-all-start = ((f32[4,64,640]{2,1,0:T(8,128)}), f32[4,64,640]{2,1,0:T(8,128)S(1)}, u32[]{:S(2)}, u32[]{:S(2)}) async-start(f32[4,64,640]{2,1,0:T(8,128)} %bitcast.9), calls=%async_computation | async-start | bytes 1310720 | tf_op jit(solution)/shard_map/all_to_all | solution.py:327
  28.8 0.0 collective-permute-done.4
  28.8 11.9 %collective-permute-done.5 = bf16[272,512]{1,0:T(8,128)(2,1)} collective-permute-done((bf16[272,512]{1,0:T(8,128)(2,1)}, bf16[272,512]{1,0:T(8,128)(2,1)}, u32[]{:S(2)}, u32[]{:S(2)}) %collective-permute-start.5) | collective-permute-done | bytes 278560 | tf_op jit(solution)/shard_map/ppermute | solution.py:47
  40.7 0.0 collective-permute-done.6
  40.7 1.3 maximum_select_fusion
  41.9 2.0 %collective-permute-start.7 = (bf16[272,512]{1,0:T(8,128)(2,1)S(1)}, bf16[272,512]{1,0:T(8,128)(2,1)}, u32[]{:S(2)}, u32[]{:S(2)}) collective-permute-start(bf16[272,512]{1,0:T(8,128)(2,1)S(1)} %maximum_select_fusion), channel_id=1, source_target_pairs={{0,4},{1,5},{2,6},{3,7},{8,12},{9,13},{10,14},{11,15},{16,20},{17,... | collective-permute-start | bytes 835592 | tf_op jit(solution)/shard_map/ppermute | solution.py:47
  44.0 0.0 all-to-all-done
  44.0 0.7 reduce_sum.18
  44.7 7.3 %all-to-all-start.1 = ((f32[4,16,640]{2,1,0:T(8,128)}), f32[4,16,640]{2,1,0:T(8,128)S(1)}, u32[]{:S(2)}, u32[]{:S(2)}) async-start(f32[4,16,640]{2,1,0:T(8,128)} %bitcast.10), calls=%async_computation.1 | async-start | bytes 327680 | tf_op jit(solution)/shard_map/all_to_all | solution.py:327
  52.0 0.0 collective-permute-done.7
  52.0 0.1 broadcast_select_fusion.g0
  52.0 4.1 %collective-permute-start.10 = (bf16[272,512]{1,0:T(8,128)(2,1)S(1)}, bf16[272,512]{1,0:T(8,128)(2,1)S(1)}, u32[]{:S(2)}, u32[]{:S(2)}) collective-permute-start(bf16[272,512]{1,0:T(8,128)(2,1)S(1)} %broadcast_select_fusion.g0), channel_id=1, source_target_pairs={{0,3},{1,0},{2,1},{3,2},{4,7},{5,4},{6,5},{7,6},{8,11},{9,8},{10,9... | collective-permute-start | bytes 835592 | tf_op jit(solution)/shard_map/ppermute | solution.py:47
  56.2 0.0 collective-permute-start.9
  56.2 1.6 collective-permute-start.8
  57.7 4.2 %all-to-all-done.1 = f32[4,16,640]{2,1,0:T(8,128)S(1)} async-done(((f32[4,16,640]{2,1,0:T(8,128)}), f32[4,16,640]{2,1,0:T(8,128)S(1)}, u32[]{:S(2)}, u32[]{:S(2)}) %all-to-all-start.1) | async-done | bytes 163872 | tf_op jit(solution)/shard_map/all_to_all | solution.py:327
  61.9 0.7 collective-permute-start.3
  62.6 3.7 %collective-permute-done.10.g3 = bf16[272,512]{1,0:T(8,128)(2,1)S(1)} collective-permute-done((bf16[272,512]{1,0:T(8,128)(2,1)S(1)}, bf16[272,512]{1,0:T(8,128)(2,1)S(1)}, u32[]{:S(2)}, u32[]{:S(2)}) %collective-permute-start.10) | collective-permute-done | bytes 278560 | tf_op jit(solution)/shard_map/ppermute | solution.py:47
  66.3 1.4 collective-permute-done.9.g2
  67.7 0.9 collective-permute-done.8.g1
  68.5 0.0 collective-permute-done.3
  68.5 5.9 %covariance.1 = f32[8,128,1024]{2,1,0:T(8,128)S(1)} custom-call(s32[6]{0:T(128)S(1)} %stack.39.pos, s32[3,64]{1,0:T(4,128)S(1)} %pad_add_fusion.table, bf16[1024,1024]{1,0:T(8,128)(2,1)S(1)} %copy-done.2, bf16[272,512]{1,0:T(8,128)(2,1)S(1)} %broadcast_select_fusion.g0, bf16[272,512]{1,0:T(8,128)(2,1)S(1)} %collective-permute-done.8.g1, ...), custom_call_target="tpu_custom_call" | custom-call | flops 5000000000 | bytes 1048576 | tf_op jit(solution)/shard_map/covariance/pallas_call | solution.py:57
  74.5 1.9 %copy-done = f32[8,128,1024]{2,1,0:T(8,128)} copy-done((f32[8,128,1024]{2,1,0:T(8,128)}, f32[8,128,1024]{2,1,0:T(8,128)S(1)}, u32[]{:S(2)}) %copy-start) | copy-done | bytes 4194328
  76.4 0.0 reduce-scatter.2.cloned.1.call-update
  76.4 0.7 collective-permute-start.13
  77.1 1.3 collective-permute-start.12
  78.4 0.7 collective-permute-start.11
  79.1 6.8 %collective-permute-done.12 = f32[16,640]{1,0:T(8,128)S(1)} collective-permute-done((f32[16,640]{1,0:T(8,128)S(1)}, f32[16,640]{1,0:T(8,128)S(1)}, u32[]{:S(2)}, u32[]{:S(2)}) %collective-permute-start.12) | collective-permute-done | bytes 40992 | tf_op jit(solution)/shard_map/ppermute | solution.py:47
  86.0 12.6 %all_to_all.20 = f32[4,16,640]{2,1,0:T(8,128)S(1)} all-to-all(f32[4,16,640]{2,1,0:T(8,128)S(1)} %broadcast_in_dim.6), channel_id=1, replica_groups=mesh['z'=4,'y'=4,'c'=2,'w'=2,'x'=4] {'z'}, dimensions={0} | all-to-all | bytes 327680 | tf_op jit(solution)/shard_map/all_to_all | solution.py:327
  98.6 18.0 %all_to_all.21 = f32[4,64,640]{2,1,0:T(8,128)S(1)} all-to-all(f32[4,64,640]{2,1,0:T(8,128)S(1)} %broadcast_in_dim.15), channel_id=1, replica_groups=mesh['z'=4,'y'=4,'c'=2,'w'=2,'x'=4] {'y'}, dimensions={0} | all-to-all | bytes 1310720 | tf_op jit(solution)/shard_map/all_to_all | solution.py:327
  116.6 0.0 collective-permute-start.14
  116.6 2.1 %collective-permute-done.14.other = f32[256,640]{1,0:T(8,128)S(1)} collective-permute-done((f32[256,640]{1,0:T(8,128)S(1)}, f32[256,640]{1,0:T(8,128)S(1)}, u32[]{:S(2)}, u32[]{:S(2)}) %collective-permute-start.14) | collective-permute-done | bytes 655392 | tf_op jit(solution)/shard_map/ppermute | solution.py:47
  118.7 5.0 %factor0.1 = (f32[512,512]{1,0:T(8,128)S(1)}, f32[512,512]{1,0:T(8,128)S(1)}) custom-call(s32[6]{0:T(128)S(1)} %stack.39.pos, f32[256,640]{1,0:T(8,128)S(1)} %bitcast.17, f32[256,640]{1,0:T(8,128)S(1)} %collective-permute-done.14.other), custom_call_target="tpu_custom_call" | custom-call | flops 5000000000 | bytes 1048576 | tf_op jit(solution)/shard_map/factor0/pallas_call | solution.py:57
  123.6 4.5 %factor128.1.v = f32[512,512]{1,0:T(8,128)S(1)} custom-call(s32[6]{0:T(128)S(1)} %stack.39.pos, f32[512,512]{1,0:T(8,128)S(1)} %get-tuple-element.25.v), custom_call_target="tpu_custom_call" | custom-call | flops 5000000000 | bytes 1048576 | tf_op jit(solution)/shard_map/factor128/pallas_call | solution.py:57
  128.2 4.3 %factor256.1.v = f32[512,512]{1,0:T(8,128)S(1)} custom-call(s32[6]{0:T(128)S(1)} %stack.39.pos, f32[512,512]{1,0:T(8,128)S(1)} %factor128.1.v), custom_call_target="tpu_custom_call" | custom-call | flops 5000000000 | bytes 1048576 | tf_op jit(solution)/shard_map/factor256/pallas_call | solution.py:57
  132.5 0.0 reduce-scatter.2.cloned.1.call-done
  132.5 1.1 fusion.2
  133.7 0.9 collective-permute-start.17
  134.5 1.3 collective-permute-start.16
  135.8 0.5 collective-permute-start.15
  136.3 3.9 %factor384.1.inv = f32[512,512]{1,0:T(8,128)S(1)} custom-call(s32[6]{0:T(128)S(1)} %stack.39.pos, f32[512,512]{1,0:T(8,128)S(1)} %factor256.1.v), custom_call_target="tpu_custom_call" | custom-call | flops 5000000000 | bytes 1048576 | tf_op jit(solution)/shard_map/factor384/pallas_call | solution.py:57
  140.2 3.2 %tau.1 = f32[16,512]{1,0:T(8,128)} custom-call(s32[6]{0:T(128)S(1)} %stack.39.pos, f32[512,512]{1,0:T(8,128)S(1)} %factor384.1.inv, f32[512,512]{1,0:T(8,128)S(1)} %get-tuple-element.32.up), custom_call_target="tpu_custom_call" | custom-call | flops 1000000000 | bytes 1048576 | tf_op jit(solution)/shard_map/tau/pallas_call | solution.py:57
  143.4 0.0 collective-permute-done.17.p3
  143.4 0.0 collective-permute-done.16.p2
  143.4 4.4 %collective-permute-done.15.p1 = f32[32,1024]{1,0:T(8,128)S(1)} collective-permute-done((f32[32,1024]{1,0:T(8,128)S(1)}, f32[32,1024]{1,0:T(8,128)S(1)}, u32[]{:S(2)}, u32[]{:S(2)}) %collective-permute-start.15) | collective-permute-done | bytes 131104 | tf_op jit(solution)/shard_map/ppermute | solution.py:47
  147.9 1.8 %whiten.1 = (f32[1,32,512]{2,1,0:T(8,128)}, f32[1,32,512]{2,1,0:T(8,128)}) custom-call(s32[6]{0:T(128)S(1)} %stack.39.pos, f32[512,512]{1,0:T(8,128)S(1)} %factor384.1.inv, f32[32,1024]{1,0:T(8,128)S(1)} %get-tuple-element.41.p0, f32[32,1024]{1,0:T(8,128)S(1)} %collective-permute-done.15.p1, f32[32,1024]{1,0:T(8,128)S(1)} %collective-permute-done.16.p2, ...), custom_call_target="tpu_custom_call" | custom-call | flops 1000000000 | bytes 1048576 | tf_op jit(solution)/shard_map/whiten/pallas_call | solution.py:57
  (12 shorter events, 0.1 us)
Async XLA Ops:
  7.9 4.9 %collective-permute-start.1 = (bf16[16,512]{1,0:T(8,128)(2,1)S(1)}, bf16[16,512]{1,0:T(8,128)(2,1)S(1)}, u32[]{:S(2)}, u32[]{:S(2)}) collective-permute-start(bf16[16,512]{1,0:T(8,128)(2,1)S(1)} %get-tuple-element.36), channel_id=1, source_target_pairs={{8,0},{16,8},{24,16},{32,24},{40,32},{48,40},{56,48},{64,56},{72,6... | collective-permute-start | bytes 49160 | tf_op jit(solution)/shard_map/ppermute | solution.py:47
  8.6 4.3 %collective-permute-start = (bf16[16,512]{1,0:T(8,128)(2,1)S(1)}, bf16[16,512]{1,0:T(8,128)(2,1)S(1)}, u32[]{:S(2)}, u32[]{:S(2)}) collective-permute-start(bf16[16,512]{1,0:T(8,128)(2,1)S(1)} %get-tuple-element.37), channel_id=1, source_target_pairs={{0,8},{8,16},{16,24},{24,32},{32,40},{40,48},{48,56},{56,64},{64,7... | collective-permute-start | bytes 49160 | tf_op jit(solution)/shard_map/ppermute | solution.py:47
  12.8 1.6 %copy-start.1 = (bf16[1024,1024]{1,0:T(8,128)(2,1)S(1)}, bf16[1024,1024]{1,0:T(8,128)(2,1)}, u32[]{:S(2)}) copy-start(bf16[1024,1024]{1,0:T(8,128)(2,1)} %x.1) | copy-start | bytes 6291460
  18.6 4.8 %collective-permute-start.2 = (f32[256,640]{1,0:T(8,128)S(1)}, f32[256,640]{1,0:T(8,128)S(1)}, u32[]{:S(2)}, u32[]{:S(2)}) collective-permute-start(f32[256,640]{1,0:T(8,128)S(1)} %get-tuple-element.20), channel_id=1, source_target_pairs={{0,8},{8,0},{16,24},{24,16},{32,40},{40,32},{48,56},{56,48},{64,72... | collective-permute-start | bytes 1966088 | tf_op jit(solution)/shard_map/ppermute | solution.py:47
  19.3 9.5 %collective-permute-start.4 = (bf16[272,512]{1,0:T(8,128)(2,1)}, bf16[272,512]{1,0:T(8,128)(2,1)}, u32[]{:S(2)}, u32[]{:S(2)}) collective-permute-start(bf16[272,512]{1,0:T(8,128)(2,1)} %get-tuple-element.21), channel_id=1, source_target_pairs={{0,2},{8,10},{16,18},{24,26},{32,34},{40,42},{48,50},{56,58},{64,6... | collective-permute-start | bytes 835592 | tf_op jit(solution)/shard_map/ppermute | solution.py:47
  20.7 20.0 %collective-permute-start.5 = (bf16[272,512]{1,0:T(8,128)(2,1)}, bf16[272,512]{1,0:T(8,128)(2,1)}, u32[]{:S(2)}, u32[]{:S(2)}) collective-permute-start(bf16[272,512]{1,0:T(8,128)(2,1)} %get-tuple-element.22), channel_id=1, source_target_pairs={{0,1},{8,9},{16,17},{24,25},{32,33},{40,41},{48,49},{56,57},{64,65... | collective-permute-start | bytes 835592 | tf_op jit(solution)/shard_map/ppermute | solution.py:47
  22.0 18.7 %collective-permute-start.6 = (bf16[272,512]{1,0:T(8,128)(2,1)S(1)}, bf16[272,512]{1,0:T(8,128)(2,1)}, u32[]{:S(2)}, u32[]{:S(2)}) collective-permute-start(bf16[272,512]{1,0:T(8,128)(2,1)S(1)} %get-tuple-element.23), channel_id=1, source_target_pairs={{0,3},{8,11},{16,19},{24,27},{32,35},{40,43},{48,51},{56,59},{64,6... | collective-permute-start | bytes 835592 | tf_op jit(solution)/shard_map/ppermute | solution.py:47
  24.3 19.7 %all-to-all-start = ((f32[4,64,640]{2,1,0:T(8,128)}), f32[4,64,640]{2,1,0:T(8,128)S(1)}, u32[]{:S(2)}, u32[]{:S(2)}) async-start(f32[4,64,640]{2,1,0:T(8,128)} %bitcast.9), calls=%async_computation | async-start | bytes 1310720 | tf_op jit(solution)/shard_map/all_to_all | solution.py:327
  28.8 39.8 %copy-start.2 = (bf16[1024,1024]{1,0:T(8,128)(2,1)S(1)}, bf16[1024,1024]{1,0:T(8,128)(2,1)}, u32[]{:S(2)}) copy-start(bf16[1024,1024]{1,0:T(8,128)(2,1)} %x.1) | copy-start | bytes 6291460
  41.9 10.0 %collective-permute-start.7 = (bf16[272,512]{1,0:T(8,128)(2,1)S(1)}, bf16[272,512]{1,0:T(8,128)(2,1)}, u32[]{:S(2)}, u32[]{:S(2)}) collective-permute-start(bf16[272,512]{1,0:T(8,128)(2,1)S(1)} %maximum_select_fusion), channel_id=1, source_target_pairs={{0,4},{1,5},{2,6},{3,7},{8,12},{9,13},{10,14},{11,15},{16,20},{17,... | collective-permute-start | bytes 835592 | tf_op jit(solution)/shard_map/ppermute | solution.py:47
  44.7 17.2 %all-to-all-start.1 = ((f32[4,16,640]{2,1,0:T(8,128)}), f32[4,16,640]{2,1,0:T(8,128)S(1)}, u32[]{:S(2)}, u32[]{:S(2)}) async-start(f32[4,16,640]{2,1,0:T(8,128)} %bitcast.10), calls=%async_computation.1 | async-start | bytes 327680 | tf_op jit(solution)/shard_map/all_to_all | solution.py:327
  52.0 80.6 %reduce-scatter.2.cloned.1.call-start = ((), (), s32[]{:S(2)}) async-start(), calls=%async_computation.5 | async-start | bytes 4718592 | tf_op jit(solution)/shard_map/reduce_scatter | solution.py:408
  52.0 14.2 %collective-permute-start.10 = (bf16[272,512]{1,0:T(8,128)(2,1)S(1)}, bf16[272,512]{1,0:T(8,128)(2,1)S(1)}, u32[]{:S(2)}, u32[]{:S(2)}) collective-permute-start(bf16[272,512]{1,0:T(8,128)(2,1)S(1)} %broadcast_select_fusion.g0), channel_id=1, source_target_pairs={{0,3},{1,0},{2,1},{3,2},{4,7},{5,4},{6,5},{7,6},{8,11},{9,8},{10,9... | collective-permute-start | bytes 835592 | tf_op jit(solution)/shard_map/ppermute | solution.py:47
  56.2 11.5 %collective-permute-start.9 = (bf16[272,512]{1,0:T(8,128)(2,1)S(1)}, bf16[272,512]{1,0:T(8,128)(2,1)S(1)}, u32[]{:S(2)}, u32[]{:S(2)}) collective-permute-start(bf16[272,512]{1,0:T(8,128)(2,1)S(1)} %broadcast_select_fusion.g0), channel_id=1, source_target_pairs={{0,2},{1,3},{2,0},{3,1},{4,6},{5,7},{6,4},{7,5},{8,10},{9,11},{10,... | collective-permute-start | bytes 835592 | tf_op jit(solution)/shard_map/ppermute | solution.py:47
  56.2 12.4 %collective-permute-start.8 = (bf16[272,512]{1,0:T(8,128)(2,1)S(1)}, bf16[272,512]{1,0:T(8,128)(2,1)S(1)}, u32[]{:S(2)}, u32[]{:S(2)}) collective-permute-start(bf16[272,512]{1,0:T(8,128)(2,1)S(1)} %broadcast_select_fusion.g0), channel_id=1, source_target_pairs={{0,1},{1,2},{2,3},{3,0},{4,5},{5,6},{6,7},{7,4},{8,9},{9,10},{10,1... | collective-permute-start | bytes 835592 | tf_op jit(solution)/shard_map/ppermute | solution.py:47
  61.9 6.6 %collective-permute-start.3 = (f32[16,640]{1,0:T(8,128)S(1)}, f32[16,640]{1,0:T(8,128)S(1)}, u32[]{:S(2)}, u32[]{:S(2)}) collective-permute-start(f32[16,640]{1,0:T(8,128)S(1)} %reduce_sum.19), channel_id=1, source_target_pairs={{0,4},{8,12},{16,20},{24,28},{32,36},{40,44},{48,52},{56,60},{64,6... | collective-permute-start | bytes 122888 | tf_op jit(solution)/shard_map/ppermute | solution.py:47
  74.5 1.9 %copy-start = (f32[8,128,1024]{2,1,0:T(8,128)}, f32[8,128,1024]{2,1,0:T(8,128)S(1)}, u32[]{:S(2)}) copy-start(f32[8,128,1024]{2,1,0:T(8,128)S(1)} %covariance.1) | copy-start | bytes 12582916
  76.4 2.6 %collective-permute-start.13 = (f32[16,640]{1,0:T(8,128)S(1)}, f32[16,640]{1,0:T(8,128)S(1)}, u32[]{:S(2)}, u32[]{:S(2)}) collective-permute-start(f32[16,640]{1,0:T(8,128)S(1)} %broadcast_select_fusion.1), channel_id=1, source_target_pairs={{0,3},{4,7},{8,11},{12,15},{16,19},{20,23},{24,27},{28,31},{32,35}... | collective-permute-start | bytes 122888 | tf_op jit(solution)/shard_map/ppermute | solution.py:47
  77.1 8.8 %collective-permute-start.12 = (f32[16,640]{1,0:T(8,128)S(1)}, f32[16,640]{1,0:T(8,128)S(1)}, u32[]{:S(2)}, u32[]{:S(2)}) collective-permute-start(f32[16,640]{1,0:T(8,128)S(1)} %broadcast_select_fusion.1), channel_id=1, source_target_pairs={{0,1},{4,5},{8,9},{12,13},{16,17},{20,21},{24,25},{28,29},{32,33},... | collective-permute-start | bytes 122888 | tf_op jit(solution)/shard_map/ppermute | solution.py:47
  78.4 7.5 %collective-permute-start.11 = (f32[16,640]{1,0:T(8,128)S(1)}, f32[16,640]{1,0:T(8,128)S(1)}, u32[]{:S(2)}, u32[]{:S(2)}) collective-permute-start(f32[16,640]{1,0:T(8,128)S(1)} %broadcast_select_fusion.1), channel_id=1, source_target_pairs={{0,2},{4,6},{8,10},{12,14},{16,18},{20,22},{24,26},{28,30},{32,34}... | collective-permute-start | bytes 122888 | tf_op jit(solution)/shard_map/ppermute | solution.py:47
  116.6 2.1 %collective-permute-start.14 = (f32[256,640]{1,0:T(8,128)S(1)}, f32[256,640]{1,0:T(8,128)S(1)}, u32[]{:S(2)}, u32[]{:S(2)}) collective-permute-start(f32[256,640]{1,0:T(8,128)S(1)} %bitcast.16), channel_id=1, source_target_pairs={{0,8},{1,9},{2,10},{3,11},{4,12},{5,13},{6,14},{7,15},{8,0},{9,1},... | collective-permute-start | bytes 1966088 | tf_op jit(solution)/shard_map/ppermute | solution.py:47
  133.7 9.7 %collective-permute-start.17 = (f32[32,1024]{1,0:T(8,128)S(1)}, f32[32,1024]{1,0:T(8,128)S(1)}, u32[]{:S(2)}, u32[]{:S(2)}) collective-permute-start(f32[32,1024]{1,0:T(8,128)S(1)} %get-tuple-element.38), channel_id=1, source_target_pairs={{0,192},{1,193},{2,194},{3,195},{4,196},{5,197},{6,198},{7,199},{8... | collective-permute-start | bytes 393224 | tf_op jit(solution)/shard_map/ppermute | solution.py:47
  134.5 8.9 %collective-permute-start.16 = (f32[32,1024]{1,0:T(8,128)S(1)}, f32[32,1024]{1,0:T(8,128)S(1)}, u32[]{:S(2)}, u32[]{:S(2)}) collective-permute-start(f32[32,1024]{1,0:T(8,128)S(1)} %get-tuple-element.39), channel_id=1, source_target_pairs={{0,64},{1,65},{2,66},{3,67},{4,68},{5,69},{6,70},{7,71},{8,72},{9,... | collective-permute-start | bytes 393224 | tf_op jit(solution)/shard_map/ppermute | solution.py:47
  135.8 12.1 %collective-permute-start.15 = (f32[32,1024]{1,0:T(8,128)S(1)}, f32[32,1024]{1,0:T(8,128)S(1)}, u32[]{:S(2)}, u32[]{:S(2)}) collective-permute-start(f32[32,1024]{1,0:T(8,128)S(1)} %get-tuple-element.40), channel_id=1, source_target_pairs={{0,128},{1,129},{2,130},{3,131},{4,132},{5,133},{6,134},{7,135},{8... | collective-permute-start | bytes 393224 | tf_op jit(solution)/shard_map/ppermute | solution.py:47
Sparse Core Ops, SparseCore 0:
  76.5 52.8 reduce-scatter.1
